TPU v7x, 32 devices: a whole 2x2x4 slice. The times are simulated.
32 devices in a mesh: row: 8 (over y, x, core), col: 4 (over z).
Axes of the slice: x: 2, y: 2, z: 4, core: 2. Of those that a mesh axis runs over, the one named last changes fastest.
Arguments:
- activations: bfloat16 [256, 32, 8192], P(('row', 'col')), may hold values from -6 to 6
- out_grads: bfloat16 [256, 32, 8192], P(('row', 'col')), may hold values from -6 to 6
- proj_in: bfloat16 [8192, 64], replicated, may hold values from -0.0625 to 0.0625
- proj_out: bfloat16 [8192, 64], replicated, may hold values from -0.0625 to 0.0625
- damp_level: int32 [4096], replicated, may hold values from 1 to 4
Outputs:
- factored: float32 [4096, 4096], P('row', 'col')
All inputs are finite; a program needn't handle non-finite values.
Results may differ from a plain program's by a relative error of at most 0.0033.
Values may be sent and summed in bfloat16 or wider, within the bound.
No kernel may reach another device: no remote copies, remote signals or barrier semaphores. Data moves between devices by JAX's collectives and lax.ppermute only.
A program may use at most 64 MiB of HBM per device.

v0:
```python
import jax
import jax.numpy as jnp
from jax import lax
from jax.sharding import PartitionSpec as P

PANEL = 128


damp_coef = 0.25


def from_root(block, axis, holder):
    block = jnp.where(lax.axis_index(axis) == holder, block, jnp.zeros_like(block))
    return lax.psum(block, axis)


def gram(left_side, right_side):
    return lax.dot_general(
        left_side, right_side, (((0,), (0,)), ((), ())), preferred_element_type=jnp.float32
    )


def solve_panel(lower, row_slab, col_slab):
    right_panel = jax.scipy.linalg.solve_triangular(lower, row_slab, lower=True)
    left_panel = jax.scipy.linalg.solve_triangular(lower, col_slab.T, lower=True).T
    return (left_panel, right_panel)


def apply_panel(tile, left_panel, right_panel, lower, first, row_glob, col_glob):
    row_span, col_span = tile.shape
    width_panel = lower.shape[0]
    beyond = first + width_panel
    trailing = tile - jnp.dot(left_panel, right_panel, precision=lax.Precision.HIGHEST)
    zero_idx = jnp.int32(0)
    row_start = jnp.clip(first - row_glob[0], 0, row_span - width_panel)
    lower_rows = lax.dynamic_update_slice(
        jnp.zeros((row_span, width_panel), jnp.float32), jnp.tril(lower), (row_start, zero_idx)
    )
    row_inside = (row_glob >= first) & (row_glob < beyond)
    col_inside = (col_glob >= first) & (col_glob < beyond)
    fixed_left = jnp.where(row_inside[:, None], lower_rows, left_panel)
    col_start = jnp.clip(first - col_glob[0], 0, col_span - width_panel)
    placed = lax.dynamic_update_slice(
        jnp.zeros((row_span, col_span), jnp.float32), fixed_left, (zero_idx, col_start)
    )
    row_later = row_glob >= beyond
    col_later = col_glob >= beyond
    result = jnp.where(row_later[:, None] & col_later[None, :], trailing, tile)
    result = jnp.where(col_inside[None, :] & (row_glob >= first)[:, None], placed, result)
    result = jnp.where(row_inside[:, None] & col_later[None, :], 0.0, result)
    return result


def shards(activations, out_grads, proj_in, proj_out, damp_level):
    local_ex, tok_len, model_dim = activations.shape
    rank_dim = proj_in.shape[1]
    feats = rank_dim * rank_dim
    n_rows = lax.axis_size("row")
    n_cols = lax.axis_size("col")
    devices = n_rows * n_cols
    total_ex = local_ex * devices
    a_proj = jnp.dot(
        activations.reshape(local_ex * tok_len, model_dim),
        proj_in,
        preferred_element_type=jnp.float32,
    )
    g_proj = jnp.dot(
        out_grads.reshape(local_ex * tok_len, model_dim),
        proj_out,
        preferred_element_type=jnp.float32,
    )
    a_proj = a_proj.reshape(local_ex, tok_len, rank_dim)
    g_proj = g_proj.reshape(local_ex, tok_len, rank_dim)
    outer = jnp.einsum(
        "est,esu->etu", g_proj, a_proj, precision=lax.Precision.HIGHEST
    ) * tok_len ** (-0.5)
    grads = outer.reshape(local_ex, feats).astype(jnp.bfloat16)
    wide = grads.astype(jnp.float32)
    total_sq = lax.psum(jnp.sum(wide * wide), ("row", "col"))
    block = feats // devices
    by_col = (
        grads.reshape(local_ex, n_cols, n_rows, block)
        .transpose(0, 2, 1, 3)
        .reshape(local_ex, feats)
    )
    mine_rows, mine_cols = (
        lax.all_to_all(grads, ("row", "col"), split_axis=1, concat_axis=0, tiled=True),
        lax.all_to_all(by_col, ("row", "col"), split_axis=1, concat_axis=0, tiled=True),
    )
    row_grads = lax.all_gather(mine_rows, "col", axis=1, tiled=True)
    row_span = row_grads.shape[1]
    both_panels = from_root(row_grads[:, : 2 * PANEL], "row", 0)
    left_side = jnp.concatenate([row_grads, both_panels], axis=1)
    extended = gram(left_side, lax.all_gather(mine_cols, "row", axis=1, tiled=True)) / total_ex
    col_span = extended.shape[1]
    row_glob = lax.axis_index("row") * row_span + jnp.arange(row_span, dtype=jnp.int32)
    col_glob = lax.axis_index("col") * col_span + jnp.arange(col_span, dtype=jnp.int32)
    damping = damp_coef * total_sq / (total_ex * feats)
    levels = damp_level.astype(jnp.float32)
    col_damp = damping * lax.dynamic_slice_in_dim(
        levels, lax.axis_index("col") * col_span, col_span
    )
    tile = extended[:row_span] + jnp.where(
        row_glob[:, None] == col_glob[None, :], col_damp[None, :], 0.0
    )
    panel_glob = jnp.arange(2 * PANEL, dtype=jnp.int32)
    panel_damp = damping * levels[: 2 * PANEL]
    strip_rows = extended[row_span:] + jnp.where(
        panel_glob[:, None] == col_glob[None, :], col_damp[None, :], 0.0
    )
    strip_cols = gram(row_grads, both_panels) / total_ex + jnp.where(
        row_glob[:, None] == panel_glob[None, :], panel_damp[None, :], 0.0
    )
    corner = gram(both_panels, both_panels) / total_ex + jnp.where(
        panel_glob[:, None] == panel_glob[None, :], panel_damp[None, :], 0.0
    )
    lower_one = jnp.linalg.cholesky(corner[:PANEL, :PANEL])
    left_one, right_one = solve_panel(lower_one, strip_rows[:PANEL], strip_cols[:, :PANEL])
    corner_left, corner_right = solve_panel(lower_one, corner[:PANEL], corner[:, :PANEL])
    rows_next = strip_rows[PANEL:] - jnp.dot(
        corner_left[PANEL:], right_one, precision=lax.Precision.HIGHEST
    )
    cols_next = strip_cols[:, PANEL:] - jnp.dot(
        left_one, corner_right[:, PANEL:], precision=lax.Precision.HIGHEST
    )
    corner_next = corner[PANEL:, PANEL:] - jnp.dot(
        corner_left[PANEL:], corner_right[:, PANEL:], precision=lax.Precision.HIGHEST
    )
    lower_two = jnp.linalg.cholesky(corner_next)
    left_two, right_two = solve_panel(lower_two, rows_next, cols_next)
    tile = apply_panel(tile, left_one, right_one, lower_one, 0, row_glob, col_glob)
    tile = apply_panel(tile, left_two, right_two, lower_two, PANEL, row_glob, col_glob)
    return tile


def solution(mesh):
    return jax.shard_map(
        shards,
        mesh=mesh,
        in_specs=(P(("row", "col"), None, None), P(("row", "col"), None, None), P(), P(), P()),
        out_specs=P("row", "col"),
        check_vma=False,
    )
```

profile of v0, /device:TPU:0, one launch (start us, length us, event | category | flops | bytes accessed | tf_op | source)
XLA Modules:
  0.0 221.1 jit_solution(7801438504682207365)
XLA Ops:
  6.5 1.2 copy-done
  7.8 4.0 %fusion.8 = f32[8,32,64]{2,1,0:T(8,128)S(1)} fusion(bf16[8,32,8192]{2,1,0:T(8,128)(2,1)} %param.12, bf16[8192,64]{0,1:T(8,128)(2,1)S(1)} %copy-done), kind=kOutput, calls=%fused_computation.20 | convolution fusion | flops 268435456 | bytes 5308416 | tf_op jit(solution)/shard_map/dot_general | solution.py:62
  11.8 1.2 fusion.10
  13.0 1.2 multiply_reduce_fusion
  14.3 0.7 copy.14
  15.0 7.3 %all-to-all-start = ((bf16[8,32,128]{2,0,1:T(8,128)(2,1)}), bf16[8,32,128]{2,0,1:T(8,128)(2,1)S(1)}, u32[]{:S(2)}, u32[]{:S(2)}) async-start(bf16[8,32,128]{2,0,1:T(8,128)(2,1)} %copy.14), calls=%async_computation | async-start | bytes 131072 | tf_op jit(solution)/shard_map/all_to_all | solution.py:87
  22.4 40.7 %psum.15 = f32[]{:T(128)} all-reduce(f32[]{:T(128)} %get-tuple-element.6), channel_id=1, replica_groups=mesh['row'=8,'col'=4] {'row','col'}, use_global_device_ids=true, to_apply=%region_2.3 | all-reduce | flops 1 | bytes 8 | tf_op jit(solution)/shard_map/psum | solution.py:79
  67.2 0.7 copy.23
  67.9 4.7 %all-to-all-start.1 = ((bf16[8,32,128]{2,0,1:T(8,128)(2,1)}), bf16[8,32,128]{2,0,1:T(8,128)(2,1)S(1)}, u32[]{:S(2)}, u32[]{:S(2)}) async-start(bf16[8,32,128]{2,0,1:T(8,128)(2,1)} %bitcast.25), calls=%async_computation.1 | async-start | bytes 131072 | tf_op jit(solution)/shard_map/all_to_all | solution.py:88
  72.6 13.2 %all_gather.6 = bf16[256,512]{1,0:T(8,128)(2,1)S(1)} all-gather(bf16[256,128]{1,0:T(8,128)(2,1)S(1)} %bitcast.92), channel_id=1, replica_groups=mesh['row'=8,'col'=4] {'col'}, dimensions={1}, use_global_device_ids=true | all-gather | bytes 327680 | tf_op jit(solution)/shard_map/all_gather | solution.py:90
  85.8 0.7 slice_select_fusion
  86.6 10.1 %all_gather.7 = bf16[256,1024]{1,0:T(8,128)(2,1)S(1)} all-gather(bf16[256,128]{1,0:T(8,128)(2,1)S(1)} %bitcast.93), channel_id=1, replica_groups=mesh['row'=8,'col'=4] {'row'}, dimensions={1}, use_global_device_ids=true | all-gather | bytes 589824 | tf_op jit(solution)/shard_map/all_gather | solution.py:94
  96.7 42.8 %all-reduce.2.cloned.1.call-done = bf16[256,256]{1,0:T(8,128)(2,1)} async-done(((bf16[256,256]{1,0:T(8,128)(2,1)}), bf16[256,256]{1,0:T(8,128)(2,1)}) %all-reduce.2.cloned.1.call-update) | async-done | bytes 131088 | tf_op jit(solution)/shard_map/psum | solution.py:14
  139.5 1.3 fusion.6
  140.9 11.7 %cholesky.44 = f32[128,128]{1,0:T(8,128)S(1)} custom-call(f32[128,128]{1,0:T(8,128)S(1)} %fusion.29), custom_call_target="Cholesky" | custom-call | tf_op jit(solution)/shard_map/jit(cholesky)/cholesky | solution.py:117
  153.3 0.7 fusion.70
  153.9 0.7 select_select_fusion.1
  154.6 9.8 %custom-call.14 = f32[1,128,128]{1,2,0:T(8,128)S(1)} custom-call(f32[1,128,128]{2,1,0:T(8,128)S(1)} %fusion.70), custom_call_target="InvertDiagBlocksLowerTriangular" | custom-call | tf_op jit(solution)/shard_map/jit(_solve_triangular)/triangular_solve | solution.py:25
  165.4 11.7 %cholesky.55 = f32[128,128]{1,0:T(8,128)S(1)} custom-call(f32[128,128]{1,0:T(8,128)S(1)} %fusion.24), custom_call_target="Cholesky" | custom-call | tf_op jit(solution)/shard_map/jit(cholesky)/cholesky | solution.py:129
  177.8 0.7 fusion.69
  178.5 0.7 select_select_fusion
  179.3 0.9 dynamic_update_slice.14
  183.8 3.2 %fusion.49 = f32[512,1024]{1,0:T(8,128)} fusion(f32[128,512]{1,0:T(8,128)S(1)} %get-tuple-element.14, f32[128,1024]{1,0:T(8,128)S(1)} %fusion.12), kind=kOutput, calls=%fused_computation.83 | convolution fusion | flops 805306368 | bytes 2883584 | tf_op jit(solution)/shard_map/dot_general | solution.py:33
  187.0 9.8 %custom-call.17 = f32[1,128,128]{1,2,0:T(8,128)S(1)} custom-call(f32[1,128,128]{2,1,0:T(8,128)S(1)} %fusion.69), custom_call_target="InvertDiagBlocksLowerTriangular" | custom-call | tf_op jit(solution)/shard_map/jit(_solve_triangular)/triangular_solve | solution.py:25
  197.0 0.7 dynamic_update_slice.12
  197.7 1.2 bitcast_select_fusion.1
  198.9 0.8 copy.20
  199.7 1.4 fusion.20
  201.4 2.3 %dynamic_update_slice.13 = f32[512,1024]{1,0:T(8,128)S(1)} dynamic-update-slice(f32[512,1024]{1,0:T(8,128)S(1)} %broadcast_in_dim.99.clone, f32[512,128]{1,0:T(8,128)} %copy.20, s32[]{:T(128)} %constant.102.clone.1, s32[]{:T(128)} %bitcast.20) | dynamic-update-slice | bytes 524292 | tf_op jit(solution)/shard_map/dynamic_update_slice | solution.py:43
  203.7 1.3 copy-done.2
  205.3 1.9 dynamic_update_slice.15
  207.2 7.1 %fusion.3 = f32[512,1024]{1,0:T(8,128)} fusion(f32[512,1024]{1,0:T(8,128)} %copy-done.2, f32[512,1024]{1,0:T(8,128)S(1)} %dynamic_update_slice.15, f32[512,1024]{1,0:T(8,128)} %fusion.49, f32[768,1024]{1,0:T(8,128)} %copy-done.1, f32[128,512]{1,0:T(8,128)} %get-tuple-element.12, f32[128,1024]{1,0:T(8,128)} %fusion.20, ...), kind=kOutput, calls=%fused_computation.5 | convolution fusion | flops 814219264 | bytes 11289088 | tf_op jit(solution)/shard_map/dot_general | solution.py:33
  (56 shorter events, 8.2 us)
Async XLA Ops:
  6.5 1.2 copy-start
  6.5 5.2 %copy-start.6 = (bf16[8192,64]{0,1:T(8,128)(2,1)S(1)}, bf16[8192,64]{0,1:T(8,128)(2,1)}, u32[]{:S(2)}) copy-start(bf16[8192,64]{0,1:T(8,128)(2,1)} %param.15) | copy-start | bytes 3145732
  6.5 5.2 %copy-start.5 = (bf16[8,32,8192]{2,1,0:T(8,128)(2,1)S(1)}, bf16[8,32,8192]{2,1,0:T(8,128)(2,1)}, u32[]{:S(2)}) copy-start(bf16[8,32,8192]{2,1,0:T(8,128)(2,1)} %param.13) | copy-start | bytes 12582916
  11.7 10.6 %copy-start.4 = (s32[4096]{0:T(1024)S(1)}, s32[4096]{0:T(1024)}, u32[]{:S(2)}) copy-start(s32[4096]{0:T(1024)} %param.16) | copy-start | bytes 49156
  15.0 52.9 %all-to-all-start = ((bf16[8,32,128]{2,0,1:T(8,128)(2,1)}), bf16[8,32,128]{2,0,1:T(8,128)(2,1)S(1)}, u32[]{:S(2)}, u32[]{:S(2)}) async-start(bf16[8,32,128]{2,0,1:T(8,128)(2,1)} %copy.14), calls=%async_computation | async-start | bytes 131072 | tf_op jit(solution)/shard_map/all_to_all | solution.py:87
  67.9 18.7 %all-to-all-start.1 = ((bf16[8,32,128]{2,0,1:T(8,128)(2,1)}), bf16[8,32,128]{2,0,1:T(8,128)(2,1)S(1)}, u32[]{:S(2)}, u32[]{:S(2)}) async-start(bf16[8,32,128]{2,0,1:T(8,128)(2,1)} %bitcast.25), calls=%async_computation.1 | async-start | bytes 131072 | tf_op jit(solution)/shard_map/all_to_all | solution.py:88
  72.6 66.9 %all-reduce.2.cloned.1.call-start = ((), (), s32[]{:S(2)}) async-start(), calls=%async_computation.2 | async-start | bytes 262144 | tf_op jit(solution)/shard_map/psum | solution.py:14
  139.5 40.7 %copy-start.3 = (bf16[256,256]{1,0:T(8,128)(2,1)S(1)}, bf16[256,256]{1,0:T(8,128)(2,1)}, u32[]{:S(2)}) copy-start(bf16[256,256]{1,0:T(8,128)(2,1)} %all-reduce.2.cloned.1.call-done) | copy-start | bytes 393220
  182.1 1.7 copy-start.1
  203.7 1.3 copy-start.2
Sparse Core Ops, SparseCore 0:
  86.7 52.7 all-reduce.1
where the time goes:
time: 222 us; the launch traced here: 221 us
  blocking collectives  64.1 us (29%)
  other arithmetic  47.9 us (22%)
  waiting for transfers between devices  42.8 us (19%)
  matrix products  24.6 us (11%)
  between operations  16.8 us (8%)
  local copies, waits for them, and re-layouts  13 us (6%)
  starting transfers between devices  12 us (5%)
    psum x1, waiting for transfers between devices, from_root(): return lax.psum(block, axis)  42.8 us
    psum x1, blocking collectives, shards(): total_sq = lax.psum(jnp.sum(wide * wide), ('row', 'col'))  40.7 us
    another operation x5, other arithmetic, solve_panel(): jax.scipy.linalg.solve_triangular(lower, col_slab.T, lower=True)  21.6 us
    all_gather x1, blocking collectives, shards(): row_grads = lax.all_gather(mine_rows, 'col', axis=1, tiled=True)  13.2 us
    another operation x3, other arithmetic, shards(): lower_one = jnp.linalg.cholesky(corner[:PANEL, :PANEL])  12.4 us
    another operation x3, other arithmetic, shards(): lower_two = jnp.linalg.cholesky(corner_next)  12.4 us
    dot_general x2, matrix products, apply_panel(): jnp.dot(left_panel, right_panel, precision=lax.Precision.HIGHEST)  10.3 us
    all_gather x1, blocking collectives, shards(): lax.all_gather(mine_cols, 'row', axis=1, tiled=True)  10.1 us
  transfers between devices with their start and end apart: 3, of which 1 were waited for; matrix products, arithmetic and copies ran while one was open for 1% of the time, Pallas kernels for 0%

commit v1 on v0

v1 whole, which is shorter than its diff:
```python
import functools

import jax
import jax.numpy as jnp
from jax import lax
from jax.experimental import pallas as pl
from jax.experimental.pallas import tpu as pltpu
from jax.sharding import PartitionSpec as P

PANEL = 128
BOTH = 2 * PANEL
LANES = 128
SUB = 8
STRIP = 64

damp_coef = 0.25

HIGHEST = lax.Precision.HIGHEST
FIRSTS = (((0,), (0,)), ((), ()))
LASTS = (((1,), (1,)), ((), ()))
PLAIN = (((1,), (0,)), ((), ()))


def mxu(left, right, dims=PLAIN):
    return lax.dot_general(left, right, dims, preferred_element_type=jnp.float32)


def halves(value):
    high = value.astype(jnp.bfloat16)
    return high, (value - high.astype(jnp.float32)).astype(jnp.bfloat16)


def project_kernel(act_ref, out_ref, in_ref, proj_ref, packed_ref, a_acc, g_acc, *, local_ex, tok_len):
    step = pl.program_id(0)

    @pl.when(step == 0)
    def _():
        a_acc[...] = jnp.zeros_like(a_acc)
        g_acc[...] = jnp.zeros_like(g_acc)

    a_acc[...] += mxu(act_ref[...], in_ref[...])
    g_acc[...] += mxu(out_ref[...], proj_ref[...])

    @pl.when(step == pl.num_programs(0) - 1)
    def _():
        a_proj = a_acc[...]
        tokens, rank_dim = a_proj.shape
        pairs = rank_dim * rank_dim // LANES
        g_turned = g_acc[...].T
        example = lax.broadcasted_iota(jnp.int32, (local_ex, tokens), 0)
        owner = lax.broadcasted_iota(jnp.int32, (local_ex, tokens), 1) // tok_len
        own = jnp.where(example == owner, tok_len ** (-0.5), 0.0).astype(jnp.float32)
        per_pair = LANES // rank_dim
        parts = []
        for part in range(per_pair):
            spread = jnp.concatenate(
                [
                    g_turned[pair * per_pair + part : pair * per_pair + part + 1, :] * own
                    for pair in range(pairs)
                ],
                axis=0,
            )
            parts.append(jnp.dot(spread, a_proj, precision=HIGHEST))
        grads = jnp.concatenate(parts, axis=1).astype(jnp.bfloat16)
        wide = grads.astype(jnp.float32)
        square = jnp.sum(jnp.sum(wide * wide, axis=0, keepdims=True), axis=1, keepdims=True)
        rows = pairs * local_ex
        packed_ref[:rows, :] = grads
        row_at = lax.broadcasted_iota(jnp.int32, (local_ex, LANES), 0)
        lane_at = lax.broadcasted_iota(jnp.int32, (local_ex, LANES), 1)
        first = square.astype(jnp.bfloat16).astype(jnp.float32)
        second = (square - first).astype(jnp.bfloat16).astype(jnp.float32)
        third = square - first - second
        coded = jnp.where(
            lane_at == 0, first, jnp.where(lane_at == 1, second, jnp.where(lane_at == 2, third, 0.0))
        )
        packed_ref[rows:, :] = jnp.where(row_at == 0, coded, 0.0).astype(jnp.bfloat16)


def project(activations, out_grads, proj_in, proj_out):
    local_ex, tok_len, model_dim = activations.shape
    rank_dim = proj_in.shape[1]
    tokens = local_ex * tok_len
    pairs = rank_dim * rank_dim // LANES
    chunk = 1024
    packed = pl.pallas_call(
        functools.partial(project_kernel, local_ex=local_ex, tok_len=tok_len),
        grid=(model_dim // chunk,),
        in_specs=[
            pl.BlockSpec((tokens, chunk), lambda d: (0, d)),
            pl.BlockSpec((tokens, chunk), lambda d: (0, d)),
            pl.BlockSpec((chunk, rank_dim), lambda d: (d, 0)),
            pl.BlockSpec((chunk, rank_dim), lambda d: (d, 0)),
        ],
        out_specs=pl.BlockSpec(((pairs + 1) * local_ex, LANES), lambda d: (0, 0)),
        out_shape=jax.ShapeDtypeStruct(((pairs + 1) * local_ex, LANES), jnp.bfloat16),
        scratch_shapes=[
            pltpu.VMEM((tokens, rank_dim), jnp.float32),
            pltpu.VMEM((tokens, rank_dim), jnp.float32),
        ],
        compiler_params=pltpu.CompilerParams(vmem_limit_bytes=32 * 2**20),
        name="project",
    )(
        activations.reshape(tokens, model_dim),
        out_grads.reshape(tokens, model_dim),
        proj_in,
        proj_out,
    )
    return packed.reshape(pairs + 1, local_ex, LANES)


def eliminate(work_ref, done_ref):
    tiles = BOTH // LANES
    sub_at = lax.broadcasted_iota(jnp.int32, (SUB, LANES), 0)
    lane_at = lax.broadcasted_iota(jnp.int32, (SUB, LANES), 1)
    for start in range(0, BOTH, STRIP):
        here = start // LANES
        live = list(range(here, tiles)) + list(range(tiles, tiles + here + 1))
        groups = STRIP // SUB
        rows = [
            {t: work_ref[start + g * SUB : start + (g + 1) * SUB, t * LANES : (t + 1) * LANES] for t in live}
            for g in range(groups)
        ]
        pivots = [jnp.ones((SUB, LANES), jnp.float32) for _ in range(groups)]

        def column(index):
            lane = (start + index) % LANES
            return [
                jnp.broadcast_to(rows[g][here][:, lane : lane + 1], (SUB, LANES)) if g >= index // SUB else None
                for g in range(groups)
            ]

        now = column(0)
        for index in range(STRIP):
            g_now, s_now = divmod(index, SUB)
            pivot = now[g_now][s_now : s_now + 1, :]
            inverse = 1.0 / pivot
            pivots[g_now] = jnp.where(sub_at == s_now, pivot, pivots[g_now])
            later = None
            if index + 1 < STRIP:
                g_next, s_next = divmod(index + 1, SUB)
                raw = column(index + 1)
                factor = now[g_next][s_next : s_next + 1, :] * inverse
                later = [
                    raw[g] - now[g] * factor if g >= g_next else None for g in range(groups)
                ]
            scaled = {t: rows[g_now][t][s_now : s_now + 1, :] * inverse for t in live}
            for g in range(g_now, groups):
                weight = now[g]
                if g == g_now:
                    if s_now == SUB - 1:
                        continue
                    weight = jnp.where(sub_at > s_now, weight, 0.0)
                for t in live:
                    rows[g][t] = rows[g][t] - weight * scaled[t]
            now = later
        for g in range(groups):
            root = lax.rsqrt(pivots[g])
            for t in range(2 * tiles):
                at = slice(start + g * SUB, start + (g + 1) * SUB), slice(t * LANES, (t + 1) * LANES)
                if t not in live:
                    done_ref[at] = jnp.zeros((SUB, LANES), jnp.float32)
                    continue
                value = rows[g][t] * root
                if t == here:
                    value = jnp.where(lane_at + t * LANES >= sub_at + start + g * SUB, value, 0.0)
                done_ref[at] = value
        beyond = start + STRIP
        if beyond < BOTH:
            first = beyond // LANES * LANES
            last = BOTH + -(-beyond // LANES) * LANES
            right = done_ref[start:beyond, first:last]
            cuts = [beyond, beyond + STRIP] + ([BOTH] if beyond + STRIP < BOTH else [])
            for low, high in zip(cuts[:-1], cuts[1:]):
                left = done_ref[start:beyond, low:high]
                work_ref[low:high, first:last] -= lax.dot_general(
                    left, right, FIRSTS, precision=HIGHEST, preferred_element_type=jnp.float32
                )


def fisher_kernel(
    place_ref, level_ref, panel_level_ref, *refs, sources, row_blocks, col_blocks, total_ex, feats
):
    arrived = refs[:sources]
    out_ref = refs[sources]
    g_row, g_col, g_panel, work, done, lower, mix_high, mix_low, panel_mix, damp_ref = refs[sources + 1 :]
    step = pl.program_id(0)
    row_at, col_at = place_ref[0], place_ref[1]
    panel_blocks = BOTH // LANES
    here = arrived[0].shape[1]

    @pl.when(step == 0)
    def _():
        row_base = lax.rem(row_at, 2) * row_blocks
        col_base = 2 * row_blocks
        panel_base = col_base + col_blocks
        total = jnp.zeros((here, LANES), jnp.float32)
        for n, piece in enumerate(arrived):
            at = slice(n * here, (n + 1) * here)
            for b in range(panel_blocks):
                g_panel[at, b * LANES : (b + 1) * LANES] = piece[panel_base + b]
            for b in range(row_blocks):
                g_row[at, b * LANES : (b + 1) * LANES] = piece[row_base + b]
            for b in range(col_blocks):
                g_col[b // panel_blocks, at, b % panel_blocks * LANES : (b % panel_blocks + 1) * LANES] = piece[
                    col_base + b
                ]
            total += piece[panel_base + panel_blocks].astype(jnp.float32)
        total_sq = jnp.sum(jnp.sum(total, axis=0, keepdims=True), axis=1, keepdims=True)
        damping = damp_coef * total_sq / (total_ex * feats)
        damp_ref[...] = jnp.broadcast_to(damping, damp_ref.shape)
        panel = g_panel[...]
        rows_at = lax.broadcasted_iota(jnp.int32, (BOTH, BOTH), 0)
        cols_at = lax.broadcasted_iota(jnp.int32, (BOTH, BOTH), 1)
        same = rows_at == cols_at
        work[:, :BOTH] = mxu(panel, panel, FIRSTS) * (1.0 / total_ex) + jnp.where(
            same, damping * panel_level_ref[...], 0.0
        )
        work[:, BOTH:] = jnp.where(same, 1.0, 0.0)
        eliminate(work, done)
        lower[...] = done[:, :BOTH].T
        w_high, w_low = halves(done[:, BOTH:])
        mixed = mxu(panel, w_high, LASTS) + mxu(panel, w_low, LASTS)
        y_high, y_low = halves(mixed)
        cross = mxu(y_high, y_low, LASTS)
        outer = mxu(y_high, y_high, LASTS) + cross + cross.T
        ex_rows = lax.broadcasted_iota(jnp.int32, outer.shape, 0)
        ex_cols = lax.broadcasted_iota(jnp.int32, outer.shape, 1)
        mix = (jnp.where(ex_rows == ex_cols, 1.0, 0.0) - outer * (1.0 / total_ex)) * (1.0 / total_ex)
        mix_high[...], mix_low[...] = halves(mix)
        panel_mix[...] = mixed * (1.0 / total_ex)

    in_panel = (col_at == 0) & (step == 0)
    cols = g_col[step]
    weights = mxu(mix_high[...], cols) + mxu(mix_low[...], cols)
    weights = jnp.where(in_panel, panel_mix[...], weights)
    high, low = halves(weights)
    rows = g_row[...]
    tile = mxu(rows, high, FIRSTS) + mxu(rows, low, FIRSTS)
    row_span, width = tile.shape
    col_first = (col_at * pl.num_programs(0) + step) * width
    row_glob = row_at * row_span + lax.broadcasted_iota(jnp.int32, tile.shape, 0)
    col_glob = col_first + lax.broadcasted_iota(jnp.int32, tile.shape, 1)
    out_ref[...] = tile + jnp.where(row_glob == col_glob, damp_ref[0:1, 0:1] * level_ref[...], 0.0)

    @pl.when(row_at == 0)
    def _():
        out_ref[:BOTH, :] = jnp.where(in_panel, lower[...], 0.0)


def fisher(place, col_levels, panel_levels, arrived, row_blocks, col_blocks, total_ex, feats):
    row_span, col_span = row_blocks * LANES, col_blocks * LANES
    sources = len(arrived)
    examples = sources * arrived[0].shape[1]
    vmem = pl.BlockSpec(memory_space=pltpu.VMEM)
    return pl.pallas_call(
        functools.partial(
            fisher_kernel,
            sources=sources,
            row_blocks=row_blocks,
            col_blocks=col_blocks,
            total_ex=total_ex,
            feats=feats,
        ),
        grid=(col_span // BOTH,),
        in_specs=[
            pl.BlockSpec(memory_space=pltpu.SMEM),
            pl.BlockSpec((1, BOTH), lambda n: (0, n)),
            vmem,
        ]
        + [vmem] * sources,
        out_specs=pl.BlockSpec((row_span, BOTH), lambda n: (0, n)),
        out_shape=jax.ShapeDtypeStruct((row_span, col_span), jnp.float32),
        scratch_shapes=[
            pltpu.VMEM((examples, row_span), jnp.bfloat16),
            pltpu.VMEM((col_span // BOTH, examples, BOTH), jnp.bfloat16),
            pltpu.VMEM((examples, BOTH), jnp.bfloat16),
            pltpu.VMEM((BOTH, 2 * BOTH), jnp.float32),
            pltpu.VMEM((BOTH, 2 * BOTH), jnp.float32),
            pltpu.VMEM((BOTH, BOTH), jnp.float32),
            pltpu.VMEM((examples, examples), jnp.bfloat16),
            pltpu.VMEM((examples, examples), jnp.bfloat16),
            pltpu.VMEM((examples, BOTH), jnp.float32),
            pltpu.VMEM((SUB, LANES), jnp.float32),
        ],
        compiler_params=pltpu.CompilerParams(vmem_limit_bytes=48 * 2**20),
        name="fisher",
    )(place, col_levels, panel_levels, *arrived)


def swap(block, axis, mask):
    size = lax.axis_size(axis)
    return lax.ppermute(block, axis, [(n, n ^ mask) for n in range(size)])


def shards(activations, out_grads, proj_in, proj_out, damp_level):
    local_ex = activations.shape[0]
    feats = proj_in.shape[1] * proj_out.shape[1]
    n_rows = lax.axis_size("row")
    n_cols = lax.axis_size("col")
    total_ex = local_ex * n_rows * n_cols
    row_at = lax.axis_index("row")
    col_at = lax.axis_index("col")
    blocks = feats // LANES
    row_blocks = blocks // n_rows
    col_blocks = blocks // n_cols

    levels = damp_level.astype(jnp.float32).reshape(1, feats)
    col_levels = lax.dynamic_slice_in_dim(levels, col_at * col_blocks * LANES, col_blocks * LANES, axis=1)
    place = jnp.stack([row_at, col_at]).astype(jnp.int32)

    packed = project(activations, out_grads, proj_in, proj_out)
    along = [packed] + [swap(packed, "col", mask) for mask in range(n_cols - 1, 0, -1)]
    line = jnp.concatenate(along, axis=1)

    common = [
        lax.dynamic_slice_in_dim(line, col_at * col_blocks, col_blocks),
        line[: BOTH // LANES],
        line[blocks:],
    ]
    pair_at = row_at // 2

    def bundle(pair):
        wanted = lax.dynamic_slice_in_dim(line, pair * 2 * row_blocks, 2 * row_blocks)
        return jnp.concatenate([wanted] + common)

    own = bundle(pair_at)
    got = [own] + [swap(bundle(pair_at ^ mask), "row", 2 * mask) for mask in range(1, n_rows // 2)]
    arrived = got + [swap(piece, "row", 1) for piece in got]
    return fisher(
        place, col_levels, levels[:, :BOTH], arrived, row_blocks, col_blocks, total_ex, feats
    )


def solution(mesh):
    return jax.shard_map(
        shards,
        mesh=mesh,
        in_specs=(P(("row", "col"), None, None), P(("row", "col"), None, None), P(), P(), P()),
        out_specs=P("row", "col"),
        check_vma=False,
    )
```

time: 222 us -> 54.7 us (0.25)
  blocking collectives: 64.1 us -> 0 us
  other arithmetic: 47.9 us -> 0.2 us
  waiting for transfers between devices: 42.8 us -> 12.9 us
  matrix products: 24.6 us -> 0 us
  Pallas kernels: 0 us -> 21.6 us
  between operations: 16.8 us -> 0.08 us
  local copies, waits for them, and re-layouts: 13 us -> 9.89 us
    another operation x11 -> x1, other arithmetic: 46.4 us -> 0.08 us  [shards(): place = jnp.stack([row_at, col_at]).astype(jnp.int32)]
    psum x1 -> x0, waiting for transfers between devices: 42.8 us -> none  [from_root(): return lax.psum(block, axis)]
    psum x1 -> x0, blocking collectives: 40.7 us -> none  [shards(): total_sq = lax.psum(jnp.sum(wide * wide), ('row', 'col'))]
    all_gather x2 -> x0, blocking collectives: 23.4 us -> none  [the longest x1 13.2 us: shards(): row_grads = lax.all_gather(mine_rows, 'col', axis=1, tiled=True)]
    pallas_call x0 -> x2, Pallas kernels: none -> 21.6 us  [the longest x1 16.7 us: fisher(): pl.pallas_call(functools.partial(fisher_kernel, sources=sources, row_bloc...]
    dot_general x11 -> x0, matrix products: 20.3 us -> none  [the longest x2 10.3 us: apply_panel(): jnp.dot(left_panel, right_panel, precision=lax.Precision.HIGHEST)]
    ppermute x0 -> x10, waiting for transfers between devices: none -> 12.9 us  [swap(): return lax.ppermute(block, axis, [(n, n ^ mask) for n in range(size)])]
    all_to_all x2 -> x0, starting transfers between devices: 12 us -> none  [the longest x1 7.3 us: shards(): lax.all_to_all(grads, ('row', 'col'), split_axis=1, concat_axis=0, tiled=...]
  transfers between devices with their start and end apart: 3 -> 10, of which waited for: 1 -> 6; matrix products, arithmetic and copies ran while one was open for 1% -> 0% of each run, Pallas kernels for 0% -> 0%
where the time goes in v1:
time: 54.7 us; the launch traced here: 54.5 us
  Pallas kernels  21.6 us (39%)
  waiting for transfers between devices  12.9 us (24%)
  local copies, waits for them, and re-layouts  9.89 us (18%)
  starting transfers between devices  9.81 us (18%)
    pallas_call x1, Pallas kernels, fisher(): pl.pallas_call(functools.partial(fisher_kernel, sources=sources, row_bloc...  16.7 us
    ppermute x10, waiting for transfers between devices, swap(): return lax.ppermute(block, axis, [(n, n ^ mask) for n in range(size)])  12.9 us
    unnamed x12, local copies, waits for them, and re-layouts  9.85 us
    ppermute x10, starting transfers between devices, swap(): return lax.ppermute(block, axis, [(n, n ^ mask) for n in range(size)])  9.81 us
    pallas_call x1, Pallas kernels, project(): pl.pallas_call(functools.partial(project_kernel, local_ex=local_ex, tok_l...  4.89 us
  transfers between devices with their start and end apart: 10, of which 6 were waited for; matrix products, arithmetic and copies ran while one was open for 0% of the time, Pallas kernels for 0%

profile of v1, /device:TPU:0, one launch (start us, length us, event | category | flops | bytes accessed | tf_op | source)
XLA Modules:
  0.0 54.5 jit_solution(5578887473004004246)
XLA Ops:
  0.0 0.0 copy-start.3
  0.0 2.1 %copy.6.in_ref = bf16[8192,64]{1,0:T(8,128)(2,1)S(1)} copy(bf16[8192,64]{0,1:T(8,128)(2,1)} %param.7) | data formatting | bytes 2097152 | tf_op args[2]
  2.1 0.0 copy-done.3
  2.1 1.8 %copy.7.proj_ref = bf16[8192,64]{1,0:T(8,128)(2,1)} copy(bf16[8192,64]{0,1:T(8,128)(2,1)S(1)} %copy-done.3) | data formatting | bytes 2097152 | tf_op args[3]
  3.9 1.6 %copy-done = bf16[8192,64]{1,0:T(8,128)(2,1)S(1)} copy-done((bf16[8192,64]{1,0:T(8,128)(2,1)S(1)}, bf16[8192,64]{1,0:T(8,128)(2,1)}, u32[]{:S(2)}) %copy-start) | copy-done | bytes 1048600
  5.5 2.2 %copy-done.1 = bf16[8,32,8192]{2,1,0:T(8,128)(2,1)S(1)} copy-done((bf16[8,32,8192]{2,1,0:T(8,128)(2,1)S(1)}, bf16[8,32,8192]{2,1,0:T(8,128)(2,1)}, u32[]{:S(2)}) %copy-start.1) | copy-done | bytes 4194328
  7.7 2.2 %copy-done.2 = bf16[8,32,8192]{2,1,0:T(8,128)(2,1)S(1)} copy-done((bf16[8,32,8192]{2,1,0:T(8,128)(2,1)S(1)}, bf16[8,32,8192]{2,1,0:T(8,128)(2,1)}, u32[]{:S(2)}) %copy-start.2) | copy-done | bytes 4194328
  9.9 4.9 %project.1 = bf16[264,128]{1,0:T(8,128)(2,1)S(1)} custom-call(bf16[256,8192]{1,0:T(8,128)(2,1)S(1)} %bitcast.7, bf16[256,8192]{1,0:T(8,128)(2,1)S(1)} %bitcast.8, bf16[8192,64]{1,0:T(8,128)(2,1)S(1)} %copy.6.in_ref, bf16[8192,64]{1,0:T(8,128)(2,1)S(1)} %copy-done), custom_call_target="tpu_custom_call" | custom-call | tf_op jit(solution)/shard_map/project/pallas_call | solution.py:86
  14.8 5.1 %collective-permute-start = (bf16[33,8,128]{2,1,0:T(8,128)(2,1)S(1)}, bf16[33,8,128]{2,1,0:T(8,128)(2,1)S(1)}, u32[]{:S(2)}, u32[]{:S(2)}) collective-permute-start(bf16[33,8,128]{2,1,0:T(8,128)(2,1)S(1)} %bitcast.9), channel_id=1, source_target_pairs={{0,3},{1,2},{2,1},{3,0},{4,7},{5,6},{6,5},{7,4},{8,11},{9,10},{10,... | collective-permute-start | bytes 202760 | tf_op jit(solution)/shard_map/ppermute | solution.py:293
  19.9 0.0 collective-permute-start.1
  19.9 0.6 %collective-permute-start.2 = (bf16[33,8,128]{2,1,0:T(8,128)(2,1)S(1)}, bf16[33,8,128]{2,1,0:T(8,128)(2,1)S(1)}, u32[]{:S(2)}, u32[]{:S(2)}) collective-permute-start(bf16[33,8,128]{2,1,0:T(8,128)(2,1)S(1)} %bitcast.11), channel_id=1, source_target_pairs={{0,1},{1,0},{2,3},{3,2},{4,5},{5,4},{6,7},{7,6},{8,9},{9,8},{10,11... | collective-permute-start | bytes 202760 | tf_op jit(solution)/shard_map/ppermute | solution.py:293
  20.5 2.0 %collective-permute-done = bf16[33,8,128]{2,1,0:T(8,128)(2,1)S(1)} collective-permute-done((bf16[33,8,128]{2,1,0:T(8,128)(2,1)S(1)}, bf16[33,8,128]{2,1,0:T(8,128)(2,1)S(1)}, u32[]{:S(2)}, u32[]{:S(2)}) %collective-permute-start) | collective-permute-done | bytes 67616 | tf_op jit(solution)/shard_map/ppermute | solution.py:293
  22.5 3.1 %collective-permute-done.1 = bf16[33,8,128]{2,1,0:T(8,128)(2,1)S(1)} collective-permute-done((bf16[33,8,128]{2,1,0:T(8,128)(2,1)S(1)}, bf16[33,8,128]{2,1,0:T(8,128)(2,1)S(1)}, u32[]{:S(2)}, u32[]{:S(2)}) %collective-permute-start.1) | collective-permute-done | bytes 67616 | tf_op jit(solution)/shard_map/ppermute | solution.py:293
  25.6 0.0 collective-permute-done.2
  25.7 0.1 pad_maximum_fusion
  25.8 1.6 %collective-permute-start.3 = (bf16[19,32,128]{2,1,0:T(8,128)(2,1)S(1)}, bf16[19,32,128]{2,1,0:T(8,128)(2,1)S(1)}, u32[]{:S(2)}, u32[]{:S(2)}) collective-permute-start(bf16[19,32,128]{2,1,0:T(8,128)(2,1)S(1)} %get-tuple-element.11), channel_id=1, source_target_pairs={{0,8},{4,12},{8,0},{12,4},{16,24},{20,28},{24,16},{28,20},{1,9},{5... | collective-permute-start | bytes 466952 | tf_op jit(solution)/shard_map/ppermute | solution.py:293
  27.4 1.5 %collective-permute-start.4 = (bf16[19,32,128]{2,1,0:T(8,128)(2,1)S(1)}, bf16[19,32,128]{2,1,0:T(8,128)(2,1)S(1)}, u32[]{:S(2)}, u32[]{:S(2)}) collective-permute-start(bf16[19,32,128]{2,1,0:T(8,128)(2,1)S(1)} %get-tuple-element.12), channel_id=1, source_target_pairs={{0,16},{4,20},{8,24},{12,28},{16,0},{20,4},{24,8},{28,12},{1,17},{... | collective-permute-start | bytes 466952 | tf_op jit(solution)/shard_map/ppermute | solution.py:293
  28.9 0.5 collective-permute-start.5
  29.4 0.0 collective-permute-start.6
  29.4 2.7 %collective-permute-done.3.refs_1_ = bf16[19,32,128]{2,1,0:T(8,128)(2,1)S(1)} collective-permute-done((bf16[19,32,128]{2,1,0:T(8,128)(2,1)S(1)}, bf16[19,32,128]{2,1,0:T(8,128)(2,1)S(1)}, u32[]{:S(2)}, u32[]{:S(2)}) %collective-permute-start.3) | collective-permute-done | bytes 155680 | tf_op jit(solution)/shard_map/ppermute | solution.py:293
  32.1 0.0 collective-permute-start.7
  32.1 4.1 %collective-permute-done.4.refs_2_ = bf16[19,32,128]{2,1,0:T(8,128)(2,1)S(1)} collective-permute-done((bf16[19,32,128]{2,1,0:T(8,128)(2,1)S(1)}, bf16[19,32,128]{2,1,0:T(8,128)(2,1)S(1)}, u32[]{:S(2)}, u32[]{:S(2)}) %collective-permute-start.4) | collective-permute-done | bytes 155680 | tf_op jit(solution)/shard_map/ppermute | solution.py:293
  36.2 0.0 collective-permute-start.8
  36.2 0.0 collective-permute-done.5.refs_3_
  36.2 0.5 collective-permute-start.9
  36.7 0.0 copy-done.4
  36.7 0.1 pad_add_fusion.place_ref
  36.8 0.0 collective-permute-done.6.refs_4_
  36.8 0.0 collective-permute-done.7.refs_5_
  36.8 0.8 %collective-permute-done.8.refs_6_ = bf16[19,32,128]{2,1,0:T(8,128)(2,1)S(1)} collective-permute-done((bf16[19,32,128]{2,1,0:T(8,128)(2,1)S(1)}, bf16[19,32,128]{2,1,0:T(8,128)(2,1)S(1)}, u32[]{:S(2)}, u32[]{:S(2)}) %collective-permute-start.8) | collective-permute-done | bytes 155680 | tf_op jit(solution)/shard_map/ppermute | solution.py:293
  37.6 0.2 collective-permute-done.9.refs_7_
  37.8 16.7 %fisher.1 = f32[512,1024]{1,0:T(8,128)} custom-call(s32[2]{0:T(128)S(1)} %pad_add_fusion.place_ref, f32[1,1024]{1,0:T(1,128)S(1)} %bitcast.13, f32[1,256]{1,0:T(1,128)S(1)} %slice.12.panel_level_ref, bf16[19,32,128]{2,1,0:T(8,128)(2,1)S(1)} %get-tuple-element.13.refs_0_, bf16[19,32,128]{2,1,0:T(8,128)(2,1)S(1)} %collective-permute-done.3.refs_1_, ...), custom_call_target="tpu_custom_call" | custom-call | tf_op jit(solution)/shard_map/fisher/pallas_call | solution.py:256
  (11 shorter events, 0.1 us)
Async XLA Ops:
  0.0 2.1 %copy-start.3 = (bf16[8192,64]{0,1:T(8,128)(2,1)S(1)}, bf16[8192,64]{0,1:T(8,128)(2,1)}, u32[]{:S(2)}) copy-start(bf16[8192,64]{0,1:T(8,128)(2,1)} %param.8) | copy-start | bytes 3145732
  3.9 1.6 %copy-start = (bf16[8192,64]{1,0:T(8,128)(2,1)S(1)}, bf16[8192,64]{1,0:T(8,128)(2,1)}, u32[]{:S(2)}) copy-start(bf16[8192,64]{1,0:T(8,128)(2,1)} %copy.7.proj_ref) | copy-start | bytes 3145732
  5.5 2.2 %copy-start.1 = (bf16[8,32,8192]{2,1,0:T(8,128)(2,1)S(1)}, bf16[8,32,8192]{2,1,0:T(8,128)(2,1)}, u32[]{:S(2)}) copy-start(bf16[8,32,8192]{2,1,0:T(8,128)(2,1)} %param.5) | copy-start | bytes 12582916
  7.7 2.2 %copy-start.2 = (bf16[8,32,8192]{2,1,0:T(8,128)(2,1)S(1)}, bf16[8,32,8192]{2,1,0:T(8,128)(2,1)}, u32[]{:S(2)}) copy-start(bf16[8,32,8192]{2,1,0:T(8,128)(2,1)} %param.6) | copy-start | bytes 12582916
  14.8 22.0 %copy-start.4 = (s32[4096]{0:T(1024)S(1)}, s32[4096]{0:T(1024)}, u32[]{:S(2)}) copy-start(s32[4096]{0:T(1024)} %param.9) | copy-start | bytes 49156
  14.8 7.7 %collective-permute-start = (bf16[33,8,128]{2,1,0:T(8,128)(2,1)S(1)}, bf16[33,8,128]{2,1,0:T(8,128)(2,1)S(1)}, u32[]{:S(2)}, u32[]{:S(2)}) collective-permute-start(bf16[33,8,128]{2,1,0:T(8,128)(2,1)S(1)} %bitcast.9), channel_id=1, source_target_pairs={{0,3},{1,2},{2,1},{3,0},{4,7},{5,6},{6,5},{7,4},{8,11},{9,10},{10,... | collective-permute-start | bytes 202760 | tf_op jit(solution)/shard_map/ppermute | solution.py:293
  19.9 5.8 %collective-permute-start.1 = (bf16[33,8,128]{2,1,0:T(8,128)(2,1)S(1)}, bf16[33,8,128]{2,1,0:T(8,128)(2,1)S(1)}, u32[]{:S(2)}, u32[]{:S(2)}) collective-permute-start(bf16[33,8,128]{2,1,0:T(8,128)(2,1)S(1)} %bitcast.10), channel_id=1, source_target_pairs={{0,2},{1,3},{2,0},{3,1},{4,6},{5,7},{6,4},{7,5},{8,10},{9,11},{10,... | collective-permute-start | bytes 202760 | tf_op jit(solution)/shard_map/ppermute | solution.py:293
  19.9 5.8 %collective-permute-start.2 = (bf16[33,8,128]{2,1,0:T(8,128)(2,1)S(1)}, bf16[33,8,128]{2,1,0:T(8,128)(2,1)S(1)}, u32[]{:S(2)}, u32[]{:S(2)}) collective-permute-start(bf16[33,8,128]{2,1,0:T(8,128)(2,1)S(1)} %bitcast.11), channel_id=1, source_target_pairs={{0,1},{1,0},{2,3},{3,2},{4,5},{5,4},{6,7},{7,6},{8,9},{9,8},{10,11... | collective-permute-start | bytes 202760 | tf_op jit(solution)/shard_map/ppermute | solution.py:293
  25.8 6.2 %collective-permute-start.3 = (bf16[19,32,128]{2,1,0:T(8,128)(2,1)S(1)}, bf16[19,32,128]{2,1,0:T(8,128)(2,1)S(1)}, u32[]{:S(2)}, u32[]{:S(2)}) collective-permute-start(bf16[19,32,128]{2,1,0:T(8,128)(2,1)S(1)} %get-tuple-element.11), channel_id=1, source_target_pairs={{0,8},{4,12},{8,0},{12,4},{16,24},{20,28},{24,16},{28,20},{1,9},{5... | collective-permute-start | bytes 466952 | tf_op jit(solution)/shard_map/ppermute | solution.py:293
  27.4 8.8 %collective-permute-start.4 = (bf16[19,32,128]{2,1,0:T(8,128)(2,1)S(1)}, bf16[19,32,128]{2,1,0:T(8,128)(2,1)S(1)}, u32[]{:S(2)}, u32[]{:S(2)}) collective-permute-start(bf16[19,32,128]{2,1,0:T(8,128)(2,1)S(1)} %get-tuple-element.12), channel_id=1, source_target_pairs={{0,16},{4,20},{8,24},{12,28},{16,0},{20,4},{24,8},{28,12},{1,17},{... | collective-permute-start | bytes 466952 | tf_op jit(solution)/shard_map/ppermute | solution.py:293
  28.9 7.3 %collective-permute-start.5 = (bf16[19,32,128]{2,1,0:T(8,128)(2,1)S(1)}, bf16[19,32,128]{2,1,0:T(8,128)(2,1)S(1)}, u32[]{:S(2)}, u32[]{:S(2)}) collective-permute-start(bf16[19,32,128]{2,1,0:T(8,128)(2,1)S(1)} %get-tuple-element.10), channel_id=1, source_target_pairs={{0,24},{4,28},{8,16},{12,20},{16,8},{20,12},{24,0},{28,4},{1,25},{... | collective-permute-start | bytes 466952 | tf_op jit(solution)/shard_map/ppermute | solution.py:293
  29.4 7.5 %collective-permute-start.6 = (bf16[19,32,128]{2,1,0:T(8,128)(2,1)S(1)}, bf16[19,32,128]{2,1,0:T(8,128)(2,1)S(1)}, u32[]{:S(2)}, u32[]{:S(2)}) collective-permute-start(bf16[19,32,128]{2,1,0:T(8,128)(2,1)S(1)} %get-tuple-element.13.refs_0_), channel_id=1, source_target_pairs={{0,4},{4,0},{8,12},{12,8},{16,20},{20,16},{24,28},{28,24},{1,5},{5... | collective-permute-start | bytes 466952 | tf_op jit(solution)/shard_map/ppermute | solution.py:293
  32.1 4.8 %collective-permute-start.7 = (bf16[19,32,128]{2,1,0:T(8,128)(2,1)S(1)}, bf16[19,32,128]{2,1,0:T(8,128)(2,1)S(1)}, u32[]{:S(2)}, u32[]{:S(2)}) collective-permute-start(bf16[19,32,128]{2,1,0:T(8,128)(2,1)S(1)} %collective-permute-done.3.refs_1_), channel_id=1, source_target_pairs={{0,4},{4,0},{8,12},{12,8},{16,20},{20,16},{24,28},{28,24},{1,5},{5... | collective-permute-start | bytes 466952 | tf_op jit(solution)/shard_map/ppermute | solution.py:293
  36.2 1.4 %collective-permute-start.8 = (bf16[19,32,128]{2,1,0:T(8,128)(2,1)S(1)}, bf16[19,32,128]{2,1,0:T(8,128)(2,1)S(1)}, u32[]{:S(2)}, u32[]{:S(2)}) collective-permute-start(bf16[19,32,128]{2,1,0:T(8,128)(2,1)S(1)} %collective-permute-done.4.refs_2_), channel_id=1, source_target_pairs={{0,4},{4,0},{8,12},{12,8},{16,20},{20,16},{24,28},{28,24},{1,5},{5... | collective-permute-start | bytes 466952 | tf_op jit(solution)/shard_map/ppermute | solution.py:293
  36.2 1.6 %collective-permute-start.9 = (bf16[19,32,128]{2,1,0:T(8,128)(2,1)S(1)}, bf16[19,32,128]{2,1,0:T(8,128)(2,1)S(1)}, u32[]{:S(2)}, u32[]{:S(2)}) collective-permute-start(bf16[19,32,128]{2,1,0:T(8,128)(2,1)S(1)} %collective-permute-done.5.refs_3_), channel_id=1, source_target_pairs={{0,4},{4,0},{8,12},{12,8},{16,20},{20,16},{24,28},{28,24},{1,5},{5... | collective-permute-start | bytes 466952 | tf_op jit(solution)/shard_map/ppermute | solution.py:293

commit v2 on v1

--- a/solution.py
+++ b/solution.py
@@ -1,3 +1,36 @@
+import functools
+
+import jax
+import jax.numpy as jnp
+from jax import lax
+from jax.experimental import pallas as pl
+from jax.experimental.pallas import tpu as pltpu
+from jax.sharding import PartitionSpec as P
+
+PANEL = 128
+BOTH = 2 * PANEL
+LANES = 128
+SUB = 8
+STRIP = 64
+AHEAD = 1
+
+damp_coef = 0.25
+
+HIGHEST = lax.Precision.HIGHEST
+FIRSTS = (((0,), (0,)), ((), ()))
+LASTS = (((1,), (1,)), ((), ()))
+PLAIN = (((1,), (0,)), ((), ()))
+
+
+def mxu(left, right, dims=PLAIN):
+    return lax.dot_general(left, right, dims, preferred_element_type=jnp.float32)
+
+
+def halves(value):
+    high = value.astype(jnp.bfloat16)
+    return high, (value - high.astype(jnp.float32)).astype(jnp.bfloat16)
+
+
 import functools
 
 import jax
@@ -340,3 +373,249 @@
         out_specs=P("row", "col"),
         check_vma=False,
     )
+
+
+def eliminate(work_ref, done_ref):
+    tiles = BOTH // LANES
+    groups = STRIP // SUB
+    sub_at = lax.broadcasted_iota(jnp.int32, (SUB, LANES), 0)
+    lane_at = lax.broadcasted_iota(jnp.int32, (SUB, LANES), 1)
+    for start in range(0, BOTH, STRIP):
+        here = start // LANES
+        live = list(range(here, tiles)) + list(range(tiles, tiles + here + 1))
+        rows = [
+            {t: work_ref[start + g * SUB : start + (g + 1) * SUB, t * LANES : (t + 1) * LANES] for t in live}
+            for g in range(groups)
+        ]
+        roots = []
+
+        def spread(block, low, high):
+            lane = start % LANES + block * SUB
+            return [
+                {
+                    g: jnp.broadcast_to(rows[g][here][:, lane + m : lane + m + 1], (SUB, LANES))
+                    for g in range(low, high)
+                }
+                for m in range(SUB)
+            ]
+
+        cols = spread(0, 0, groups)
+        for block in range(groups):
+            near = min(block + 1 + AHEAD, groups)
+            ahead = spread(block + 1, block + 1, near) if block + 1 < groups else None
+            pivots = jnp.ones((SUB, LANES), jnp.float32)
+            inverses = []
+            for j in range(SUB):
+                lead = cols[j]
+                pivot = lead[block][j : j + 1, :]
+                inverse = 1.0 / pivot
+                inverses.append(inverse)
+                pivots = jnp.where(sub_at == j, pivot, pivots)
+                for m in range(j + 1, SUB):
+                    factor = lead[block][m : m + 1, :] * inverse
+                    for g in cols[m]:
+                        cols[m][g] = cols[m][g] - lead[g] * factor
+                if ahead is not None:
+                    for m in range(SUB):
+                        factor = lead[block + 1][m : m + 1, :] * inverse
+                        for g in ahead[m]:
+                            ahead[m][g] = ahead[m][g] - lead[g] * factor
+                scaled = {t: rows[block][t][j : j + 1, :] * inverse for t in live}
+                for g in range(block, groups):
+                    weight = lead[g]
+                    if g == block:
+                        if j == SUB - 1:
+                            continue
+                        weight = jnp.where(sub_at > j, weight, 0.0)
+                    for t in live:
+                        rows[g][t] = rows[g][t] - weight * scaled[t]
+            roots.append(lax.rsqrt(pivots))
+            if ahead is not None:
+                cols = ahead
+                for m, late in enumerate(spread(block + 1, near, groups)):
+                    cols[m].update(late)
+        for g in range(groups):
+            for t in range(2 * tiles):
+                at = slice(start + g * SUB, start + (g + 1) * SUB), slice(t * LANES, (t + 1) * LANES)
+                if t not in live:
+                    done_ref[at] = jnp.zeros((SUB, LANES), jnp.float32)
+                    continue
+                value = rows[g][t] * roots[g]
+                if t == here:
+                    value = jnp.where(lane_at + t * LANES >= sub_at + start + g * SUB, value, 0.0)
+                done_ref[at] = value
+        beyond = start + STRIP
+        if beyond < BOTH:
+            first = beyond // LANES * LANES
+            last = BOTH + -(-beyond // LANES) * LANES
+            right = done_ref[start:beyond, first:last]
+            cuts = [beyond, beyond + STRIP] + ([BOTH] if beyond + STRIP < BOTH else [])
+            for low, high in zip(cuts[:-1], cuts[1:]):
+                left = done_ref[start:beyond, low:high]
+                work_ref[low:high, first:last] -= lax.dot_general(
+                    left, right, FIRSTS, precision=HIGHEST, preferred_element_type=jnp.float32
+                )
+
+
+def fisher_kernel(
+    place_ref, level_ref, panel_level_ref, *refs, sources, row_blocks, col_blocks, total_ex, feats
+):
+    arrived = refs[:sources]
+    out_ref = refs[sources]
+    g_row, g_col, g_panel, work, done, lower, mix_high, mix_low, panel_mix, damp_ref = refs[sources + 1 :]
+    step = pl.program_id(0)
+    row_at, col_at = place_ref[0], place_ref[1]
+    panel_blocks = BOTH // LANES
+    here = arrived[0].shape[1]
+
+    @pl.when(step == 0)
+    def _():
+        row_base = lax.rem(row_at, 2) * row_blocks
+        col_base = 2 * row_blocks
+        panel_base = col_base + col_blocks
+        total = jnp.zeros((here, LANES), jnp.float32)
+        for n, piece in enumerate(arrived):
+            at = slice(n * here, (n + 1) * here)
+            for b in range(panel_blocks):
+                g_panel[at, b * LANES : (b + 1) * LANES] = piece[panel_base + b]
+            for b in range(row_blocks):
+                g_row[at, b * LANES : (b + 1) * LANES] = piece[row_base + b]
+            for b in range(col_blocks):
+                g_col[b // panel_blocks, at, b % panel_blocks * LANES : (b % panel_blocks + 1) * LANES] = piece[
+                    col_base + b
+                ]
+            total += piece[panel_base + panel_blocks].astype(jnp.float32)
+        total_sq = jnp.sum(jnp.sum(total, axis=0, keepdims=True), axis=1, keepdims=True)
+        damping = damp_coef * total_sq / (total_ex * feats)
+        damp_ref[...] = jnp.broadcast_to(damping, damp_ref.shape)
+        panel = g_panel[...]
+        rows_at = lax.broadcasted_iota(jnp.int32, (BOTH, BOTH), 0)
+        cols_at = lax.broadcasted_iota(jnp.int32, (BOTH, BOTH), 1)
+        same = rows_at == cols_at
+        work[:, :BOTH] = mxu(panel, panel, FIRSTS) * (1.0 / total_ex) + jnp.where(
+            same, damping * panel_level_ref[...], 0.0
+        )
+        work[:, BOTH:] = jnp.where(same, 1.0, 0.0)
+        eliminate(work, done)
+        lower[...] = done[:, :BOTH].T
+        w_high, w_low = halves(done[:, BOTH:])
+        mixed = mxu(panel, w_high, LASTS) + mxu(panel, w_low, LASTS)
+        y_high, y_low = halves(mixed)
+        cross = mxu(y_high, y_low, LASTS)
+        outer = mxu(y_high, y_high, LASTS) + cross + cross.T
+        ex_rows = lax.broadcasted_iota(jnp.int32, outer.shape, 0)
+        ex_cols = lax.broadcasted_iota(jnp.int32, outer.shape, 1)
+        mix = (jnp.where(ex_rows == ex_cols, 1.0, 0.0) - outer * (1.0 / total_ex)) * (1.0 / total_ex)
+        mix_high[...], mix_low[...] = halves(mix)
+        panel_mix[...] = mixed * (1.0 / total_ex)
+
+    in_panel = (col_at == 0) & (step == 0)
+    cols = g_col[step]
+    weights = mxu(mix_high[...], cols) + mxu(mix_low[...], cols)
+    weights = jnp.where(in_panel, panel_mix[...], weights)
+    high, low = halves(weights)
+    rows = g_row[...]
+    tile = mxu(rows, high, FIRSTS) + mxu(rows, low, FIRSTS)
+    row_span, width = tile.shape
+    col_first = (col_at * pl.num_programs(0) + step) * width
+    row_glob = row_at * row_span + lax.broadcasted_iota(jnp.int32, tile.shape, 0)
+    col_glob = col_first + lax.broadcasted_iota(jnp.int32, tile.shape, 1)
+    out_ref[...] = tile + jnp.where(row_glob == col_glob, damp_ref[0:1, 0:1] * level_ref[...], 0.0)
+
+    @pl.when(row_at == 0)
+    def _():
+        out_ref[:BOTH, :] = jnp.where(in_panel, lower[...], 0.0)
+
+
+def fisher(place, col_levels, panel_levels, arrived, row_blocks, col_blocks, total_ex, feats):
+    row_span, col_span = row_blocks * LANES, col_blocks * LANES
+    sources = len(arrived)
+    examples = sources * arrived[0].shape[1]
+    vmem = pl.BlockSpec(memory_space=pltpu.VMEM)
+    return pl.pallas_call(
+        functools.partial(
+            fisher_kernel,
+            sources=sources,
+            row_blocks=row_blocks,
+            col_blocks=col_blocks,
+            total_ex=total_ex,
+            feats=feats,
+        ),
+        grid=(col_span // BOTH,),
+        in_specs=[
+            pl.BlockSpec(memory_space=pltpu.SMEM),
+            pl.BlockSpec((1, BOTH), lambda n: (0, n)),
+            vmem,
+        ]
+        + [vmem] * sources,
+        out_specs=pl.BlockSpec((row_span, BOTH), lambda n: (0, n)),
+        out_shape=jax.ShapeDtypeStruct((row_span, col_span), jnp.float32),
+        scratch_shapes=[
+            pltpu.VMEM((examples, row_span), jnp.bfloat16),
+            pltpu.VMEM((col_span // BOTH, examples, BOTH), jnp.bfloat16),
+            pltpu.VMEM((examples, BOTH), jnp.bfloat16),
+            pltpu.VMEM((BOTH, 2 * BOTH), jnp.float32),
+            pltpu.VMEM((BOTH, 2 * BOTH), jnp.float32),
+            pltpu.VMEM((BOTH, BOTH), jnp.float32),
+            pltpu.VMEM((examples, examples), jnp.bfloat16),
+            pltpu.VMEM((examples, examples), jnp.bfloat16),
+            pltpu.VMEM((examples, BOTH), jnp.float32),
+            pltpu.VMEM((SUB, LANES), jnp.float32),
+        ],
+        compiler_params=pltpu.CompilerParams(vmem_limit_bytes=48 * 2**20),
+        name="fisher",
+    )(place, col_levels, panel_levels, *arrived)
+
+
+def swap(block, axis, mask):
+    size = lax.axis_size(axis)
+    return lax.ppermute(block, axis, [(n, n ^ mask) for n in range(size)])
+
+
+def shards(activations, out_grads, proj_in, proj_out, damp_level):
+    local_ex = activations.shape[0]
+    feats = proj_in.shape[1] * proj_out.shape[1]
+    n_rows = lax.axis_size("row")
+    n_cols = lax.axis_size("col")
+    total_ex = local_ex * n_rows * n_cols
+    row_at = lax.axis_index("row")
+    col_at = lax.axis_index("col")
+    blocks = feats // LANES
+    row_blocks = blocks // n_rows
+    col_blocks = blocks // n_cols
+
+    levels = damp_level.astype(jnp.float32).reshape(1, feats)
+    col_levels = lax.dynamic_slice_in_dim(levels, col_at * col_blocks * LANES, col_blocks * LANES, axis=1)
+    place = jnp.stack([row_at, col_at]).astype(jnp.int32)
+
+    packed = project(activations, out_grads, proj_in, proj_out)
+    along = [packed] + [swap(packed, "col", mask) for mask in range(n_cols - 1, 0, -1)]
+    line = jnp.concatenate(along, axis=1)
+
+    common = [
+        lax.dynamic_slice_in_dim(line, col_at * col_blocks, col_blocks),
+        line[: BOTH // LANES],
+        line[blocks:],
+    ]
+    pair_at = row_at // 2
+
+    def bundle(pair):
+        wanted = lax.dynamic_slice_in_dim(line, pair * 2 * row_blocks, 2 * row_blocks)
+        return jnp.concatenate([wanted] + common)
+
+    own = bundle(pair_at)
+    got = [own] + [swap(bundle(pair_at ^ mask), "row", 2 * mask) for mask in range(1, n_rows // 2)]
+    arrived = got + [swap(piece, "row", 1) for piece in got]
+    return fisher(
+        place, col_levels, levels[:, :BOTH], arrived, row_blocks, col_blocks, total_ex, feats
+    )
+
+
+def solution(mesh):
+    return jax.shard_map(
+        shards,
+        mesh=mesh,
+        in_specs=(P(("row", "col"), None, None), P(("row", "col"), None, None), P(), P(), P()),
+        out_specs=P("row", "col"),
+        check_vma=False,
+    )

time: 54.7 us -> 48.9 us (0.89)
  Pallas kernels: 21.6 us -> 15.8 us
    pallas_call x1, Pallas kernels: 16.7 us -> 10.9 us  [fisher(): pl.pallas_call(functools.partial(fisher_kernel, sources=sources, row_bloc...]
where the time goes in v2:
time: 48.9 us; the launch traced here: 48.7 us
  Pallas kernels  15.8 us (32%)
  waiting for transfers between devices  12.9 us (26%)
  local copies, waits for them, and re-layouts  9.89 us (20%)
  starting transfers between devices  9.81 us (20%)
    ppermute x10, waiting for transfers between devices, swap(): return lax.ppermute(block, axis, [(n, n ^ mask) for n in range(size)])  12.9 us
    pallas_call x1, Pallas kernels, fisher(): pl.pallas_call(functools.partial(fisher_kernel, sources=sources, row_bloc...  10.9 us
    unnamed x12, local copies, waits for them, and re-layouts  9.85 us
    ppermute x10, starting transfers between devices, swap(): return lax.ppermute(block, axis, [(n, n ^ mask) for n in range(size)])  9.81 us
    pallas_call x1, Pallas kernels, project(): pl.pallas_call(functools.partial(project_kernel, local_ex=local_ex, tok_l...  4.89 us
  transfers between devices with their start and end apart: 10, of which 6 were waited for; matrix products, arithmetic and copies ran while one was open for 0% of the time, Pallas kernels for 0%

profile of v2, /device:TPU:0, one launch (start us, length us, event | category | flops | bytes accessed | tf_op | source)
XLA Modules:
  0.0 48.7 jit_solution(8583725899223866072)
XLA Ops:
  0.0 0.0 copy-start.3
  0.0 2.1 %copy.6.in_ref = bf16[8192,64]{1,0:T(8,128)(2,1)S(1)} copy(bf16[8192,64]{0,1:T(8,128)(2,1)} %param.7) | data formatting | bytes 2097152 | tf_op args[2]
  2.1 0.0 copy-done.3
  2.1 1.8 %copy.7.proj_ref = bf16[8192,64]{1,0:T(8,128)(2,1)} copy(bf16[8192,64]{0,1:T(8,128)(2,1)S(1)} %copy-done.3) | data formatting | bytes 2097152 | tf_op args[3]
  3.9 1.6 %copy-done = bf16[8192,64]{1,0:T(8,128)(2,1)S(1)} copy-done((bf16[8192,64]{1,0:T(8,128)(2,1)S(1)}, bf16[8192,64]{1,0:T(8,128)(2,1)}, u32[]{:S(2)}) %copy-start) | copy-done | bytes 1048600
  5.5 2.2 %copy-done.1 = bf16[8,32,8192]{2,1,0:T(8,128)(2,1)S(1)} copy-done((bf16[8,32,8192]{2,1,0:T(8,128)(2,1)S(1)}, bf16[8,32,8192]{2,1,0:T(8,128)(2,1)}, u32[]{:S(2)}) %copy-start.1) | copy-done | bytes 4194328
  7.7 2.2 %copy-done.2 = bf16[8,32,8192]{2,1,0:T(8,128)(2,1)S(1)} copy-done((bf16[8,32,8192]{2,1,0:T(8,128)(2,1)S(1)}, bf16[8,32,8192]{2,1,0:T(8,128)(2,1)}, u32[]{:S(2)}) %copy-start.2) | copy-done | bytes 4194328
  9.9 4.9 %project.1 = bf16[264,128]{1,0:T(8,128)(2,1)S(1)} custom-call(bf16[256,8192]{1,0:T(8,128)(2,1)S(1)} %bitcast.7, bf16[256,8192]{1,0:T(8,128)(2,1)S(1)} %bitcast.8, bf16[8192,64]{1,0:T(8,128)(2,1)S(1)} %copy.6.in_ref, bf16[8192,64]{1,0:T(8,128)(2,1)S(1)} %copy-done), custom_call_target="tpu_custom_call" | custom-call | tf_op jit(solution)/shard_map/project/pallas_call | solution.py:119
  14.8 5.1 %collective-permute-start = (bf16[33,8,128]{2,1,0:T(8,128)(2,1)S(1)}, bf16[33,8,128]{2,1,0:T(8,128)(2,1)S(1)}, u32[]{:S(2)}, u32[]{:S(2)}) collective-permute-start(bf16[33,8,128]{2,1,0:T(8,128)(2,1)S(1)} %bitcast.9), channel_id=1, source_target_pairs={{0,3},{1,2},{2,1},{3,0},{4,7},{5,6},{6,5},{7,4},{8,11},{9,10},{10,... | collective-permute-start | bytes 202760 | tf_op jit(solution)/shard_map/ppermute | solution.py:572
  19.9 0.0 collective-permute-start.1
  19.9 0.6 %collective-permute-start.2 = (bf16[33,8,128]{2,1,0:T(8,128)(2,1)S(1)}, bf16[33,8,128]{2,1,0:T(8,128)(2,1)S(1)}, u32[]{:S(2)}, u32[]{:S(2)}) collective-permute-start(bf16[33,8,128]{2,1,0:T(8,128)(2,1)S(1)} %bitcast.11), channel_id=1, source_target_pairs={{0,1},{1,0},{2,3},{3,2},{4,5},{5,4},{6,7},{7,6},{8,9},{9,8},{10,11... | collective-permute-start | bytes 202760 | tf_op jit(solution)/shard_map/ppermute | solution.py:572
  20.5 2.0 %collective-permute-done = bf16[33,8,128]{2,1,0:T(8,128)(2,1)S(1)} collective-permute-done((bf16[33,8,128]{2,1,0:T(8,128)(2,1)S(1)}, bf16[33,8,128]{2,1,0:T(8,128)(2,1)S(1)}, u32[]{:S(2)}, u32[]{:S(2)}) %collective-permute-start) | collective-permute-done | bytes 67616 | tf_op jit(solution)/shard_map/ppermute | solution.py:572
  22.5 3.1 %collective-permute-done.1 = bf16[33,8,128]{2,1,0:T(8,128)(2,1)S(1)} collective-permute-done((bf16[33,8,128]{2,1,0:T(8,128)(2,1)S(1)}, bf16[33,8,128]{2,1,0:T(8,128)(2,1)S(1)}, u32[]{:S(2)}, u32[]{:S(2)}) %collective-permute-start.1) | collective-permute-done | bytes 67616 | tf_op jit(solution)/shard_map/ppermute | solution.py:572
  25.6 0.0 collective-permute-done.2
  25.7 0.1 pad_maximum_fusion
  25.8 1.6 %collective-permute-start.3 = (bf16[19,32,128]{2,1,0:T(8,128)(2,1)S(1)}, bf16[19,32,128]{2,1,0:T(8,128)(2,1)S(1)}, u32[]{:S(2)}, u32[]{:S(2)}) collective-permute-start(bf16[19,32,128]{2,1,0:T(8,128)(2,1)S(1)} %get-tuple-element.11), channel_id=1, source_target_pairs={{0,8},{4,12},{8,0},{12,4},{16,24},{20,28},{24,16},{28,20},{1,9},{5... | collective-permute-start | bytes 466952 | tf_op jit(solution)/shard_map/ppermute | solution.py:572
  27.4 1.5 %collective-permute-start.4 = (bf16[19,32,128]{2,1,0:T(8,128)(2,1)S(1)}, bf16[19,32,128]{2,1,0:T(8,128)(2,1)S(1)}, u32[]{:S(2)}, u32[]{:S(2)}) collective-permute-start(bf16[19,32,128]{2,1,0:T(8,128)(2,1)S(1)} %get-tuple-element.12), channel_id=1, source_target_pairs={{0,16},{4,20},{8,24},{12,28},{16,0},{20,4},{24,8},{28,12},{1,17},{... | collective-permute-start | bytes 466952 | tf_op jit(solution)/shard_map/ppermute | solution.py:572
  28.9 0.5 collective-permute-start.5
  29.4 0.0 collective-permute-start.6
  29.4 2.7 %collective-permute-done.3.refs_1_ = bf16[19,32,128]{2,1,0:T(8,128)(2,1)S(1)} collective-permute-done((bf16[19,32,128]{2,1,0:T(8,128)(2,1)S(1)}, bf16[19,32,128]{2,1,0:T(8,128)(2,1)S(1)}, u32[]{:S(2)}, u32[]{:S(2)}) %collective-permute-start.3) | collective-permute-done | bytes 155680 | tf_op jit(solution)/shard_map/ppermute | solution.py:572
  32.1 0.0 collective-permute-start.7
  32.1 4.1 %collective-permute-done.4.refs_2_ = bf16[19,32,128]{2,1,0:T(8,128)(2,1)S(1)} collective-permute-done((bf16[19,32,128]{2,1,0:T(8,128)(2,1)S(1)}, bf16[19,32,128]{2,1,0:T(8,128)(2,1)S(1)}, u32[]{:S(2)}, u32[]{:S(2)}) %collective-permute-start.4) | collective-permute-done | bytes 155680 | tf_op jit(solution)/shard_map/ppermute | solution.py:572
  36.2 0.0 collective-permute-start.8
  36.2 0.0 collective-permute-done.5.refs_3_
  36.2 0.5 %collective-permute-start.9 = (bf16[19,32,128]{2,1,0:T(8,128)(2,1)S(1)}, bf16[19,32,128]{2,1,0:T(8,128)(2,1)S(1)}, u32[]{:S(2)}, u32[]{:S(2)}) collective-permute-start(bf16[19,32,128]{2,1,0:T(8,128)(2,1)S(1)} %collective-permute-done.5.refs_3_), channel_id=1, source_target_pairs={{0,4},{4,0},{8,12},{12,8},{16,20},{20,16},{24,28},{28,24},{1,5},{5... | collective-permute-start | bytes 466952 | tf_op jit(solution)/shard_map/ppermute | solution.py:572
  36.7 0.0 copy-done.4
  36.7 0.1 pad_add_fusion.place_ref
  36.8 0.0 collective-permute-done.6.refs_4_
  36.8 0.0 collective-permute-done.7.refs_5_
  36.8 0.8 %collective-permute-done.8.refs_6_ = bf16[19,32,128]{2,1,0:T(8,128)(2,1)S(1)} collective-permute-done((bf16[19,32,128]{2,1,0:T(8,128)(2,1)S(1)}, bf16[19,32,128]{2,1,0:T(8,128)(2,1)S(1)}, u32[]{:S(2)}, u32[]{:S(2)}) %collective-permute-start.8) | collective-permute-done | bytes 155680 | tf_op jit(solution)/shard_map/ppermute | solution.py:572
  37.6 0.2 collective-permute-done.9.refs_7_
  37.8 10.9 %fisher.1 = f32[512,1024]{1,0:T(8,128)} custom-call(s32[2]{0:T(128)S(1)} %pad_add_fusion.place_ref, f32[1,1024]{1,0:T(1,128)S(1)} %bitcast.13, f32[1,256]{1,0:T(1,128)S(1)} %slice.12.panel_level_ref, bf16[19,32,128]{2,1,0:T(8,128)(2,1)S(1)} %get-tuple-element.13.refs_0_, bf16[19,32,128]{2,1,0:T(8,128)(2,1)S(1)} %collective-permute-done.3.refs_1_, ...), custom_call_target="tpu_custom_call" | custom-call | tf_op jit(solution)/shard_map/fisher/pallas_call | solution.py:535
  (11 shorter events, 0.1 us)
Async XLA Ops:
  0.0 2.1 %copy-start.3 = (bf16[8192,64]{0,1:T(8,128)(2,1)S(1)}, bf16[8192,64]{0,1:T(8,128)(2,1)}, u32[]{:S(2)}) copy-start(bf16[8192,64]{0,1:T(8,128)(2,1)} %param.8) | copy-start | bytes 3145732
  3.9 1.6 %copy-start = (bf16[8192,64]{1,0:T(8,128)(2,1)S(1)}, bf16[8192,64]{1,0:T(8,128)(2,1)}, u32[]{:S(2)}) copy-start(bf16[8192,64]{1,0:T(8,128)(2,1)} %copy.7.proj_ref) | copy-start | bytes 3145732
  5.5 2.2 %copy-start.1 = (bf16[8,32,8192]{2,1,0:T(8,128)(2,1)S(1)}, bf16[8,32,8192]{2,1,0:T(8,128)(2,1)}, u32[]{:S(2)}) copy-start(bf16[8,32,8192]{2,1,0:T(8,128)(2,1)} %param.5) | copy-start | bytes 12582916
  7.7 2.2 %copy-start.2 = (bf16[8,32,8192]{2,1,0:T(8,128)(2,1)S(1)}, bf16[8,32,8192]{2,1,0:T(8,128)(2,1)}, u32[]{:S(2)}) copy-start(bf16[8,32,8192]{2,1,0:T(8,128)(2,1)} %param.6) | copy-start | bytes 12582916
  14.8 22.0 %copy-start.4 = (s32[4096]{0:T(1024)S(1)}, s32[4096]{0:T(1024)}, u32[]{:S(2)}) copy-start(s32[4096]{0:T(1024)} %param.9) | copy-start | bytes 49156
  14.8 7.7 %collective-permute-start = (bf16[33,8,128]{2,1,0:T(8,128)(2,1)S(1)}, bf16[33,8,128]{2,1,0:T(8,128)(2,1)S(1)}, u32[]{:S(2)}, u32[]{:S(2)}) collective-permute-start(bf16[33,8,128]{2,1,0:T(8,128)(2,1)S(1)} %bitcast.9), channel_id=1, source_target_pairs={{0,3},{1,2},{2,1},{3,0},{4,7},{5,6},{6,5},{7,4},{8,11},{9,10},{10,... | collective-permute-start | bytes 202760 | tf_op jit(solution)/shard_map/ppermute | solution.py:572
  19.9 5.8 %collective-permute-start.1 = (bf16[33,8,128]{2,1,0:T(8,128)(2,1)S(1)}, bf16[33,8,128]{2,1,0:T(8,128)(2,1)S(1)}, u32[]{:S(2)}, u32[]{:S(2)}) collective-permute-start(bf16[33,8,128]{2,1,0:T(8,128)(2,1)S(1)} %bitcast.10), channel_id=1, source_target_pairs={{0,2},{1,3},{2,0},{3,1},{4,6},{5,7},{6,4},{7,5},{8,10},{9,11},{10,... | collective-permute-start | bytes 202760 | tf_op jit(solution)/shard_map/ppermute | solution.py:572
  19.9 5.8 %collective-permute-start.2 = (bf16[33,8,128]{2,1,0:T(8,128)(2,1)S(1)}, bf16[33,8,128]{2,1,0:T(8,128)(2,1)S(1)}, u32[]{:S(2)}, u32[]{:S(2)}) collective-permute-start(bf16[33,8,128]{2,1,0:T(8,128)(2,1)S(1)} %bitcast.11), channel_id=1, source_target_pairs={{0,1},{1,0},{2,3},{3,2},{4,5},{5,4},{6,7},{7,6},{8,9},{9,8},{10,11... | collective-permute-start | bytes 202760 | tf_op jit(solution)/shard_map/ppermute | solution.py:572
  25.8 6.2 %collective-permute-start.3 = (bf16[19,32,128]{2,1,0:T(8,128)(2,1)S(1)}, bf16[19,32,128]{2,1,0:T(8,128)(2,1)S(1)}, u32[]{:S(2)}, u32[]{:S(2)}) collective-permute-start(bf16[19,32,128]{2,1,0:T(8,128)(2,1)S(1)} %get-tuple-element.11), channel_id=1, source_target_pairs={{0,8},{4,12},{8,0},{12,4},{16,24},{20,28},{24,16},{28,20},{1,9},{5... | collective-permute-start | bytes 466952 | tf_op jit(solution)/shard_map/ppermute | solution.py:572
  27.4 8.8 %collective-permute-start.4 = (bf16[19,32,128]{2,1,0:T(8,128)(2,1)S(1)}, bf16[19,32,128]{2,1,0:T(8,128)(2,1)S(1)}, u32[]{:S(2)}, u32[]{:S(2)}) collective-permute-start(bf16[19,32,128]{2,1,0:T(8,128)(2,1)S(1)} %get-tuple-element.12), channel_id=1, source_target_pairs={{0,16},{4,20},{8,24},{12,28},{16,0},{20,4},{24,8},{28,12},{1,17},{... | collective-permute-start | bytes 466952 | tf_op jit(solution)/shard_map/ppermute | solution.py:572
  28.9 7.3 %collective-permute-start.5 = (bf16[19,32,128]{2,1,0:T(8,128)(2,1)S(1)}, bf16[19,32,128]{2,1,0:T(8,128)(2,1)S(1)}, u32[]{:S(2)}, u32[]{:S(2)}) collective-permute-start(bf16[19,32,128]{2,1,0:T(8,128)(2,1)S(1)} %get-tuple-element.10), channel_id=1, source_target_pairs={{0,24},{4,28},{8,16},{12,20},{16,8},{20,12},{24,0},{28,4},{1,25},{... | collective-permute-start | bytes 466952 | tf_op jit(solution)/shard_map/ppermute | solution.py:572
  29.4 7.5 %collective-permute-start.6 = (bf16[19,32,128]{2,1,0:T(8,128)(2,1)S(1)}, bf16[19,32,128]{2,1,0:T(8,128)(2,1)S(1)}, u32[]{:S(2)}, u32[]{:S(2)}) collective-permute-start(bf16[19,32,128]{2,1,0:T(8,128)(2,1)S(1)} %get-tuple-element.13.refs_0_), channel_id=1, source_target_pairs={{0,4},{4,0},{8,12},{12,8},{16,20},{20,16},{24,28},{28,24},{1,5},{5... | collective-permute-start | bytes 466952 | tf_op jit(solution)/shard_map/ppermute | solution.py:572
  32.1 4.8 %collective-permute-start.7 = (bf16[19,32,128]{2,1,0:T(8,128)(2,1)S(1)}, bf16[19,32,128]{2,1,0:T(8,128)(2,1)S(1)}, u32[]{:S(2)}, u32[]{:S(2)}) collective-permute-start(bf16[19,32,128]{2,1,0:T(8,128)(2,1)S(1)} %collective-permute-done.3.refs_1_), channel_id=1, source_target_pairs={{0,4},{4,0},{8,12},{12,8},{16,20},{20,16},{24,28},{28,24},{1,5},{5... | collective-permute-start | bytes 466952 | tf_op jit(solution)/shard_map/ppermute | solution.py:572
  36.2 1.4 %collective-permute-start.8 = (bf16[19,32,128]{2,1,0:T(8,128)(2,1)S(1)}, bf16[19,32,128]{2,1,0:T(8,128)(2,1)S(1)}, u32[]{:S(2)}, u32[]{:S(2)}) collective-permute-start(bf16[19,32,128]{2,1,0:T(8,128)(2,1)S(1)} %collective-permute-done.4.refs_2_), channel_id=1, source_target_pairs={{0,4},{4,0},{8,12},{12,8},{16,20},{20,16},{24,28},{28,24},{1,5},{5... | collective-permute-start | bytes 466952 | tf_op jit(solution)/shard_map/ppermute | solution.py:572
  36.2 1.6 %collective-permute-start.9 = (bf16[19,32,128]{2,1,0:T(8,128)(2,1)S(1)}, bf16[19,32,128]{2,1,0:T(8,128)(2,1)S(1)}, u32[]{:S(2)}, u32[]{:S(2)}) collective-permute-start(bf16[19,32,128]{2,1,0:T(8,128)(2,1)S(1)} %collective-permute-done.5.refs_3_), channel_id=1, source_target_pairs={{0,4},{4,0},{8,12},{12,8},{16,20},{20,16},{24,28},{28,24},{1,5},{5... | collective-permute-start | bytes 466952 | tf_op jit(solution)/shard_map/ppermute | solution.py:572

commit v3 on v1

--- a/solution.py
+++ b/solution.py
@@ -12,6 +12,7 @@
 LANES = 128
 SUB = 8
 STRIP = 64
+AHEAD = 1
 
 damp_coef = 0.25
 
@@ -30,51 +31,46 @@
     return high, (value - high.astype(jnp.float32)).astype(jnp.bfloat16)
 
 
-def project_kernel(act_ref, out_ref, in_ref, proj_ref, packed_ref, a_acc, g_acc, *, local_ex, tok_len):
-    step = pl.program_id(0)
-
-    @pl.when(step == 0)
-    def _():
-        a_acc[...] = jnp.zeros_like(a_acc)
-        g_acc[...] = jnp.zeros_like(g_acc)
-
-    a_acc[...] += mxu(act_ref[...], in_ref[...])
-    g_acc[...] += mxu(out_ref[...], proj_ref[...])
-
-    @pl.when(step == pl.num_programs(0) - 1)
-    def _():
-        a_proj = a_acc[...]
-        tokens, rank_dim = a_proj.shape
-        pairs = rank_dim * rank_dim // LANES
-        g_turned = g_acc[...].T
-        example = lax.broadcasted_iota(jnp.int32, (local_ex, tokens), 0)
-        owner = lax.broadcasted_iota(jnp.int32, (local_ex, tokens), 1) // tok_len
-        own = jnp.where(example == owner, tok_len ** (-0.5), 0.0).astype(jnp.float32)
-        per_pair = LANES // rank_dim
-        parts = []
-        for part in range(per_pair):
-            spread = jnp.concatenate(
-                [
-                    g_turned[pair * per_pair + part : pair * per_pair + part + 1, :] * own
-                    for pair in range(pairs)
-                ],
-                axis=0,
-            )
-            parts.append(jnp.dot(spread, a_proj, precision=HIGHEST))
-        grads = jnp.concatenate(parts, axis=1).astype(jnp.bfloat16)
-        wide = grads.astype(jnp.float32)
-        square = jnp.sum(jnp.sum(wide * wide, axis=0, keepdims=True), axis=1, keepdims=True)
-        rows = pairs * local_ex
-        packed_ref[:rows, :] = grads
-        row_at = lax.broadcasted_iota(jnp.int32, (local_ex, LANES), 0)
-        lane_at = lax.broadcasted_iota(jnp.int32, (local_ex, LANES), 1)
-        first = square.astype(jnp.bfloat16).astype(jnp.float32)
-        second = (square - first).astype(jnp.bfloat16).astype(jnp.float32)
-        third = square - first - second
-        coded = jnp.where(
-            lane_at == 0, first, jnp.where(lane_at == 1, second, jnp.where(lane_at == 2, third, 0.0))
-        )
-        packed_ref[rows:, :] = jnp.where(row_at == 0, coded, 0.0).astype(jnp.bfloat16)
+def project_kernel(
+    act_hbm, out_hbm, in_hbm, proj_hbm, packed_ref, act_buf, out_buf, in_buf, proj_buf, sems, *, local_ex, tok_len
+):
+    tokens, rank_dim = act_buf.shape[0], in_buf.shape[0]
+    pieces = (in_hbm, in_buf), (act_hbm, act_buf), (proj_hbm, proj_buf), (out_hbm, out_buf)
+    copies = [pltpu.make_async_copy(whole, buf, sems.at[n]) for n, (whole, buf) in enumerate(pieces)]
+    for copy in copies:
+        copy.start()
+    for copy in copies:
+        copy.wait()
+    a_proj = mxu(act_buf[...], in_buf[...], LASTS)
+    g_turned = mxu(out_buf[...], proj_buf[...], LASTS).T
+    pairs = rank_dim * rank_dim // LANES
+    example = lax.broadcasted_iota(jnp.int32, (local_ex, tokens), 0)
+    owner = lax.broadcasted_iota(jnp.int32, (local_ex, tokens), 1) // tok_len
+    own = jnp.where(example == owner, 1.0, 0.0).astype(jnp.float32)
+    per_pair = LANES // rank_dim
+    a_high, a_low = halves(a_proj)
+    both = jnp.concatenate([a_high, a_low], axis=1)
+    g_high, g_low = [half.astype(jnp.float32) for half in halves(g_turned * tok_len ** (-0.5))]
+
+    def spread(source, part):
+        picks = [source[n * per_pair + part : n * per_pair + part + 1, :] * own for n in range(pairs)]
+        return jnp.concatenate(picks, axis=0).astype(jnp.bfloat16)
+
+    parts = []
+    for part in range(per_pair):
+        wide = mxu(spread(g_high, part), both)
+        parts.append(wide[:, :rank_dim] + wide[:, rank_dim:] + mxu(spread(g_low, part), a_high))
+    grads = jnp.concatenate(parts, axis=1).astype(jnp.bfloat16)
+    wide = grads.astype(jnp.float32)
+    square = jnp.sum(wide * wide, axis=0, keepdims=True)
+    rows = pairs * local_ex
+    packed_ref[:rows, :] = grads
+    row_at = lax.broadcasted_iota(jnp.int32, (local_ex, LANES), 0)
+    first = square.astype(jnp.bfloat16).astype(jnp.float32)
+    second = (square - first).astype(jnp.bfloat16).astype(jnp.float32)
+    third = square - first - second
+    coded = jnp.where(row_at == 0, first, jnp.where(row_at == 1, second, jnp.where(row_at == 2, third, 0.0)))
+    packed_ref[rows:, :] = coded.astype(jnp.bfloat16)
 
 
 def project(activations, out_grads, proj_in, proj_out):
@@ -82,86 +78,96 @@
     rank_dim = proj_in.shape[1]
     tokens = local_ex * tok_len
     pairs = rank_dim * rank_dim // LANES
-    chunk = 1024
+    hbm = pl.BlockSpec(memory_space=pltpu.HBM)
     packed = pl.pallas_call(
         functools.partial(project_kernel, local_ex=local_ex, tok_len=tok_len),
-        grid=(model_dim // chunk,),
-        in_specs=[
-            pl.BlockSpec((tokens, chunk), lambda d: (0, d)),
-            pl.BlockSpec((tokens, chunk), lambda d: (0, d)),
-            pl.BlockSpec((chunk, rank_dim), lambda d: (d, 0)),
-            pl.BlockSpec((chunk, rank_dim), lambda d: (d, 0)),
-        ],
-        out_specs=pl.BlockSpec(((pairs + 1) * local_ex, LANES), lambda d: (0, 0)),
+        in_specs=[hbm] * 4,
+        out_specs=pl.BlockSpec(memory_space=pltpu.VMEM),
         out_shape=jax.ShapeDtypeStruct(((pairs + 1) * local_ex, LANES), jnp.bfloat16),
         scratch_shapes=[
-            pltpu.VMEM((tokens, rank_dim), jnp.float32),
-            pltpu.VMEM((tokens, rank_dim), jnp.float32),
+            pltpu.VMEM((tokens, model_dim), jnp.bfloat16),
+            pltpu.VMEM((tokens, model_dim), jnp.bfloat16),
+            pltpu.VMEM((rank_dim, model_dim), jnp.bfloat16),
+            pltpu.VMEM((rank_dim, model_dim), jnp.bfloat16),
+            pltpu.SemaphoreType.DMA((4,)),
         ],
         compiler_params=pltpu.CompilerParams(vmem_limit_bytes=32 * 2**20),
         name="project",
     )(
         activations.reshape(tokens, model_dim),
         out_grads.reshape(tokens, model_dim),
-        proj_in,
-        proj_out,
+        proj_in.T,
+        proj_out.T,
     )
     return packed.reshape(pairs + 1, local_ex, LANES)
 
 
 def eliminate(work_ref, done_ref):
     tiles = BOTH // LANES
+    groups = STRIP // SUB
     sub_at = lax.broadcasted_iota(jnp.int32, (SUB, LANES), 0)
     lane_at = lax.broadcasted_iota(jnp.int32, (SUB, LANES), 1)
     for start in range(0, BOTH, STRIP):
         here = start // LANES
         live = list(range(here, tiles)) + list(range(tiles, tiles + here + 1))
-        groups = STRIP // SUB
         rows = [
             {t: work_ref[start + g * SUB : start + (g + 1) * SUB, t * LANES : (t + 1) * LANES] for t in live}
             for g in range(groups)
         ]
-        pivots = [jnp.ones((SUB, LANES), jnp.float32) for _ in range(groups)]
-
-        def column(index):
-            lane = (start + index) % LANES
+        roots = []
+
+        def spread(block, low, high):
+            lane = start % LANES + block * SUB
             return [
-                jnp.broadcast_to(rows[g][here][:, lane : lane + 1], (SUB, LANES)) if g >= index // SUB else None
-                for g in range(groups)
+                {
+                    g: jnp.broadcast_to(rows[g][here][:, lane + m : lane + m + 1], (SUB, LANES))
+                    for g in range(low, high)
+                }
+                for m in range(SUB)
             ]
 
-        now = column(0)
-        for index in range(STRIP):
-            g_now, s_now = divmod(index, SUB)
-            pivot = now[g_now][s_now : s_now + 1, :]
-            inverse = 1.0 / pivot
-            pivots[g_now] = jnp.where(sub_at == s_now, pivot, pivots[g_now])
-            later = None
-            if index + 1 < STRIP:
-                g_next, s_next = divmod(index + 1, SUB)
-                raw = column(index + 1)
-                factor = now[g_next][s_next : s_next + 1, :] * inverse
-                later = [
-                    raw[g] - now[g] * factor if g >= g_next else None for g in range(groups)
-                ]
-            scaled = {t: rows[g_now][t][s_now : s_now + 1, :] * inverse for t in live}
-            for g in range(g_now, groups):
-                weight = now[g]
-                if g == g_now:
-                    if s_now == SUB - 1:
-                        continue
-                    weight = jnp.where(sub_at > s_now, weight, 0.0)
-                for t in live:
-                    rows[g][t] = rows[g][t] - weight * scaled[t]
-            now = later
+        cols = spread(0, 0, groups)
+        for block in range(groups):
+            near = min(block + 1 + AHEAD, groups)
+            ahead = spread(block + 1, block + 1, near) if block + 1 < groups else None
+            pivots = jnp.ones((SUB, LANES), jnp.float32)
+            inverses = []
+            for j in range(SUB):
+                lead = cols[j]
+                pivot = lead[block][j : j + 1, :]
+                inverse = 1.0 / pivot
+                inverses.append(inverse)
+                pivots = jnp.where(sub_at == j, pivot, pivots)
+                for m in range(j + 1, SUB):
+                    factor = lead[block][m : m + 1, :] * inverse
+                    for g in cols[m]:
+                        cols[m][g] = cols[m][g] - lead[g] * factor
+                if ahead is not None:
+                    for m in range(SUB):
+                        factor = lead[block + 1][m : m + 1, :] * inverse
+                        for g in ahead[m]:
+                            ahead[m][g] = ahead[m][g] - lead[g] * factor
+                scaled = {t: rows[block][t][j : j + 1, :] * inverse for t in live}
+                for g in range(block, groups):
+                    weight = lead[g]
+                    if g == block:
+                        if j == SUB - 1:
+                            continue
+                        weight = jnp.where(sub_at > j, weight, 0.0)
+                    for t in live:
+                        rows[g][t] = rows[g][t] - weight * scaled[t]
+            roots.append(lax.rsqrt(pivots))
+            if ahead is not None:
+                cols = ahead
+                for m, late in enumerate(spread(block + 1, near, groups)):
+                    cols[m].update(late)
         for g in range(groups):
-            root = lax.rsqrt(pivots[g])
             for t in range(2 * tiles):
                 at = slice(start + g * SUB, start + (g + 1) * SUB), slice(t * LANES, (t + 1) * LANES)
                 if t not in live:
                     done_ref[at] = jnp.zeros((SUB, LANES), jnp.float32)
                     continue
-                value = rows[g][t] * root
+                value = rows[g][t] * roots[g]
                 if t == here:
                     value = jnp.where(lane_at + t * LANES >= sub_at + start + g * SUB, value, 0.0)
                 done_ref[at] = value

time: 54.7 us -> 43.6 us (0.80)
  Pallas kernels: 21.6 us -> 14.4 us
  local copies, waits for them, and re-layouts: 9.89 us -> 6.88 us
  waiting for transfers between devices: 12.9 us -> 12 us
    pallas_call x1, Pallas kernels: 16.7 us -> 10.9 us  [fisher(): pl.pallas_call(functools.partial(fisher_kernel, sources=sources, row_bloc...]
    unnamed x12 -> x10, local copies, waits for them, and re-layouts: 9.85 us -> 6.83 us
    pallas_call x1, Pallas kernels: 4.89 us -> 3.57 us  [project(): pl.pallas_call(functools.partial(project_kernel, local_ex=local_ex, tok_l...]
    ppermute x10, waiting for transfers between devices: 12.9 us -> 12 us  [swap(): return lax.ppermute(block, axis, [(n, n ^ mask) for n in range(size)])]
where the time goes in v3:
time: 43.6 us; the launch traced here: 43.4 us
  Pallas kernels  14.4 us (33%)
  waiting for transfers between devices  12 us (28%)
  starting transfers between devices  9.76 us (22%)
  local copies, waits for them, and re-layouts  6.88 us (16%)
    ppermute x10, waiting for transfers between devices, swap(): return lax.ppermute(block, axis, [(n, n ^ mask) for n in range(size)])  12 us
    pallas_call x1, Pallas kernels, fisher(): pl.pallas_call(functools.partial(fisher_kernel, sources=sources, row_bloc...  10.9 us
    ppermute x10, starting transfers between devices, swap(): return lax.ppermute(block, axis, [(n, n ^ mask) for n in range(size)])  9.76 us
    unnamed x10, local copies, waits for them, and re-layouts  6.83 us
    pallas_call x1, Pallas kernels, project(): pl.pallas_call(functools.partial(project_kernel, local_ex=local_ex, tok_l...  3.57 us
  transfers between devices with their start and end apart: 10, of which 6 were waited for; matrix products, arithmetic and copies ran while one was open for 0% of the time, Pallas kernels for 0%

profile of v3, /device:TPU:0, one launch (start us, length us, event | category | flops | bytes accessed | tf_op | source)
XLA Modules:
  0.0 43.4 jit_solution(12898304676046826862)
XLA Ops:
  0.0 2.2 %copy-done = bf16[8,32,8192]{2,1,0:T(8,128)(2,1)S(1)} copy-done((bf16[8,32,8192]{2,1,0:T(8,128)(2,1)S(1)}, bf16[8,32,8192]{2,1,0:T(8,128)(2,1)}, u32[]{:S(2)}) %copy-start) | copy-done | bytes 4194328
  2.2 0.0 copy-start.1
  2.2 2.2 %copy-done.1 = bf16[8,32,8192]{2,1,0:T(8,128)(2,1)S(1)} copy-done((bf16[8,32,8192]{2,1,0:T(8,128)(2,1)S(1)}, bf16[8,32,8192]{2,1,0:T(8,128)(2,1)}, u32[]{:S(2)}) %copy-start.1) | copy-done | bytes 4194328
  4.4 0.0 copy-start.2
  4.4 1.2 %copy-done.2 = bf16[8192,64]{0,1:T(8,128)(2,1)S(1)} copy-done((bf16[8192,64]{0,1:T(8,128)(2,1)S(1)}, bf16[8192,64]{0,1:T(8,128)(2,1)}, u32[]{:S(2)}) %copy-start.2) | copy-done | bytes 1048600
  5.6 0.0 copy-start.3
  5.6 1.2 %copy-done.3 = bf16[8192,64]{0,1:T(8,128)(2,1)S(1)} copy-done((bf16[8192,64]{0,1:T(8,128)(2,1)S(1)}, bf16[8192,64]{0,1:T(8,128)(2,1)}, u32[]{:S(2)}) %copy-start.3) | copy-done | bytes 1048600
  6.8 3.6 %project.1 = bf16[264,128]{1,0:T(8,128)(2,1)S(1)} custom-call(bf16[256,8192]{1,0:T(8,128)(2,1)S(1)} %bitcast.9, bf16[256,8192]{1,0:T(8,128)(2,1)S(1)} %bitcast.10, bf16[64,8192]{1,0:T(8,128)(2,1)S(1)} %bitcast.11, bf16[64,8192]{1,0:T(8,128)(2,1)S(1)} %bitcast.12), custom_call_target="tpu_custom_call" | custom-call | tf_op jit(solution)/shard_map/project/pallas_call | solution.py:82
  10.4 3.1 %collective-permute-start.2 = (bf16[33,8,128]{2,1,0:T(8,128)(2,1)S(1)}, bf16[33,8,128]{2,1,0:T(8,128)(2,1)S(1)}, u32[]{:S(2)}, u32[]{:S(2)}) collective-permute-start(bf16[33,8,128]{2,1,0:T(8,128)(2,1)S(1)} %bitcast.13), channel_id=1, source_target_pairs={{0,1},{1,0},{2,3},{3,2},{4,5},{5,4},{6,7},{7,6},{8,9},{9,8},{10,11... | collective-permute-start | bytes 202760 | tf_op jit(solution)/shard_map/ppermute | solution.py:299
  13.5 2.6 %collective-permute-start.1 = (bf16[33,8,128]{2,1,0:T(8,128)(2,1)S(1)}, bf16[33,8,128]{2,1,0:T(8,128)(2,1)S(1)}, u32[]{:S(2)}, u32[]{:S(2)}) collective-permute-start(bf16[33,8,128]{2,1,0:T(8,128)(2,1)S(1)} %bitcast.14), channel_id=1, source_target_pairs={{0,2},{1,3},{2,0},{3,1},{4,6},{5,7},{6,4},{7,5},{8,10},{9,11},{10,... | collective-permute-start | bytes 202760 | tf_op jit(solution)/shard_map/ppermute | solution.py:299
  16.1 0.0 collective-permute-start
  16.1 0.0 collective-permute-done.2
  16.1 4.8 %collective-permute-done.1 = bf16[33,8,128]{2,1,0:T(8,128)(2,1)S(1)} collective-permute-done((bf16[33,8,128]{2,1,0:T(8,128)(2,1)S(1)}, bf16[33,8,128]{2,1,0:T(8,128)(2,1)S(1)}, u32[]{:S(2)}, u32[]{:S(2)}) %collective-permute-start.1) | collective-permute-done | bytes 67616 | tf_op jit(solution)/shard_map/ppermute | solution.py:299
  20.9 1.4 %collective-permute-done = bf16[33,8,128]{2,1,0:T(8,128)(2,1)S(1)} collective-permute-done((bf16[33,8,128]{2,1,0:T(8,128)(2,1)S(1)}, bf16[33,8,128]{2,1,0:T(8,128)(2,1)S(1)}, u32[]{:S(2)}, u32[]{:S(2)}) %collective-permute-start) | collective-permute-done | bytes 67616 | tf_op jit(solution)/shard_map/ppermute | solution.py:299
  22.4 0.1 pad_maximum_fusion
  22.5 2.5 %collective-permute-start.5 = (bf16[19,32,128]{2,1,0:T(8,128)(2,1)S(1)}, bf16[19,32,128]{2,1,0:T(8,128)(2,1)S(1)}, u32[]{:S(2)}, u32[]{:S(2)}) collective-permute-start(bf16[19,32,128]{2,1,0:T(8,128)(2,1)S(1)} %get-tuple-element.10), channel_id=1, source_target_pairs={{0,24},{4,28},{8,16},{12,20},{16,8},{20,12},{24,0},{28,4},{1,25},{... | collective-permute-start | bytes 466952 | tf_op jit(solution)/shard_map/ppermute | solution.py:299
  25.0 0.5 %collective-permute-start.3 = (bf16[19,32,128]{2,1,0:T(8,128)(2,1)S(1)}, bf16[19,32,128]{2,1,0:T(8,128)(2,1)S(1)}, u32[]{:S(2)}, u32[]{:S(2)}) collective-permute-start(bf16[19,32,128]{2,1,0:T(8,128)(2,1)S(1)} %get-tuple-element.11), channel_id=1, source_target_pairs={{0,8},{4,12},{8,0},{12,4},{16,24},{20,28},{24,16},{28,20},{1,9},{5... | collective-permute-start | bytes 466952 | tf_op jit(solution)/shard_map/ppermute | solution.py:299
  25.5 0.5 %collective-permute-start.4 = (bf16[19,32,128]{2,1,0:T(8,128)(2,1)S(1)}, bf16[19,32,128]{2,1,0:T(8,128)(2,1)S(1)}, u32[]{:S(2)}, u32[]{:S(2)}) collective-permute-start(bf16[19,32,128]{2,1,0:T(8,128)(2,1)S(1)} %get-tuple-element.12), channel_id=1, source_target_pairs={{0,16},{4,20},{8,24},{12,28},{16,0},{20,4},{24,8},{28,12},{1,17},{... | collective-permute-start | bytes 466952 | tf_op jit(solution)/shard_map/ppermute | solution.py:299
  26.0 0.0 collective-permute-start.6
  26.0 3.1 %collective-permute-done.5.refs_3_ = bf16[19,32,128]{2,1,0:T(8,128)(2,1)S(1)} collective-permute-done((bf16[19,32,128]{2,1,0:T(8,128)(2,1)S(1)}, bf16[19,32,128]{2,1,0:T(8,128)(2,1)S(1)}, u32[]{:S(2)}, u32[]{:S(2)}) %collective-permute-start.5) | collective-permute-done | bytes 155680 | tf_op jit(solution)/shard_map/ppermute | solution.py:299
  29.2 0.0 collective-permute-start.9
  29.2 1.7 %collective-permute-done.3.refs_1_ = bf16[19,32,128]{2,1,0:T(8,128)(2,1)S(1)} collective-permute-done((bf16[19,32,128]{2,1,0:T(8,128)(2,1)S(1)}, bf16[19,32,128]{2,1,0:T(8,128)(2,1)S(1)}, u32[]{:S(2)}, u32[]{:S(2)}) %collective-permute-start.3) | collective-permute-done | bytes 155680 | tf_op jit(solution)/shard_map/ppermute | solution.py:299
  30.9 0.0 collective-permute-start.7
  30.9 0.0 collective-permute-done.4.refs_2_
  30.9 0.5 %collective-permute-start.8 = (bf16[19,32,128]{2,1,0:T(8,128)(2,1)S(1)}, bf16[19,32,128]{2,1,0:T(8,128)(2,1)S(1)}, u32[]{:S(2)}, u32[]{:S(2)}) collective-permute-start(bf16[19,32,128]{2,1,0:T(8,128)(2,1)S(1)} %collective-permute-done.4.refs_2_), channel_id=1, source_target_pairs={{0,4},{4,0},{8,12},{12,8},{16,20},{20,16},{24,28},{28,24},{1,5},{5... | collective-permute-start | bytes 466952 | tf_op jit(solution)/shard_map/ppermute | solution.py:299
  31.4 0.0 copy-done.4
  31.4 0.1 pad_add_fusion.place_ref
  31.5 0.0 collective-permute-done.6.refs_4_
  31.5 0.0 collective-permute-done.9.refs_7_
  31.5 0.8 %collective-permute-done.7.refs_5_ = bf16[19,32,128]{2,1,0:T(8,128)(2,1)S(1)} collective-permute-done((bf16[19,32,128]{2,1,0:T(8,128)(2,1)S(1)}, bf16[19,32,128]{2,1,0:T(8,128)(2,1)S(1)}, u32[]{:S(2)}, u32[]{:S(2)}) %collective-permute-start.7) | collective-permute-done | bytes 155680 | tf_op jit(solution)/shard_map/ppermute | solution.py:299
  32.3 0.2 collective-permute-done.8.refs_6_
  32.5 10.9 %fisher.1 = f32[512,1024]{1,0:T(8,128)} custom-call(s32[2]{0:T(128)S(1)} %pad_add_fusion.place_ref, f32[1,1024]{1,0:T(1,128)S(1)} %bitcast.17, f32[1,256]{1,0:T(1,128)S(1)} %slice.12.panel_level_ref, bf16[19,32,128]{2,1,0:T(8,128)(2,1)S(1)} %get-tuple-element.13.refs_0_, bf16[19,32,128]{2,1,0:T(8,128)(2,1)S(1)} %collective-permute-done.3.refs_1_, ...), custom_call_target="tpu_custom_call" | custom-call | tf_op jit(solution)/shard_map/fisher/pallas_call | solution.py:262
  (9 shorter events, 0.1 us)
Async XLA Ops:
  0.0 2.2 %copy-start = (bf16[8,32,8192]{2,1,0:T(8,128)(2,1)S(1)}, bf16[8,32,8192]{2,1,0:T(8,128)(2,1)}, u32[]{:S(2)}) copy-start(bf16[8,32,8192]{2,1,0:T(8,128)(2,1)} %param.5) | copy-start | bytes 12582916
  2.2 2.2 %copy-start.1 = (bf16[8,32,8192]{2,1,0:T(8,128)(2,1)S(1)}, bf16[8,32,8192]{2,1,0:T(8,128)(2,1)}, u32[]{:S(2)}) copy-start(bf16[8,32,8192]{2,1,0:T(8,128)(2,1)} %param.6) | copy-start | bytes 12582916
  4.4 1.2 %copy-start.2 = (bf16[8192,64]{0,1:T(8,128)(2,1)S(1)}, bf16[8192,64]{0,1:T(8,128)(2,1)}, u32[]{:S(2)}) copy-start(bf16[8192,64]{0,1:T(8,128)(2,1)} %param.7) | copy-start | bytes 3145732
  5.6 1.2 %copy-start.3 = (bf16[8192,64]{0,1:T(8,128)(2,1)S(1)}, bf16[8192,64]{0,1:T(8,128)(2,1)}, u32[]{:S(2)}) copy-start(bf16[8192,64]{0,1:T(8,128)(2,1)} %param.8) | copy-start | bytes 3145732
  6.8 24.6 %copy-start.4 = (s32[4096]{0:T(1024)S(1)}, s32[4096]{0:T(1024)}, u32[]{:S(2)}) copy-start(s32[4096]{0:T(1024)} %param.9) | copy-start | bytes 49156
  10.4 5.7 %collective-permute-start.2 = (bf16[33,8,128]{2,1,0:T(8,128)(2,1)S(1)}, bf16[33,8,128]{2,1,0:T(8,128)(2,1)S(1)}, u32[]{:S(2)}, u32[]{:S(2)}) collective-permute-start(bf16[33,8,128]{2,1,0:T(8,128)(2,1)S(1)} %bitcast.13), channel_id=1, source_target_pairs={{0,1},{1,0},{2,3},{3,2},{4,5},{5,4},{6,7},{7,6},{8,9},{9,8},{10,11... | collective-permute-start | bytes 202760 | tf_op jit(solution)/shard_map/ppermute | solution.py:299
  13.5 7.4 %collective-permute-start.1 = (bf16[33,8,128]{2,1,0:T(8,128)(2,1)S(1)}, bf16[33,8,128]{2,1,0:T(8,128)(2,1)S(1)}, u32[]{:S(2)}, u32[]{:S(2)}) collective-permute-start(bf16[33,8,128]{2,1,0:T(8,128)(2,1)S(1)} %bitcast.14), channel_id=1, source_target_pairs={{0,2},{1,3},{2,0},{3,1},{4,6},{5,7},{6,4},{7,5},{8,10},{9,11},{10,... | collective-permute-start | bytes 202760 | tf_op jit(solution)/shard_map/ppermute | solution.py:299
  16.1 6.2 %collective-permute-start = (bf16[33,8,128]{2,1,0:T(8,128)(2,1)S(1)}, bf16[33,8,128]{2,1,0:T(8,128)(2,1)S(1)}, u32[]{:S(2)}, u32[]{:S(2)}) collective-permute-start(bf16[33,8,128]{2,1,0:T(8,128)(2,1)S(1)} %bitcast.15), channel_id=1, source_target_pairs={{0,3},{1,2},{2,1},{3,0},{4,7},{5,6},{6,5},{7,4},{8,11},{9,10},{10,... | collective-permute-start | bytes 202760 | tf_op jit(solution)/shard_map/ppermute | solution.py:299
  22.5 6.7 %collective-permute-start.5 = (bf16[19,32,128]{2,1,0:T(8,128)(2,1)S(1)}, bf16[19,32,128]{2,1,0:T(8,128)(2,1)S(1)}, u32[]{:S(2)}, u32[]{:S(2)}) collective-permute-start(bf16[19,32,128]{2,1,0:T(8,128)(2,1)S(1)} %get-tuple-element.10), channel_id=1, source_target_pairs={{0,24},{4,28},{8,16},{12,20},{16,8},{20,12},{24,0},{28,4},{1,25},{... | collective-permute-start | bytes 466952 | tf_op jit(solution)/shard_map/ppermute | solution.py:299
  25.0 5.9 %collective-permute-start.3 = (bf16[19,32,128]{2,1,0:T(8,128)(2,1)S(1)}, bf16[19,32,128]{2,1,0:T(8,128)(2,1)S(1)}, u32[]{:S(2)}, u32[]{:S(2)}) collective-permute-start(bf16[19,32,128]{2,1,0:T(8,128)(2,1)S(1)} %get-tuple-element.11), channel_id=1, source_target_pairs={{0,8},{4,12},{8,0},{12,4},{16,24},{20,28},{24,16},{28,20},{1,9},{5... | collective-permute-start | bytes 466952 | tf_op jit(solution)/shard_map/ppermute | solution.py:299
  25.5 5.4 %collective-permute-start.4 = (bf16[19,32,128]{2,1,0:T(8,128)(2,1)S(1)}, bf16[19,32,128]{2,1,0:T(8,128)(2,1)S(1)}, u32[]{:S(2)}, u32[]{:S(2)}) collective-permute-start(bf16[19,32,128]{2,1,0:T(8,128)(2,1)S(1)} %get-tuple-element.12), channel_id=1, source_target_pairs={{0,16},{4,20},{8,24},{12,28},{16,0},{20,4},{24,8},{28,12},{1,17},{... | collective-permute-start | bytes 466952 | tf_op jit(solution)/shard_map/ppermute | solution.py:299
  26.0 5.5 %collective-permute-start.6 = (bf16[19,32,128]{2,1,0:T(8,128)(2,1)S(1)}, bf16[19,32,128]{2,1,0:T(8,128)(2,1)S(1)}, u32[]{:S(2)}, u32[]{:S(2)}) collective-permute-start(bf16[19,32,128]{2,1,0:T(8,128)(2,1)S(1)} %get-tuple-element.13.refs_0_), channel_id=1, source_target_pairs={{0,4},{4,0},{8,12},{12,8},{16,20},{20,16},{24,28},{28,24},{1,5},{5... | collective-permute-start | bytes 466952 | tf_op jit(solution)/shard_map/ppermute | solution.py:299
  29.2 2.3 %collective-permute-start.9 = (bf16[19,32,128]{2,1,0:T(8,128)(2,1)S(1)}, bf16[19,32,128]{2,1,0:T(8,128)(2,1)S(1)}, u32[]{:S(2)}, u32[]{:S(2)}) collective-permute-start(bf16[19,32,128]{2,1,0:T(8,128)(2,1)S(1)} %collective-permute-done.5.refs_3_), channel_id=1, source_target_pairs={{0,4},{4,0},{8,12},{12,8},{16,20},{20,16},{24,28},{28,24},{1,5},{5... | collective-permute-start | bytes 466952 | tf_op jit(solution)/shard_map/ppermute | solution.py:299
  30.9 1.4 %collective-permute-start.7 = (bf16[19,32,128]{2,1,0:T(8,128)(2,1)S(1)}, bf16[19,32,128]{2,1,0:T(8,128)(2,1)S(1)}, u32[]{:S(2)}, u32[]{:S(2)}) collective-permute-start(bf16[19,32,128]{2,1,0:T(8,128)(2,1)S(1)} %collective-permute-done.3.refs_1_), channel_id=1, source_target_pairs={{0,4},{4,0},{8,12},{12,8},{16,20},{20,16},{24,28},{28,24},{1,5},{5... | collective-permute-start | bytes 466952 | tf_op jit(solution)/shard_map/ppermute | solution.py:299
  30.9 1.6 %collective-permute-start.8 = (bf16[19,32,128]{2,1,0:T(8,128)(2,1)S(1)}, bf16[19,32,128]{2,1,0:T(8,128)(2,1)S(1)}, u32[]{:S(2)}, u32[]{:S(2)}) collective-permute-start(bf16[19,32,128]{2,1,0:T(8,128)(2,1)S(1)} %collective-permute-done.4.refs_2_), channel_id=1, source_target_pairs={{0,4},{4,0},{8,12},{12,8},{16,20},{20,16},{24,28},{28,24},{1,5},{5... | collective-permute-start | bytes 466952 | tf_op jit(solution)/shard_map/ppermute | solution.py:299

commit v4 on v3

--- a/solution.py
+++ b/solution.py
@@ -1,4 +1,5 @@
 import functools
+import itertools
 
 import jax
 import jax.numpy as jnp
@@ -13,6 +14,7 @@
 SUB = 8
 STRIP = 64
 AHEAD = 1
+FILL = 2
 
 damp_coef = 0.25
 
@@ -31,18 +33,33 @@
     return high, (value - high.astype(jnp.float32)).astype(jnp.bfloat16)
 
 
+CUTS = 8
+
+
 def project_kernel(
     act_hbm, out_hbm, in_hbm, proj_hbm, packed_ref, act_buf, out_buf, in_buf, proj_buf, sems, *, local_ex, tok_len
 ):
-    tokens, rank_dim = act_buf.shape[0], in_buf.shape[0]
+    _, tokens, chunk = act_buf.shape
+    rank_dim = in_buf.shape[1]
     pieces = (in_hbm, in_buf), (act_hbm, act_buf), (proj_hbm, proj_buf), (out_hbm, out_buf)
-    copies = [pltpu.make_async_copy(whole, buf, sems.at[n]) for n, (whole, buf) in enumerate(pieces)]
-    for copy in copies:
-        copy.start()
-    for copy in copies:
-        copy.wait()
-    a_proj = mxu(act_buf[...], in_buf[...], LASTS)
-    g_turned = mxu(out_buf[...], proj_buf[...], LASTS).T
+    copies = [
+        [
+            pltpu.make_async_copy(whole.at[:, pl.ds(n * chunk, chunk)], buf.at[n], sems.at[n, which])
+            for which, (whole, buf) in enumerate(pieces)
+        ]
+        for n in range(CUTS)
+    ]
+    for group in copies:
+        for copy in group:
+            copy.start()
+    a_proj = jnp.zeros((tokens, rank_dim), jnp.float32)
+    g_proj = jnp.zeros((tokens, rank_dim), jnp.float32)
+    for n, group in enumerate(copies):
+        for copy in group:
+            copy.wait()
+        a_proj += mxu(act_buf[n], in_buf[n], LASTS)
+        g_proj += mxu(out_buf[n], proj_buf[n], LASTS)
+    g_turned = g_proj.T
     pairs = rank_dim * rank_dim // LANES
     example = lax.broadcasted_iota(jnp.int32, (local_ex, tokens), 0)
     owner = lax.broadcasted_iota(jnp.int32, (local_ex, tokens), 1) // tok_len
@@ -85,24 +102,29 @@
         out_specs=pl.BlockSpec(memory_space=pltpu.VMEM),
         out_shape=jax.ShapeDtypeStruct(((pairs + 1) * local_ex, LANES), jnp.bfloat16),
         scratch_shapes=[
-            pltpu.VMEM((tokens, model_dim), jnp.bfloat16),
-            pltpu.VMEM((tokens, model_dim), jnp.bfloat16),
-            pltpu.VMEM((rank_dim, model_dim), jnp.bfloat16),
-            pltpu.VMEM((rank_dim, model_dim), jnp.bfloat16),
-            pltpu.SemaphoreType.DMA((4,)),
+            pltpu.VMEM((CUTS, tokens, model_dim // CUTS), jnp.bfloat16),
+            pltpu.VMEM((CUTS, tokens, model_dim // CUTS), jnp.bfloat16),
+            pltpu.VMEM((CUTS, rank_dim, model_dim // CUTS), jnp.bfloat16),
+            pltpu.VMEM((CUTS, rank_dim, model_dim // CUTS), jnp.bfloat16),
+            pltpu.SemaphoreType.DMA((CUTS, 4)),
         ],
         compiler_params=pltpu.CompilerParams(vmem_limit_bytes=32 * 2**20),
         name="project",
     )(
-        activations.reshape(tokens, model_dim),
-        out_grads.reshape(tokens, model_dim),
-        proj_in.T,
-        proj_out.T,
+        *[
+            pltpu.with_memory_space_constraint(whole, pltpu.HBM)
+            for whole in (
+                activations.reshape(tokens, model_dim),
+                out_grads.reshape(tokens, model_dim),
+                proj_in.T,
+                proj_out.T,
+            )
+        ]
     )
     return packed.reshape(pairs + 1, local_ex, LANES)
 
 
-def eliminate(work_ref, done_ref):
+def eliminate(work_ref, done_ref, fillers):
     tiles = BOTH // LANES
     groups = STRIP // SUB
     sub_at = lax.broadcasted_iota(jnp.int32, (SUB, LANES), 0)
@@ -157,6 +179,8 @@
                     for t in live:
                         rows[g][t] = rows[g][t] - weight * scaled[t]
             roots.append(lax.rsqrt(pivots))
+            for filler in itertools.islice(fillers, FILL):
+                filler()
             if ahead is not None:
                 cols = ahead
                 for m, late in enumerate(spread(block + 1, near, groups)):
@@ -185,111 +209,115 @@
 
 
 def fisher_kernel(
-    place_ref, level_ref, panel_level_ref, *refs, sources, row_blocks, col_blocks, total_ex, feats
+    place_ref, level_ref, panel_level_ref, *refs, sources, total_ex, feats
 ):
     arrived = refs[:sources]
-    out_ref = refs[sources]
-    g_row, g_col, g_panel, work, done, lower, mix_high, mix_low, panel_mix, damp_ref = refs[sources + 1 :]
-    step = pl.program_id(0)
+    out_ref, g_panel, g_row, g_col, turned, work, done, weights, held, sems = refs[sources:]
     row_at, col_at = place_ref[0], place_ref[1]
-    panel_blocks = BOTH // LANES
     here = arrived[0].shape[1]
-
-    @pl.when(step == 0)
-    def _():
-        row_base = lax.rem(row_at, 2) * row_blocks
-        col_base = 2 * row_blocks
-        panel_base = col_base + col_blocks
-        total = jnp.zeros((here, LANES), jnp.float32)
-        for n, piece in enumerate(arrived):
-            at = slice(n * here, (n + 1) * here)
-            for b in range(panel_blocks):
-                g_panel[at, b * LANES : (b + 1) * LANES] = piece[panel_base + b]
-            for b in range(row_blocks):
-                g_row[at, b * LANES : (b + 1) * LANES] = piece[row_base + b]
-            for b in range(col_blocks):
-                g_col[b // panel_blocks, at, b % panel_blocks * LANES : (b % panel_blocks + 1) * LANES] = piece[
-                    col_base + b
-                ]
-            total += piece[panel_base + panel_blocks].astype(jnp.float32)
-        total_sq = jnp.sum(jnp.sum(total, axis=0, keepdims=True), axis=1, keepdims=True)
-        damping = damp_coef * total_sq / (total_ex * feats)
-        damp_ref[...] = jnp.broadcast_to(damping, damp_ref.shape)
-        panel = g_panel[...]
-        rows_at = lax.broadcasted_iota(jnp.int32, (BOTH, BOTH), 0)
-        cols_at = lax.broadcasted_iota(jnp.int32, (BOTH, BOTH), 1)
-        same = rows_at == cols_at
-        work[:, :BOTH] = mxu(panel, panel, FIRSTS) * (1.0 / total_ex) + jnp.where(
-            same, damping * panel_level_ref[...], 0.0
-        )
-        work[:, BOTH:] = jnp.where(same, 1.0, 0.0)
-        eliminate(work, done)
-        lower[...] = done[:, :BOTH].T
-        w_high, w_low = halves(done[:, BOTH:])
-        mixed = mxu(panel, w_high, LASTS) + mxu(panel, w_low, LASTS)
-        y_high, y_low = halves(mixed)
-        cross = mxu(y_high, y_low, LASTS)
-        outer = mxu(y_high, y_high, LASTS) + cross + cross.T
-        ex_rows = lax.broadcasted_iota(jnp.int32, outer.shape, 0)
-        ex_cols = lax.broadcasted_iota(jnp.int32, outer.shape, 1)
-        mix = (jnp.where(ex_rows == ex_cols, 1.0, 0.0) - outer * (1.0 / total_ex)) * (1.0 / total_ex)
-        mix_high[...], mix_low[...] = halves(mix)
-        panel_mix[...] = mixed * (1.0 / total_ex)
-
-    in_panel = (col_at == 0) & (step == 0)
-    cols = g_col[step]
-    weights = mxu(mix_high[...], cols) + mxu(mix_low[...], cols)
-    weights = jnp.where(in_panel, panel_mix[...], weights)
-    high, low = halves(weights)
-    rows = g_row[...]
-    tile = mxu(rows, high, FIRSTS) + mxu(rows, low, FIRSTS)
-    row_span, width = tile.shape
-    col_first = (col_at * pl.num_programs(0) + step) * width
-    row_glob = row_at * row_span + lax.broadcasted_iota(jnp.int32, tile.shape, 0)
-    col_glob = col_first + lax.broadcasted_iota(jnp.int32, tile.shape, 1)
-    out_ref[...] = tile + jnp.where(row_glob == col_glob, damp_ref[0:1, 0:1] * level_ref[...], 0.0)
-
-    @pl.when(row_at == 0)
-    def _():
-        out_ref[:BOTH, :] = jnp.where(in_panel, lower[...], 0.0)
+    row_span, col_span = held.shape
+    row_blocks, col_blocks, panel_blocks = row_span // LANES, col_span // LANES, BOTH // LANES
+    examples = sources * here
+    col_base = 2 * row_blocks
+    panel_base = col_base + col_blocks
+    row_base = lax.rem(row_at, 2) * row_blocks
+
+    def gather(target, base, blocks, n):
+        for b in range(blocks):
+            target[n * here : (n + 1) * here, b * LANES : (b + 1) * LANES] = arrived[n][base + b]
+
+    total = jnp.zeros((here, LANES), jnp.float32)
+    for n in range(sources):
+        gather(g_panel, panel_base, panel_blocks, n)
+        total += arrived[n][panel_base + panel_blocks].astype(jnp.float32)
+    total_sq = jnp.sum(jnp.sum(total, axis=0, keepdims=True), axis=1, keepdims=True)
+    damping = damp_coef * total_sq / (total_ex * feats)
+    panel = g_panel[...]
+    rows_at = lax.broadcasted_iota(jnp.int32, (BOTH, BOTH), 0)
+    cols_at = lax.broadcasted_iota(jnp.int32, (BOTH, BOTH), 1)
+    same = rows_at == cols_at
+    work[:, :BOTH] = mxu(panel, panel, FIRSTS) * (1.0 / total_ex) + jnp.where(
+        same, damping * panel_level_ref[...], 0.0
+    )
+    work[:, BOTH:] = jnp.where(same, 1.0, 0.0)
+
+    def turn(first):
+        turned[first : first + LANES, :] = g_row[:, first : first + LANES].T
+
+    fillers = iter(
+        [functools.partial(gather, g_row, row_base, row_blocks, n) for n in range(sources)]
+        + [functools.partial(turn, first) for first in range(0, row_span, LANES)]
+        + [functools.partial(gather, g_col, col_base, col_blocks, n) for n in range(sources)]
+    )
+    eliminate(work, done, fillers)
+    for filler in fillers:
+        filler()
+
+    w_high, w_low = halves(done[:, BOTH:])
+    mixed = mxu(panel, w_high, LASTS) + mxu(panel, w_low, LASTS)
+    y_high, y_low = halves(mixed)
+    cross = mxu(y_high, y_low, LASTS)
+    outer = mxu(y_high, y_high, LASTS) + cross + cross.T
+    ex_rows = lax.broadcasted_iota(jnp.int32, outer.shape, 0)
+    ex_cols = lax.broadcasted_iota(jnp.int32, outer.shape, 1)
+    mix = (jnp.where(ex_rows == ex_cols, 1.0, 0.0) - outer * (1.0 / total_ex)) * (1.0 / total_ex)
+    both = jnp.concatenate(halves(mix), axis=1)
+    for first in range(0, col_span, BOTH):
+        lanes = slice(first, first + BOTH)
+        cols = g_col[:, lanes]
+        value = mxu(both, jnp.concatenate([cols, cols], axis=0))
+        if first == 0:
+            value = jnp.where(col_at == 0, mixed * (1.0 / total_ex), value)
+        weights[:examples, lanes], weights[examples:, lanes] = halves(value)
+
+    lower = done[:, :BOTH].T
+    eye = lax.broadcasted_iota(jnp.int32, (LANES, LANES), 0) == lax.broadcasted_iota(
+        jnp.int32, (LANES, LANES), 1
+    )
+    copies = []
+    for strip in range(row_blocks):
+        rows = slice(strip * LANES, (strip + 1) * LANES)
+        left = turned[rows, :]
+        held[rows, :] = mxu(jnp.concatenate([left, left], axis=1), weights[...])
+        block = row_at * row_blocks + strip - col_at * col_blocks
+        inside = (block >= 0) & (block < col_blocks)
+        lanes = pl.ds(pl.multiple_of(jnp.clip(block, 0, col_blocks - 1) * LANES, LANES), LANES)
+        held[rows, lanes] += jnp.where(eye & inside, level_ref[:, lanes] * damping, 0.0)
+        if strip * LANES < BOTH:
+
+            @pl.when(row_at == 0)
+            def _(rows=rows):
+                held[rows, :] = jnp.zeros((LANES, col_span), jnp.float32)
+                held[rows, :BOTH] = jnp.where(col_at == 0, lower[rows, :], 0.0)
+
+        copy = pltpu.make_async_copy(held.at[rows, :], out_ref.at[rows, :], sems.at[strip])
+        copy.start()
+        copies.append(copy)
+    for copy in copies:
+        copy.wait()
 
 
 def fisher(place, col_levels, panel_levels, arrived, row_blocks, col_blocks, total_ex, feats):
     row_span, col_span = row_blocks * LANES, col_blocks * LANES
     sources = len(arrived)
-    examples = sources * arrived[0].shape[1]
     vmem = pl.BlockSpec(memory_space=pltpu.VMEM)
     return pl.pallas_call(
-        functools.partial(
-            fisher_kernel,
-            sources=sources,
-            row_blocks=row_blocks,
-            col_blocks=col_blocks,
-            total_ex=total_ex,
-            feats=feats,
-        ),
-        grid=(col_span // BOTH,),
-        in_specs=[
-            pl.BlockSpec(memory_space=pltpu.SMEM),
-            pl.BlockSpec((1, BOTH), lambda n: (0, n)),
-            vmem,
-        ]
-        + [vmem] * sources,
-        out_specs=pl.BlockSpec((row_span, BOTH), lambda n: (0, n)),
+        functools.partial(fisher_kernel, sources=sources, total_ex=total_ex, feats=feats),
+        in_specs=[pl.BlockSpec(memory_space=pltpu.SMEM)] + [vmem] * (2 + sources),
+        out_specs=pl.BlockSpec(memory_space=pltpu.HBM),
         out_shape=jax.ShapeDtypeStruct((row_span, col_span), jnp.float32),
         scratch_shapes=[
-            pltpu.VMEM((examples, row_span), jnp.bfloat16),
-            pltpu.VMEM((col_span // BOTH, examples, BOTH), jnp.bfloat16),
-            pltpu.VMEM((examples, BOTH), jnp.bfloat16),
+            pltpu.VMEM((total_ex, BOTH), jnp.bfloat16),
+            pltpu.VMEM((total_ex, row_span), jnp.bfloat16),
+            pltpu.VMEM((total_ex, col_span), jnp.bfloat16),
+            pltpu.VMEM((row_span, total_ex), jnp.bfloat16),
             pltpu.VMEM((BOTH, 2 * BOTH), jnp.float32),
             pltpu.VMEM((BOTH, 2 * BOTH), jnp.float32),
-            pltpu.VMEM((BOTH, BOTH), jnp.float32),
-            pltpu.VMEM((examples, examples), jnp.bfloat16),
-            pltpu.VMEM((examples, examples), jnp.bfloat16),
-            pltpu.VMEM((examples, BOTH), jnp.float32),
-            pltpu.VMEM((SUB, LANES), jnp.float32),
+            pltpu.VMEM((2 * total_ex, col_span), jnp.bfloat16),
+            pltpu.VMEM((row_span, col_span), jnp.float32),
+            pltpu.SemaphoreType.DMA((row_blocks,)),
         ],
-        compiler_params=pltpu.CompilerParams(vmem_limit_bytes=48 * 2**20),
+        compiler_params=pltpu.CompilerParams(vmem_limit_bytes=32 * 2**20),
         name="fisher",
     )(place, col_levels, panel_levels, *arrived)
 
@@ -324,14 +352,14 @@
         line[: BOTH // LANES],
         line[blocks:],
     ]
+    pairs = n_rows // 2
     pair_at = row_at // 2
 
     def bundle(pair):
         wanted = lax.dynamic_slice_in_dim(line, pair * 2 * row_blocks, 2 * row_blocks)
         return jnp.concatenate([wanted] + common)
 
-    own = bundle(pair_at)
-    got = [own] + [swap(bundle(pair_at ^ mask), "row", 2 * mask) for mask in range(1, n_rows // 2)]
+    got = [bundle(pair_at)] + [swap(bundle(pair_at ^ mask), "row", 2 * mask) for mask in range(1, pairs)]
     arrived = got + [swap(piece, "row", 1) for piece in got]
     return fisher(
         place, col_levels, levels[:, :BOTH], arrived, row_blocks, col_blocks, total_ex, feats

time: 43.6 us -> 37 us (0.85)
  local copies, waits for them, and re-layouts: 6.88 us -> 0.06 us
    unnamed x10 -> x2, local copies, waits for them, and re-layouts: 6.83 us -> 0.01 us
    pallas_call x1, Pallas kernels: 3.57 us -> 5.27 us  [project(): pl.pallas_call(functools.partial(project_kernel, local_ex=local_ex, tok_l...]
    pallas_call x1, Pallas kernels: 10.9 us -> 9.49 us  [fisher(): pl.pallas_call(functools.partial(fisher_kernel, sources=sources, total_ex...]
where the time goes in v4:
time: 37 us; the launch traced here: 36.9 us
  Pallas kernels  14.8 us (40%)
  waiting for transfers between devices  12 us (32%)
  starting transfers between devices  9.74 us (26%)
    ppermute x10, waiting for transfers between devices, swap(): return lax.ppermute(block, axis, [(n, n ^ mask) for n in range(size)])  12 us
    ppermute x10, starting transfers between devices, swap(): return lax.ppermute(block, axis, [(n, n ^ mask) for n in range(size)])  9.74 us
    pallas_call x1, Pallas kernels, fisher(): pl.pallas_call(functools.partial(fisher_kernel, sources=sources, total_ex...  9.49 us
    pallas_call x1, Pallas kernels, project(): pl.pallas_call(functools.partial(project_kernel, local_ex=local_ex, tok_l...  5.27 us
  transfers between devices with their start and end apart: 10, of which 6 were waited for; matrix products, arithmetic and copies ran while one was open for 0% of the time, Pallas kernels for 0%

profile of v4, /device:TPU:0, one launch (start us, length us, event | category | flops | bytes accessed | tf_op | source)
XLA Modules:
  0.0 36.9 jit_solution(1362086134644409579)
XLA Ops:
  0.0 0.0 copy-start
  0.0 5.3 %project.1 = bf16[264,128]{1,0:T(8,128)(2,1)S(1)} custom-call(bf16[256,8192]{1,0:T(8,128)(2,1)} %bitcast.14, bf16[256,8192]{1,0:T(8,128)(2,1)} %bitcast.15, bf16[64,8192]{1,0:T(8,128)(2,1)} %bitcast.16, bf16[64,8192]{1,0:T(8,128)(2,1)} %bitcast.17), custom_call_target="tpu_custom_call" | custom-call | tf_op jit(solution)/shard_map/project/pallas_call | solution.py:99
  5.3 3.1 %collective-permute-start.2 = (bf16[33,8,128]{2,1,0:T(8,128)(2,1)S(1)}, bf16[33,8,128]{2,1,0:T(8,128)(2,1)S(1)}, u32[]{:S(2)}, u32[]{:S(2)}) collective-permute-start(bf16[33,8,128]{2,1,0:T(8,128)(2,1)S(1)} %bitcast.9), channel_id=1, source_target_pairs={{0,1},{1,0},{2,3},{3,2},{4,5},{5,4},{6,7},{7,6},{8,9},{9,8},{10,11... | collective-permute-start | bytes 202760 | tf_op jit(solution)/shard_map/ppermute | solution.py:327
  8.4 2.6 %collective-permute-start.1 = (bf16[33,8,128]{2,1,0:T(8,128)(2,1)S(1)}, bf16[33,8,128]{2,1,0:T(8,128)(2,1)S(1)}, u32[]{:S(2)}, u32[]{:S(2)}) collective-permute-start(bf16[33,8,128]{2,1,0:T(8,128)(2,1)S(1)} %bitcast.10), channel_id=1, source_target_pairs={{0,2},{1,3},{2,0},{3,1},{4,6},{5,7},{6,4},{7,5},{8,10},{9,11},{10,... | collective-permute-start | bytes 202760 | tf_op jit(solution)/shard_map/ppermute | solution.py:327
  11.0 0.0 collective-permute-start
  11.0 0.0 collective-permute-done.2
  11.0 4.8 %collective-permute-done.1 = bf16[33,8,128]{2,1,0:T(8,128)(2,1)S(1)} collective-permute-done((bf16[33,8,128]{2,1,0:T(8,128)(2,1)S(1)}, bf16[33,8,128]{2,1,0:T(8,128)(2,1)S(1)}, u32[]{:S(2)}, u32[]{:S(2)}) %collective-permute-start.1) | collective-permute-done | bytes 67616 | tf_op jit(solution)/shard_map/ppermute | solution.py:327
  15.8 1.4 %collective-permute-done = bf16[33,8,128]{2,1,0:T(8,128)(2,1)S(1)} collective-permute-done((bf16[33,8,128]{2,1,0:T(8,128)(2,1)S(1)}, bf16[33,8,128]{2,1,0:T(8,128)(2,1)S(1)}, u32[]{:S(2)}, u32[]{:S(2)}) %collective-permute-start) | collective-permute-done | bytes 67616 | tf_op jit(solution)/shard_map/ppermute | solution.py:327
  17.3 0.1 pad_maximum_fusion
  17.3 2.5 %collective-permute-start.5 = (bf16[19,32,128]{2,1,0:T(8,128)(2,1)S(1)}, bf16[19,32,128]{2,1,0:T(8,128)(2,1)S(1)}, u32[]{:S(2)}, u32[]{:S(2)}) collective-permute-start(bf16[19,32,128]{2,1,0:T(8,128)(2,1)S(1)} %get-tuple-element.10), channel_id=1, source_target_pairs={{0,24},{4,28},{8,16},{12,20},{16,8},{20,12},{24,0},{28,4},{1,25},{... | collective-permute-start | bytes 466952 | tf_op jit(solution)/shard_map/ppermute | solution.py:327
  19.9 0.5 %collective-permute-start.3 = (bf16[19,32,128]{2,1,0:T(8,128)(2,1)S(1)}, bf16[19,32,128]{2,1,0:T(8,128)(2,1)S(1)}, u32[]{:S(2)}, u32[]{:S(2)}) collective-permute-start(bf16[19,32,128]{2,1,0:T(8,128)(2,1)S(1)} %get-tuple-element.11), channel_id=1, source_target_pairs={{0,8},{4,12},{8,0},{12,4},{16,24},{20,28},{24,16},{28,20},{1,9},{5... | collective-permute-start | bytes 466952 | tf_op jit(solution)/shard_map/ppermute | solution.py:327
  20.4 0.5 %collective-permute-start.4 = (bf16[19,32,128]{2,1,0:T(8,128)(2,1)S(1)}, bf16[19,32,128]{2,1,0:T(8,128)(2,1)S(1)}, u32[]{:S(2)}, u32[]{:S(2)}) collective-permute-start(bf16[19,32,128]{2,1,0:T(8,128)(2,1)S(1)} %get-tuple-element.12), channel_id=1, source_target_pairs={{0,16},{4,20},{8,24},{12,28},{16,0},{20,4},{24,8},{28,12},{1,17},{... | collective-permute-start | bytes 466952 | tf_op jit(solution)/shard_map/ppermute | solution.py:327
  20.9 0.0 collective-permute-start.6
  20.9 3.1 %collective-permute-done.5.refs_3_ = bf16[19,32,128]{2,1,0:T(8,128)(2,1)S(1)} collective-permute-done((bf16[19,32,128]{2,1,0:T(8,128)(2,1)S(1)}, bf16[19,32,128]{2,1,0:T(8,128)(2,1)S(1)}, u32[]{:S(2)}, u32[]{:S(2)}) %collective-permute-start.5) | collective-permute-done | bytes 155680 | tf_op jit(solution)/shard_map/ppermute | solution.py:327
  24.0 0.0 collective-permute-start.9
  24.0 1.7 %collective-permute-done.3.refs_1_ = bf16[19,32,128]{2,1,0:T(8,128)(2,1)S(1)} collective-permute-done((bf16[19,32,128]{2,1,0:T(8,128)(2,1)S(1)}, bf16[19,32,128]{2,1,0:T(8,128)(2,1)S(1)}, u32[]{:S(2)}, u32[]{:S(2)}) %collective-permute-start.3) | collective-permute-done | bytes 155680 | tf_op jit(solution)/shard_map/ppermute | solution.py:327
  25.8 0.0 collective-permute-start.7
  25.8 0.0 collective-permute-done.4.refs_2_
  25.8 0.5 %collective-permute-start.8 = (bf16[19,32,128]{2,1,0:T(8,128)(2,1)S(1)}, bf16[19,32,128]{2,1,0:T(8,128)(2,1)S(1)}, u32[]{:S(2)}, u32[]{:S(2)}) collective-permute-start(bf16[19,32,128]{2,1,0:T(8,128)(2,1)S(1)} %collective-permute-done.4.refs_2_), channel_id=1, source_target_pairs={{0,4},{4,0},{8,12},{12,8},{16,20},{20,16},{24,28},{28,24},{1,5},{5... | collective-permute-start | bytes 466952 | tf_op jit(solution)/shard_map/ppermute | solution.py:327
  26.3 0.0 copy-done
  26.3 0.1 pad_add_fusion.place_ref
  26.4 0.0 collective-permute-done.6.refs_4_
  26.4 0.0 collective-permute-done.9.refs_7_
  26.4 0.8 %collective-permute-done.7.refs_5_ = bf16[19,32,128]{2,1,0:T(8,128)(2,1)S(1)} collective-permute-done((bf16[19,32,128]{2,1,0:T(8,128)(2,1)S(1)}, bf16[19,32,128]{2,1,0:T(8,128)(2,1)S(1)}, u32[]{:S(2)}, u32[]{:S(2)}) %collective-permute-start.7) | collective-permute-done | bytes 155680 | tf_op jit(solution)/shard_map/ppermute | solution.py:327
  27.1 0.2 collective-permute-done.8.refs_6_
  27.4 9.5 %fisher.1 = f32[512,1024]{1,0:T(8,128)} custom-call(s32[2]{0:T(128)S(1)} %pad_add_fusion.place_ref, f32[1,1024]{1,0:T(1,128)S(1)} %bitcast.13, f32[1,256]{1,0:T(1,128)S(1)} %slice.12.panel_level_ref, bf16[19,32,128]{2,1,0:T(8,128)(2,1)S(1)} %get-tuple-element.13.refs_0_, bf16[19,32,128]{2,1,0:T(8,128)(2,1)S(1)} %collective-permute-done.3.refs_1_, ...), custom_call_target="tpu_custom_call" | custom-call | tf_op jit(solution)/shard_map/fisher/pallas_call | solution.py:304
  (7 shorter events, 0.1 us)
Async XLA Ops:
  0.0 26.3 %copy-start = (s32[4096]{0:T(1024)S(1)}, s32[4096]{0:T(1024)}, u32[]{:S(2)}) copy-start(s32[4096]{0:T(1024)} %param.9) | copy-start | bytes 49156
  5.3 5.7 %collective-permute-start.2 = (bf16[33,8,128]{2,1,0:T(8,128)(2,1)S(1)}, bf16[33,8,128]{2,1,0:T(8,128)(2,1)S(1)}, u32[]{:S(2)}, u32[]{:S(2)}) collective-permute-start(bf16[33,8,128]{2,1,0:T(8,128)(2,1)S(1)} %bitcast.9), channel_id=1, source_target_pairs={{0,1},{1,0},{2,3},{3,2},{4,5},{5,4},{6,7},{7,6},{8,9},{9,8},{10,11... | collective-permute-start | bytes 202760 | tf_op jit(solution)/shard_map/ppermute | solution.py:327
  8.4 7.4 %collective-permute-start.1 = (bf16[33,8,128]{2,1,0:T(8,128)(2,1)S(1)}, bf16[33,8,128]{2,1,0:T(8,128)(2,1)S(1)}, u32[]{:S(2)}, u32[]{:S(2)}) collective-permute-start(bf16[33,8,128]{2,1,0:T(8,128)(2,1)S(1)} %bitcast.10), channel_id=1, source_target_pairs={{0,2},{1,3},{2,0},{3,1},{4,6},{5,7},{6,4},{7,5},{8,10},{9,11},{10,... | collective-permute-start | bytes 202760 | tf_op jit(solution)/shard_map/ppermute | solution.py:327
  11.0 6.2 %collective-permute-start = (bf16[33,8,128]{2,1,0:T(8,128)(2,1)S(1)}, bf16[33,8,128]{2,1,0:T(8,128)(2,1)S(1)}, u32[]{:S(2)}, u32[]{:S(2)}) collective-permute-start(bf16[33,8,128]{2,1,0:T(8,128)(2,1)S(1)} %bitcast.11), channel_id=1, source_target_pairs={{0,3},{1,2},{2,1},{3,0},{4,7},{5,6},{6,5},{7,4},{8,11},{9,10},{10,... | collective-permute-start | bytes 202760 | tf_op jit(solution)/shard_map/ppermute | solution.py:327
  17.3 6.7 %collective-permute-start.5 = (bf16[19,32,128]{2,1,0:T(8,128)(2,1)S(1)}, bf16[19,32,128]{2,1,0:T(8,128)(2,1)S(1)}, u32[]{:S(2)}, u32[]{:S(2)}) collective-permute-start(bf16[19,32,128]{2,1,0:T(8,128)(2,1)S(1)} %get-tuple-element.10), channel_id=1, source_target_pairs={{0,24},{4,28},{8,16},{12,20},{16,8},{20,12},{24,0},{28,4},{1,25},{... | collective-permute-start | bytes 466952 | tf_op jit(solution)/shard_map/ppermute | solution.py:327
  19.9 5.9 %collective-permute-start.3 = (bf16[19,32,128]{2,1,0:T(8,128)(2,1)S(1)}, bf16[19,32,128]{2,1,0:T(8,128)(2,1)S(1)}, u32[]{:S(2)}, u32[]{:S(2)}) collective-permute-start(bf16[19,32,128]{2,1,0:T(8,128)(2,1)S(1)} %get-tuple-element.11), channel_id=1, source_target_pairs={{0,8},{4,12},{8,0},{12,4},{16,24},{20,28},{24,16},{28,20},{1,9},{5... | collective-permute-start | bytes 466952 | tf_op jit(solution)/shard_map/ppermute | solution.py:327
  20.4 5.4 %collective-permute-start.4 = (bf16[19,32,128]{2,1,0:T(8,128)(2,1)S(1)}, bf16[19,32,128]{2,1,0:T(8,128)(2,1)S(1)}, u32[]{:S(2)}, u32[]{:S(2)}) collective-permute-start(bf16[19,32,128]{2,1,0:T(8,128)(2,1)S(1)} %get-tuple-element.12), channel_id=1, source_target_pairs={{0,16},{4,20},{8,24},{12,28},{16,0},{20,4},{24,8},{28,12},{1,17},{... | collective-permute-start | bytes 466952 | tf_op jit(solution)/shard_map/ppermute | solution.py:327
  20.9 5.5 %collective-permute-start.6 = (bf16[19,32,128]{2,1,0:T(8,128)(2,1)S(1)}, bf16[19,32,128]{2,1,0:T(8,128)(2,1)S(1)}, u32[]{:S(2)}, u32[]{:S(2)}) collective-permute-start(bf16[19,32,128]{2,1,0:T(8,128)(2,1)S(1)} %get-tuple-element.13.refs_0_), channel_id=1, source_target_pairs={{0,4},{4,0},{8,12},{12,8},{16,20},{20,16},{24,28},{28,24},{1,5},{5... | collective-permute-start | bytes 466952 | tf_op jit(solution)/shard_map/ppermute | solution.py:327
  24.0 2.3 %collective-permute-start.9 = (bf16[19,32,128]{2,1,0:T(8,128)(2,1)S(1)}, bf16[19,32,128]{2,1,0:T(8,128)(2,1)S(1)}, u32[]{:S(2)}, u32[]{:S(2)}) collective-permute-start(bf16[19,32,128]{2,1,0:T(8,128)(2,1)S(1)} %collective-permute-done.5.refs_3_), channel_id=1, source_target_pairs={{0,4},{4,0},{8,12},{12,8},{16,20},{20,16},{24,28},{28,24},{1,5},{5... | collective-permute-start | bytes 466952 | tf_op jit(solution)/shard_map/ppermute | solution.py:327
  25.8 1.4 %collective-permute-start.7 = (bf16[19,32,128]{2,1,0:T(8,128)(2,1)S(1)}, bf16[19,32,128]{2,1,0:T(8,128)(2,1)S(1)}, u32[]{:S(2)}, u32[]{:S(2)}) collective-permute-start(bf16[19,32,128]{2,1,0:T(8,128)(2,1)S(1)} %collective-permute-done.3.refs_1_), channel_id=1, source_target_pairs={{0,4},{4,0},{8,12},{12,8},{16,20},{20,16},{24,28},{28,24},{1,5},{5... | collective-permute-start | bytes 466952 | tf_op jit(solution)/shard_map/ppermute | solution.py:327
  25.8 1.6 %collective-permute-start.8 = (bf16[19,32,128]{2,1,0:T(8,128)(2,1)S(1)}, bf16[19,32,128]{2,1,0:T(8,128)(2,1)S(1)}, u32[]{:S(2)}, u32[]{:S(2)}) collective-permute-start(bf16[19,32,128]{2,1,0:T(8,128)(2,1)S(1)} %collective-permute-done.4.refs_2_), channel_id=1, source_target_pairs={{0,4},{4,0},{8,12},{12,8},{16,20},{20,16},{24,28},{28,24},{1,5},{5... | collective-permute-start | bytes 466952 | tf_op jit(solution)/shard_map/ppermute | solution.py:327

commit v5 on v4

--- a/solution.py
+++ b/solution.py
@@ -34,6 +34,11 @@
 
 
 CUTS = 8
+
+
+def thirds(value):
+    high = value.astype(jnp.bfloat16)
+    return (high, *halves(value - high.astype(jnp.float32)))
 
 
 def project_kernel(
@@ -160,13 +165,15 @@
                 inverse = 1.0 / pivot
                 inverses.append(inverse)
                 pivots = jnp.where(sub_at == j, pivot, pivots)
+                near_scaled = lead[block] * inverse
+                next_scaled = lead[block + 1] * inverse if ahead is not None else None
                 for m in range(j + 1, SUB):
-                    factor = lead[block][m : m + 1, :] * inverse
+                    factor = near_scaled[m : m + 1, :]
                     for g in cols[m]:
                         cols[m][g] = cols[m][g] - lead[g] * factor
                 if ahead is not None:
                     for m in range(SUB):
-                        factor = lead[block + 1][m : m + 1, :] * inverse
+                        factor = next_scaled[m : m + 1, :]
                         for g in ahead[m]:
                             ahead[m][g] = ahead[m][g] - lead[g] * factor
                 scaled = {t: rows[block][t][j : j + 1, :] * inverse for t in live}
@@ -200,11 +207,15 @@
             first = beyond // LANES * LANES
             last = BOTH + -(-beyond // LANES) * LANES
             right = done_ref[start:beyond, first:last]
+            rh, rm, rl = thirds(right)
             cuts = [beyond, beyond + STRIP] + ([BOTH] if beyond + STRIP < BOTH else [])
             for low, high in zip(cuts[:-1], cuts[1:]):
                 left = done_ref[start:beyond, low:high]
-                work_ref[low:high, first:last] -= lax.dot_general(
-                    left, right, FIRSTS, precision=HIGHEST, preferred_element_type=jnp.float32
+                lh, lm, ll = thirds(left)
+                work_ref[low:high, first:last] -= mxu(
+                    jnp.concatenate([lh, lh, lm, lh, ll, lm], axis=0),
+                    jnp.concatenate([rh, rm, rh, rl, rh, rm], axis=0),
+                    FIRSTS,
                 )
 
 
@@ -253,20 +264,22 @@
     for filler in fillers:
         filler()
 
-    w_high, w_low = halves(done[:, BOTH:])
-    mixed = mxu(panel, w_high, LASTS) + mxu(panel, w_low, LASTS)
+    mixed = mxu(
+        jnp.concatenate([panel, panel], axis=1), jnp.concatenate(halves(done[:, BOTH:]), axis=1), LASTS
+    )
     y_high, y_low = halves(mixed)
-    cross = mxu(y_high, y_low, LASTS)
-    outer = mxu(y_high, y_high, LASTS) + cross + cross.T
+    outer = mxu(
+        jnp.concatenate([y_high, y_high, y_low], axis=1), jnp.concatenate([y_high, y_low, y_high], axis=1), LASTS
+    )
     ex_rows = lax.broadcasted_iota(jnp.int32, outer.shape, 0)
     ex_cols = lax.broadcasted_iota(jnp.int32, outer.shape, 1)
     mix = (jnp.where(ex_rows == ex_cols, 1.0, 0.0) - outer * (1.0 / total_ex)) * (1.0 / total_ex)
-    both = jnp.concatenate(halves(mix), axis=1)
-    for first in range(0, col_span, BOTH):
-        lanes = slice(first, first + BOTH)
-        cols = g_col[:, lanes]
-        value = mxu(both, jnp.concatenate([cols, cols], axis=0))
-        if first == 0:
+    both = jnp.concatenate(halves(mix), axis=0)
+    chunks = [slice(first, first + BOTH) for first in reversed(range(0, col_span, BOTH))]
+    for lanes in chunks:
+        value = mxu(both, g_col[:, lanes])
+        value = value[:examples] + value[examples:]
+        if lanes.start == 0:
             value = jnp.where(col_at == 0, mixed * (1.0 / total_ex), value)
         weights[:examples, lanes], weights[examples:, lanes] = halves(value)
 
@@ -274,23 +287,25 @@
     eye = lax.broadcasted_iota(jnp.int32, (LANES, LANES), 0) == lax.broadcasted_iota(
         jnp.int32, (LANES, LANES), 1
     )
+    left = jnp.concatenate([turned[...], turned[...]], axis=1)
     copies = []
-    for strip in range(row_blocks):
-        rows = slice(strip * LANES, (strip + 1) * LANES)
-        left = turned[rows, :]
-        held[rows, :] = mxu(jnp.concatenate([left, left], axis=1), weights[...])
-        block = row_at * row_blocks + strip - col_at * col_blocks
-        inside = (block >= 0) & (block < col_blocks)
-        lanes = pl.ds(pl.multiple_of(jnp.clip(block, 0, col_blocks - 1) * LANES, LANES), LANES)
-        held[rows, lanes] += jnp.where(eye & inside, level_ref[:, lanes] * damping, 0.0)
-        if strip * LANES < BOTH:
-
-            @pl.when(row_at == 0)
-            def _(rows=rows):
-                held[rows, :] = jnp.zeros((LANES, col_span), jnp.float32)
-                held[rows, :BOTH] = jnp.where(col_at == 0, lower[rows, :], 0.0)
-
-        copy = pltpu.make_async_copy(held.at[rows, :], out_ref.at[rows, :], sems.at[strip])
+    for n, lanes in enumerate(chunks):
+        value = mxu(left, weights[:, lanes])
+        special = jnp.where(col_at == 0, lower, 0.0) if lanes.start == 0 else jnp.zeros_like(lower)
+        held[:BOTH, lanes] = jnp.where(row_at == 0, special, value[:BOTH])
+        if row_span > BOTH:
+            held[BOTH:, lanes] = value[BOTH:]
+        for b in range(panel_blocks):
+            start = lanes.start + b * LANES
+            block = col_at * col_blocks + start // LANES - row_at * row_blocks
+            inside = (block >= 0) & (block < row_blocks)
+            if lanes.start == 0:
+                inside = inside & (col_at > 0)
+            rows = pl.ds(pl.multiple_of(jnp.clip(block, 0, row_blocks - 1) * LANES, LANES), LANES)
+            held[rows, start : start + LANES] += jnp.where(
+                eye & inside, level_ref[:, start : start + LANES] * damping, 0.0
+            )
+        copy = pltpu.make_async_copy(held.at[:, lanes], out_ref.at[:, lanes], sems.at[n])
         copy.start()
         copies.append(copy)
     for copy in copies:
@@ -315,7 +330,7 @@
             pltpu.VMEM((BOTH, 2 * BOTH), jnp.float32),
             pltpu.VMEM((2 * total_ex, col_span), jnp.bfloat16),
             pltpu.VMEM((row_span, col_span), jnp.float32),
-            pltpu.SemaphoreType.DMA((row_blocks,)),
+            pltpu.SemaphoreType.DMA((col_span // BOTH,)),
         ],
         compiler_params=pltpu.CompilerParams(vmem_limit_bytes=32 * 2**20),
         name="fisher",

time: 37 us -> 36.2 us (0.978)
  Pallas kernels: 14.8 us -> 14 us
    pallas_call x1, Pallas kernels: 9.49 us -> 8.74 us  [fisher(): pl.pallas_call(functools.partial(fisher_kernel, sources=sources, total_ex...]
where the time goes in v5:
time: 36.2 us; the launch traced here: 36.1 us
  Pallas kernels  14 us (39%)
  waiting for transfers between devices  12 us (33%)
  starting transfers between devices  9.74 us (27%)
    ppermute x10, waiting for transfers between devices, swap(): return lax.ppermute(block, axis, [(n, n ^ mask) for n in range(size)])  12 us
    ppermute x10, starting transfers between devices, swap(): return lax.ppermute(block, axis, [(n, n ^ mask) for n in range(size)])  9.74 us
    pallas_call x1, Pallas kernels, fisher(): pl.pallas_call(functools.partial(fisher_kernel, sources=sources, total_ex...  8.74 us
    pallas_call x1, Pallas kernels, project(): pl.pallas_call(functools.partial(project_kernel, local_ex=local_ex, tok_l...  5.27 us
  transfers between devices with their start and end apart: 10, of which 6 were waited for; matrix products, arithmetic and copies ran while one was open for 0% of the time, Pallas kernels for 0%

profile of v5, /device:TPU:0, one launch (start us, length us, event | category | flops | bytes accessed | tf_op | source)
XLA Modules:
  0.0 36.1 jit_solution(16606653937319870220)
XLA Ops:
  0.0 0.0 copy-start
  0.0 5.3 %project.1 = bf16[264,128]{1,0:T(8,128)(2,1)S(1)} custom-call(bf16[256,8192]{1,0:T(8,128)(2,1)} %bitcast.14, bf16[256,8192]{1,0:T(8,128)(2,1)} %bitcast.15, bf16[64,8192]{1,0:T(8,128)(2,1)} %bitcast.16, bf16[64,8192]{1,0:T(8,128)(2,1)} %bitcast.17), custom_call_target="tpu_custom_call" | custom-call | tf_op jit(solution)/shard_map/project/pallas_call | solution.py:104
  5.3 3.1 %collective-permute-start.2 = (bf16[33,8,128]{2,1,0:T(8,128)(2,1)S(1)}, bf16[33,8,128]{2,1,0:T(8,128)(2,1)S(1)}, u32[]{:S(2)}, u32[]{:S(2)}) collective-permute-start(bf16[33,8,128]{2,1,0:T(8,128)(2,1)S(1)} %bitcast.9), channel_id=1, source_target_pairs={{0,1},{1,0},{2,3},{3,2},{4,5},{5,4},{6,7},{7,6},{8,9},{9,8},{10,11... | collective-permute-start | bytes 202760 | tf_op jit(solution)/shard_map/ppermute | solution.py:342
  8.4 2.6 %collective-permute-start.1 = (bf16[33,8,128]{2,1,0:T(8,128)(2,1)S(1)}, bf16[33,8,128]{2,1,0:T(8,128)(2,1)S(1)}, u32[]{:S(2)}, u32[]{:S(2)}) collective-permute-start(bf16[33,8,128]{2,1,0:T(8,128)(2,1)S(1)} %bitcast.10), channel_id=1, source_target_pairs={{0,2},{1,3},{2,0},{3,1},{4,6},{5,7},{6,4},{7,5},{8,10},{9,11},{10,... | collective-permute-start | bytes 202760 | tf_op jit(solution)/shard_map/ppermute | solution.py:342
  11.0 0.0 collective-permute-start
  11.0 0.0 collective-permute-done.2
  11.0 4.8 %collective-permute-done.1 = bf16[33,8,128]{2,1,0:T(8,128)(2,1)S(1)} collective-permute-done((bf16[33,8,128]{2,1,0:T(8,128)(2,1)S(1)}, bf16[33,8,128]{2,1,0:T(8,128)(2,1)S(1)}, u32[]{:S(2)}, u32[]{:S(2)}) %collective-permute-start.1) | collective-permute-done | bytes 67616 | tf_op jit(solution)/shard_map/ppermute | solution.py:342
  15.8 1.4 %collective-permute-done = bf16[33,8,128]{2,1,0:T(8,128)(2,1)S(1)} collective-permute-done((bf16[33,8,128]{2,1,0:T(8,128)(2,1)S(1)}, bf16[33,8,128]{2,1,0:T(8,128)(2,1)S(1)}, u32[]{:S(2)}, u32[]{:S(2)}) %collective-permute-start) | collective-permute-done | bytes 67616 | tf_op jit(solution)/shard_map/ppermute | solution.py:342
  17.3 0.1 pad_maximum_fusion
  17.3 2.5 %collective-permute-start.5 = (bf16[19,32,128]{2,1,0:T(8,128)(2,1)S(1)}, bf16[19,32,128]{2,1,0:T(8,128)(2,1)S(1)}, u32[]{:S(2)}, u32[]{:S(2)}) collective-permute-start(bf16[19,32,128]{2,1,0:T(8,128)(2,1)S(1)} %get-tuple-element.10), channel_id=1, source_target_pairs={{0,24},{4,28},{8,16},{12,20},{16,8},{20,12},{24,0},{28,4},{1,25},{... | collective-permute-start | bytes 466952 | tf_op jit(solution)/shard_map/ppermute | solution.py:342
  19.9 0.5 %collective-permute-start.3 = (bf16[19,32,128]{2,1,0:T(8,128)(2,1)S(1)}, bf16[19,32,128]{2,1,0:T(8,128)(2,1)S(1)}, u32[]{:S(2)}, u32[]{:S(2)}) collective-permute-start(bf16[19,32,128]{2,1,0:T(8,128)(2,1)S(1)} %get-tuple-element.11), channel_id=1, source_target_pairs={{0,8},{4,12},{8,0},{12,4},{16,24},{20,28},{24,16},{28,20},{1,9},{5... | collective-permute-start | bytes 466952 | tf_op jit(solution)/shard_map/ppermute | solution.py:342
  20.4 0.5 %collective-permute-start.4 = (bf16[19,32,128]{2,1,0:T(8,128)(2,1)S(1)}, bf16[19,32,128]{2,1,0:T(8,128)(2,1)S(1)}, u32[]{:S(2)}, u32[]{:S(2)}) collective-permute-start(bf16[19,32,128]{2,1,0:T(8,128)(2,1)S(1)} %get-tuple-element.12), channel_id=1, source_target_pairs={{0,16},{4,20},{8,24},{12,28},{16,0},{20,4},{24,8},{28,12},{1,17},{... | collective-permute-start | bytes 466952 | tf_op jit(solution)/shard_map/ppermute | solution.py:342
  20.9 0.0 collective-permute-start.6
  20.9 3.1 %collective-permute-done.5.refs_3_ = bf16[19,32,128]{2,1,0:T(8,128)(2,1)S(1)} collective-permute-done((bf16[19,32,128]{2,1,0:T(8,128)(2,1)S(1)}, bf16[19,32,128]{2,1,0:T(8,128)(2,1)S(1)}, u32[]{:S(2)}, u32[]{:S(2)}) %collective-permute-start.5) | collective-permute-done | bytes 155680 | tf_op jit(solution)/shard_map/ppermute | solution.py:342
  24.0 0.0 collective-permute-start.9
  24.0 1.7 %collective-permute-done.3.refs_1_ = bf16[19,32,128]{2,1,0:T(8,128)(2,1)S(1)} collective-permute-done((bf16[19,32,128]{2,1,0:T(8,128)(2,1)S(1)}, bf16[19,32,128]{2,1,0:T(8,128)(2,1)S(1)}, u32[]{:S(2)}, u32[]{:S(2)}) %collective-permute-start.3) | collective-permute-done | bytes 155680 | tf_op jit(solution)/shard_map/ppermute | solution.py:342
  25.8 0.0 collective-permute-start.7
  25.8 0.0 collective-permute-done.4.refs_2_
  25.8 0.5 %collective-permute-start.8 = (bf16[19,32,128]{2,1,0:T(8,128)(2,1)S(1)}, bf16[19,32,128]{2,1,0:T(8,128)(2,1)S(1)}, u32[]{:S(2)}, u32[]{:S(2)}) collective-permute-start(bf16[19,32,128]{2,1,0:T(8,128)(2,1)S(1)} %collective-permute-done.4.refs_2_), channel_id=1, source_target_pairs={{0,4},{4,0},{8,12},{12,8},{16,20},{20,16},{24,28},{28,24},{1,5},{5... | collective-permute-start | bytes 466952 | tf_op jit(solution)/shard_map/ppermute | solution.py:342
  26.3 0.0 copy-done
  26.3 0.1 pad_add_fusion.place_ref
  26.4 0.0 collective-permute-done.6.refs_4_
  26.4 0.0 collective-permute-done.9.refs_7_
  26.4 0.8 %collective-permute-done.7.refs_5_ = bf16[19,32,128]{2,1,0:T(8,128)(2,1)S(1)} collective-permute-done((bf16[19,32,128]{2,1,0:T(8,128)(2,1)S(1)}, bf16[19,32,128]{2,1,0:T(8,128)(2,1)S(1)}, u32[]{:S(2)}, u32[]{:S(2)}) %collective-permute-start.7) | collective-permute-done | bytes 155680 | tf_op jit(solution)/shard_map/ppermute | solution.py:342
  27.1 0.2 collective-permute-done.8.refs_6_
  27.4 8.7 %fisher.1 = f32[512,1024]{1,0:T(8,128)} custom-call(s32[2]{0:T(128)S(1)} %pad_add_fusion.place_ref, f32[1,1024]{1,0:T(1,128)S(1)} %bitcast.13, f32[1,256]{1,0:T(1,128)S(1)} %slice.12.panel_level_ref, bf16[19,32,128]{2,1,0:T(8,128)(2,1)S(1)} %get-tuple-element.13.refs_0_, bf16[19,32,128]{2,1,0:T(8,128)(2,1)S(1)} %collective-permute-done.3.refs_1_, ...), custom_call_target="tpu_custom_call" | custom-call | tf_op jit(solution)/shard_map/fisher/pallas_call | solution.py:319
  (7 shorter events, 0.1 us)
Async XLA Ops:
  0.0 26.3 %copy-start = (s32[4096]{0:T(1024)S(1)}, s32[4096]{0:T(1024)}, u32[]{:S(2)}) copy-start(s32[4096]{0:T(1024)} %param.9) | copy-start | bytes 49156
  5.3 5.7 %collective-permute-start.2 = (bf16[33,8,128]{2,1,0:T(8,128)(2,1)S(1)}, bf16[33,8,128]{2,1,0:T(8,128)(2,1)S(1)}, u32[]{:S(2)}, u32[]{:S(2)}) collective-permute-start(bf16[33,8,128]{2,1,0:T(8,128)(2,1)S(1)} %bitcast.9), channel_id=1, source_target_pairs={{0,1},{1,0},{2,3},{3,2},{4,5},{5,4},{6,7},{7,6},{8,9},{9,8},{10,11... | collective-permute-start | bytes 202760 | tf_op jit(solution)/shard_map/ppermute | solution.py:342
  8.4 7.4 %collective-permute-start.1 = (bf16[33,8,128]{2,1,0:T(8,128)(2,1)S(1)}, bf16[33,8,128]{2,1,0:T(8,128)(2,1)S(1)}, u32[]{:S(2)}, u32[]{:S(2)}) collective-permute-start(bf16[33,8,128]{2,1,0:T(8,128)(2,1)S(1)} %bitcast.10), channel_id=1, source_target_pairs={{0,2},{1,3},{2,0},{3,1},{4,6},{5,7},{6,4},{7,5},{8,10},{9,11},{10,... | collective-permute-start | bytes 202760 | tf_op jit(solution)/shard_map/ppermute | solution.py:342
  11.0 6.2 %collective-permute-start = (bf16[33,8,128]{2,1,0:T(8,128)(2,1)S(1)}, bf16[33,8,128]{2,1,0:T(8,128)(2,1)S(1)}, u32[]{:S(2)}, u32[]{:S(2)}) collective-permute-start(bf16[33,8,128]{2,1,0:T(8,128)(2,1)S(1)} %bitcast.11), channel_id=1, source_target_pairs={{0,3},{1,2},{2,1},{3,0},{4,7},{5,6},{6,5},{7,4},{8,11},{9,10},{10,... | collective-permute-start | bytes 202760 | tf_op jit(solution)/shard_map/ppermute | solution.py:342
  17.3 6.7 %collective-permute-start.5 = (bf16[19,32,128]{2,1,0:T(8,128)(2,1)S(1)}, bf16[19,32,128]{2,1,0:T(8,128)(2,1)S(1)}, u32[]{:S(2)}, u32[]{:S(2)}) collective-permute-start(bf16[19,32,128]{2,1,0:T(8,128)(2,1)S(1)} %get-tuple-element.10), channel_id=1, source_target_pairs={{0,24},{4,28},{8,16},{12,20},{16,8},{20,12},{24,0},{28,4},{1,25},{... | collective-permute-start | bytes 466952 | tf_op jit(solution)/shard_map/ppermute | solution.py:342
  19.9 5.9 %collective-permute-start.3 = (bf16[19,32,128]{2,1,0:T(8,128)(2,1)S(1)}, bf16[19,32,128]{2,1,0:T(8,128)(2,1)S(1)}, u32[]{:S(2)}, u32[]{:S(2)}) collective-permute-start(bf16[19,32,128]{2,1,0:T(8,128)(2,1)S(1)} %get-tuple-element.11), channel_id=1, source_target_pairs={{0,8},{4,12},{8,0},{12,4},{16,24},{20,28},{24,16},{28,20},{1,9},{5... | collective-permute-start | bytes 466952 | tf_op jit(solution)/shard_map/ppermute | solution.py:342
  20.4 5.4 %collective-permute-start.4 = (bf16[19,32,128]{2,1,0:T(8,128)(2,1)S(1)}, bf16[19,32,128]{2,1,0:T(8,128)(2,1)S(1)}, u32[]{:S(2)}, u32[]{:S(2)}) collective-permute-start(bf16[19,32,128]{2,1,0:T(8,128)(2,1)S(1)} %get-tuple-element.12), channel_id=1, source_target_pairs={{0,16},{4,20},{8,24},{12,28},{16,0},{20,4},{24,8},{28,12},{1,17},{... | collective-permute-start | bytes 466952 | tf_op jit(solution)/shard_map/ppermute | solution.py:342
  20.9 5.5 %collective-permute-start.6 = (bf16[19,32,128]{2,1,0:T(8,128)(2,1)S(1)}, bf16[19,32,128]{2,1,0:T(8,128)(2,1)S(1)}, u32[]{:S(2)}, u32[]{:S(2)}) collective-permute-start(bf16[19,32,128]{2,1,0:T(8,128)(2,1)S(1)} %get-tuple-element.13.refs_0_), channel_id=1, source_target_pairs={{0,4},{4,0},{8,12},{12,8},{16,20},{20,16},{24,28},{28,24},{1,5},{5... | collective-permute-start | bytes 466952 | tf_op jit(solution)/shard_map/ppermute | solution.py:342
  24.0 2.3 %collective-permute-start.9 = (bf16[19,32,128]{2,1,0:T(8,128)(2,1)S(1)}, bf16[19,32,128]{2,1,0:T(8,128)(2,1)S(1)}, u32[]{:S(2)}, u32[]{:S(2)}) collective-permute-start(bf16[19,32,128]{2,1,0:T(8,128)(2,1)S(1)} %collective-permute-done.5.refs_3_), channel_id=1, source_target_pairs={{0,4},{4,0},{8,12},{12,8},{16,20},{20,16},{24,28},{28,24},{1,5},{5... | collective-permute-start | bytes 466952 | tf_op jit(solution)/shard_map/ppermute | solution.py:342
  25.8 1.4 %collective-permute-start.7 = (bf16[19,32,128]{2,1,0:T(8,128)(2,1)S(1)}, bf16[19,32,128]{2,1,0:T(8,128)(2,1)S(1)}, u32[]{:S(2)}, u32[]{:S(2)}) collective-permute-start(bf16[19,32,128]{2,1,0:T(8,128)(2,1)S(1)} %collective-permute-done.3.refs_1_), channel_id=1, source_target_pairs={{0,4},{4,0},{8,12},{12,8},{16,20},{20,16},{24,28},{28,24},{1,5},{5... | collective-permute-start | bytes 466952 | tf_op jit(solution)/shard_map/ppermute | solution.py:342
  25.8 1.6 %collective-permute-start.8 = (bf16[19,32,128]{2,1,0:T(8,128)(2,1)S(1)}, bf16[19,32,128]{2,1,0:T(8,128)(2,1)S(1)}, u32[]{:S(2)}, u32[]{:S(2)}) collective-permute-start(bf16[19,32,128]{2,1,0:T(8,128)(2,1)S(1)} %collective-permute-done.4.refs_2_), channel_id=1, source_target_pairs={{0,4},{4,0},{8,12},{12,8},{16,20},{20,16},{24,28},{28,24},{1,5},{5... | collective-permute-start | bytes 466952 | tf_op jit(solution)/shard_map/ppermute | solution.py:342

commit v6 on v5

--- a/solution.py
+++ b/solution.py
@@ -359,7 +359,8 @@
     place = jnp.stack([row_at, col_at]).astype(jnp.int32)
 
     packed = project(activations, out_grads, proj_in, proj_out)
-    along = [packed] + [swap(packed, "col", mask) for mask in range(n_cols - 1, 0, -1)]
+    order = [*range(1, min(2, n_cols)), *range(n_cols - 1, 1, -1)]
+    along = [packed] + [swap(packed, "col", mask) for mask in order]
     line = jnp.concatenate(along, axis=1)
 
     common = [

time: 36.2 us -> 35.7 us (0.986)
  waiting for transfers between devices: 12 us -> 11.2 us
    ppermute x10, waiting for transfers between devices: 12 us -> 11.2 us  [swap(): return lax.ppermute(block, axis, [(n, n ^ mask) for n in range(size)])]
  transfers between devices with their start and end apart: 10 -> 10, of which waited for: 6 -> 7; matrix products, arithmetic and copies ran while one was open for 0% -> 0% of each run, Pallas kernels for 0% -> 0%
where the time goes in v6:
time: 35.7 us; the launch traced here: 35.3 us
  Pallas kernels  14 us (39%)
  waiting for transfers between devices  11.2 us (31%)
  starting transfers between devices  9.74 us (27%)
    ppermute x10, waiting for transfers between devices, swap(): return lax.ppermute(block, axis, [(n, n ^ mask) for n in range(size)])  11.2 us
    ppermute x10, starting transfers between devices, swap(): return lax.ppermute(block, axis, [(n, n ^ mask) for n in range(size)])  9.74 us
    pallas_call x1, Pallas kernels, fisher(): pl.pallas_call(functools.partial(fisher_kernel, sources=sources, total_ex...  8.74 us
    pallas_call x1, Pallas kernels, project(): pl.pallas_call(functools.partial(project_kernel, local_ex=local_ex, tok_l...  5.27 us
  transfers between devices with their start and end apart: 10, of which 7 were waited for; matrix products, arithmetic and copies ran while one was open for 0% of the time, Pallas kernels for 0%

profile of v6, /device:TPU:0, one launch (start us, length us, event | category | flops | bytes accessed | tf_op | source)
XLA Modules:
  0.0 35.3 jit_solution(7105319890902697410)
XLA Ops:
  0.0 0.0 copy-start
  0.0 5.3 %project.1 = bf16[264,128]{1,0:T(8,128)(2,1)S(1)} custom-call(bf16[256,8192]{1,0:T(8,128)(2,1)} %bitcast.14, bf16[256,8192]{1,0:T(8,128)(2,1)} %bitcast.15, bf16[64,8192]{1,0:T(8,128)(2,1)} %bitcast.16, bf16[64,8192]{1,0:T(8,128)(2,1)} %bitcast.17), custom_call_target="tpu_custom_call" | custom-call | tf_op jit(solution)/shard_map/project/pallas_call | solution.py:104
  5.3 4.1 %collective-permute-start.2 = (bf16[33,8,128]{2,1,0:T(8,128)(2,1)S(1)}, bf16[33,8,128]{2,1,0:T(8,128)(2,1)S(1)}, u32[]{:S(2)}, u32[]{:S(2)}) collective-permute-start(bf16[33,8,128]{2,1,0:T(8,128)(2,1)S(1)} %bitcast.9), channel_id=1, source_target_pairs={{0,2},{1,3},{2,0},{3,1},{4,6},{5,7},{6,4},{7,5},{8,10},{9,11},{10,... | collective-permute-start | bytes 202760 | tf_op jit(solution)/shard_map/ppermute | solution.py:342
  9.4 1.4 %collective-permute-start.1 = (bf16[33,8,128]{2,1,0:T(8,128)(2,1)S(1)}, bf16[33,8,128]{2,1,0:T(8,128)(2,1)S(1)}, u32[]{:S(2)}, u32[]{:S(2)}) collective-permute-start(bf16[33,8,128]{2,1,0:T(8,128)(2,1)S(1)} %bitcast.10), channel_id=1, source_target_pairs={{0,3},{1,2},{2,1},{3,0},{4,7},{5,6},{6,5},{7,4},{8,11},{9,10},{10,... | collective-permute-start | bytes 202760 | tf_op jit(solution)/shard_map/ppermute | solution.py:342
  10.7 0.2 collective-permute-start
  11.0 2.2 %collective-permute-done.2 = bf16[33,8,128]{2,1,0:T(8,128)(2,1)S(1)} collective-permute-done((bf16[33,8,128]{2,1,0:T(8,128)(2,1)S(1)}, bf16[33,8,128]{2,1,0:T(8,128)(2,1)S(1)}, u32[]{:S(2)}, u32[]{:S(2)}) %collective-permute-start.2) | collective-permute-done | bytes 67616 | tf_op jit(solution)/shard_map/ppermute | solution.py:342
  13.2 2.5 %collective-permute-done.1 = bf16[33,8,128]{2,1,0:T(8,128)(2,1)S(1)} collective-permute-done((bf16[33,8,128]{2,1,0:T(8,128)(2,1)S(1)}, bf16[33,8,128]{2,1,0:T(8,128)(2,1)S(1)}, u32[]{:S(2)}, u32[]{:S(2)}) %collective-permute-start.1) | collective-permute-done | bytes 67616 | tf_op jit(solution)/shard_map/ppermute | solution.py:342
  15.7 0.1 collective-permute-done
  15.9 0.1 pad_maximum_fusion
  15.9 2.6 %collective-permute-start.5 = (bf16[19,32,128]{2,1,0:T(8,128)(2,1)S(1)}, bf16[19,32,128]{2,1,0:T(8,128)(2,1)S(1)}, u32[]{:S(2)}, u32[]{:S(2)}) collective-permute-start(bf16[19,32,128]{2,1,0:T(8,128)(2,1)S(1)} %get-tuple-element.10), channel_id=1, source_target_pairs={{0,24},{4,28},{8,16},{12,20},{16,8},{20,12},{24,0},{28,4},{1,25},{... | collective-permute-start | bytes 466952 | tf_op jit(solution)/shard_map/ppermute | solution.py:342
  18.5 0.5 %collective-permute-start.3 = (bf16[19,32,128]{2,1,0:T(8,128)(2,1)S(1)}, bf16[19,32,128]{2,1,0:T(8,128)(2,1)S(1)}, u32[]{:S(2)}, u32[]{:S(2)}) collective-permute-start(bf16[19,32,128]{2,1,0:T(8,128)(2,1)S(1)} %get-tuple-element.11), channel_id=1, source_target_pairs={{0,8},{4,12},{8,0},{12,4},{16,24},{20,28},{24,16},{28,20},{1,9},{5... | collective-permute-start | bytes 466952 | tf_op jit(solution)/shard_map/ppermute | solution.py:342
  19.1 0.4 %collective-permute-start.4 = (bf16[19,32,128]{2,1,0:T(8,128)(2,1)S(1)}, bf16[19,32,128]{2,1,0:T(8,128)(2,1)S(1)}, u32[]{:S(2)}, u32[]{:S(2)}) collective-permute-start(bf16[19,32,128]{2,1,0:T(8,128)(2,1)S(1)} %get-tuple-element.12), channel_id=1, source_target_pairs={{0,16},{4,20},{8,24},{12,28},{16,0},{20,4},{24,8},{28,12},{1,17},{... | collective-permute-start | bytes 466952 | tf_op jit(solution)/shard_map/ppermute | solution.py:342
  19.5 0.0 collective-permute-start.6
  19.5 3.7 %collective-permute-done.5.refs_3_ = bf16[19,32,128]{2,1,0:T(8,128)(2,1)S(1)} collective-permute-done((bf16[19,32,128]{2,1,0:T(8,128)(2,1)S(1)}, bf16[19,32,128]{2,1,0:T(8,128)(2,1)S(1)}, u32[]{:S(2)}, u32[]{:S(2)}) %collective-permute-start.5) | collective-permute-done | bytes 155680 | tf_op jit(solution)/shard_map/ppermute | solution.py:342
  23.2 0.0 collective-permute-start.9
  23.2 1.8 %collective-permute-done.3.refs_1_ = bf16[19,32,128]{2,1,0:T(8,128)(2,1)S(1)} collective-permute-done((bf16[19,32,128]{2,1,0:T(8,128)(2,1)S(1)}, bf16[19,32,128]{2,1,0:T(8,128)(2,1)S(1)}, u32[]{:S(2)}, u32[]{:S(2)}) %collective-permute-start.3) | collective-permute-done | bytes 155680 | tf_op jit(solution)/shard_map/ppermute | solution.py:342
  25.0 0.0 collective-permute-start.7
  25.0 0.0 collective-permute-done.4.refs_2_
  25.0 0.5 %collective-permute-start.8 = (bf16[19,32,128]{2,1,0:T(8,128)(2,1)S(1)}, bf16[19,32,128]{2,1,0:T(8,128)(2,1)S(1)}, u32[]{:S(2)}, u32[]{:S(2)}) collective-permute-start(bf16[19,32,128]{2,1,0:T(8,128)(2,1)S(1)} %collective-permute-done.4.refs_2_), channel_id=1, source_target_pairs={{0,4},{4,0},{8,12},{12,8},{16,20},{20,16},{24,28},{28,24},{1,5},{5... | collective-permute-start | bytes 466952 | tf_op jit(solution)/shard_map/ppermute | solution.py:342
  25.5 0.0 copy-done
  25.5 0.1 pad_add_fusion.place_ref
  25.6 0.0 collective-permute-done.6.refs_4_
  25.6 0.0 collective-permute-done.9.refs_7_
  25.6 0.8 %collective-permute-done.7.refs_5_ = bf16[19,32,128]{2,1,0:T(8,128)(2,1)S(1)} collective-permute-done((bf16[19,32,128]{2,1,0:T(8,128)(2,1)S(1)}, bf16[19,32,128]{2,1,0:T(8,128)(2,1)S(1)}, u32[]{:S(2)}, u32[]{:S(2)}) %collective-permute-start.7) | collective-permute-done | bytes 155680 | tf_op jit(solution)/shard_map/ppermute | solution.py:342
  26.4 0.2 collective-permute-done.8.refs_6_
  26.6 8.7 %fisher.1 = f32[512,1024]{1,0:T(8,128)} custom-call(s32[2]{0:T(128)S(1)} %pad_add_fusion.place_ref, f32[1,1024]{1,0:T(1,128)S(1)} %bitcast.13, f32[1,256]{1,0:T(1,128)S(1)} %slice.12.panel_level_ref, bf16[19,32,128]{2,1,0:T(8,128)(2,1)S(1)} %get-tuple-element.13.refs_0_, bf16[19,32,128]{2,1,0:T(8,128)(2,1)S(1)} %collective-permute-done.3.refs_1_, ...), custom_call_target="tpu_custom_call" | custom-call | tf_op jit(solution)/shard_map/fisher/pallas_call | solution.py:319
  (7 shorter events, 0.1 us)
Async XLA Ops:
  0.0 25.5 %copy-start = (s32[4096]{0:T(1024)S(1)}, s32[4096]{0:T(1024)}, u32[]{:S(2)}) copy-start(s32[4096]{0:T(1024)} %param.9) | copy-start | bytes 49156
  5.3 7.9 %collective-permute-start.2 = (bf16[33,8,128]{2,1,0:T(8,128)(2,1)S(1)}, bf16[33,8,128]{2,1,0:T(8,128)(2,1)S(1)}, u32[]{:S(2)}, u32[]{:S(2)}) collective-permute-start(bf16[33,8,128]{2,1,0:T(8,128)(2,1)S(1)} %bitcast.9), channel_id=1, source_target_pairs={{0,2},{1,3},{2,0},{3,1},{4,6},{5,7},{6,4},{7,5},{8,10},{9,11},{10,... | collective-permute-start | bytes 202760 | tf_op jit(solution)/shard_map/ppermute | solution.py:342
  9.4 6.3 %collective-permute-start.1 = (bf16[33,8,128]{2,1,0:T(8,128)(2,1)S(1)}, bf16[33,8,128]{2,1,0:T(8,128)(2,1)S(1)}, u32[]{:S(2)}, u32[]{:S(2)}) collective-permute-start(bf16[33,8,128]{2,1,0:T(8,128)(2,1)S(1)} %bitcast.10), channel_id=1, source_target_pairs={{0,3},{1,2},{2,1},{3,0},{4,7},{5,6},{6,5},{7,4},{8,11},{9,10},{10,... | collective-permute-start | bytes 202760 | tf_op jit(solution)/shard_map/ppermute | solution.py:342
  10.7 5.0 %collective-permute-start = (bf16[33,8,128]{2,1,0:T(8,128)(2,1)S(1)}, bf16[33,8,128]{2,1,0:T(8,128)(2,1)S(1)}, u32[]{:S(2)}, u32[]{:S(2)}) collective-permute-start(bf16[33,8,128]{2,1,0:T(8,128)(2,1)S(1)} %bitcast.11), channel_id=1, source_target_pairs={{0,1},{1,0},{2,3},{3,2},{4,5},{5,4},{6,7},{7,6},{8,9},{9,8},{10,11... | collective-permute-start | bytes 202760 | tf_op jit(solution)/shard_map/ppermute | solution.py:342
  15.9 7.2 %collective-permute-start.5 = (bf16[19,32,128]{2,1,0:T(8,128)(2,1)S(1)}, bf16[19,32,128]{2,1,0:T(8,128)(2,1)S(1)}, u32[]{:S(2)}, u32[]{:S(2)}) collective-permute-start(bf16[19,32,128]{2,1,0:T(8,128)(2,1)S(1)} %get-tuple-element.10), channel_id=1, source_target_pairs={{0,24},{4,28},{8,16},{12,20},{16,8},{20,12},{24,0},{28,4},{1,25},{... | collective-permute-start | bytes 466952 | tf_op jit(solution)/shard_map/ppermute | solution.py:342
  18.5 6.4 %collective-permute-start.3 = (bf16[19,32,128]{2,1,0:T(8,128)(2,1)S(1)}, bf16[19,32,128]{2,1,0:T(8,128)(2,1)S(1)}, u32[]{:S(2)}, u32[]{:S(2)}) collective-permute-start(bf16[19,32,128]{2,1,0:T(8,128)(2,1)S(1)} %get-tuple-element.11), channel_id=1, source_target_pairs={{0,8},{4,12},{8,0},{12,4},{16,24},{20,28},{24,16},{28,20},{1,9},{5... | collective-permute-start | bytes 466952 | tf_op jit(solution)/shard_map/ppermute | solution.py:342
  19.1 5.9 %collective-permute-start.4 = (bf16[19,32,128]{2,1,0:T(8,128)(2,1)S(1)}, bf16[19,32,128]{2,1,0:T(8,128)(2,1)S(1)}, u32[]{:S(2)}, u32[]{:S(2)}) collective-permute-start(bf16[19,32,128]{2,1,0:T(8,128)(2,1)S(1)} %get-tuple-element.12), channel_id=1, source_target_pairs={{0,16},{4,20},{8,24},{12,28},{16,0},{20,4},{24,8},{28,12},{1,17},{... | collective-permute-start | bytes 466952 | tf_op jit(solution)/shard_map/ppermute | solution.py:342
  19.5 6.1 %collective-permute-start.6 = (bf16[19,32,128]{2,1,0:T(8,128)(2,1)S(1)}, bf16[19,32,128]{2,1,0:T(8,128)(2,1)S(1)}, u32[]{:S(2)}, u32[]{:S(2)}) collective-permute-start(bf16[19,32,128]{2,1,0:T(8,128)(2,1)S(1)} %get-tuple-element.13.refs_0_), channel_id=1, source_target_pairs={{0,4},{4,0},{8,12},{12,8},{16,20},{20,16},{24,28},{28,24},{1,5},{5... | collective-permute-start | bytes 466952 | tf_op jit(solution)/shard_map/ppermute | solution.py:342
  23.2 2.4 %collective-permute-start.9 = (bf16[19,32,128]{2,1,0:T(8,128)(2,1)S(1)}, bf16[19,32,128]{2,1,0:T(8,128)(2,1)S(1)}, u32[]{:S(2)}, u32[]{:S(2)}) collective-permute-start(bf16[19,32,128]{2,1,0:T(8,128)(2,1)S(1)} %collective-permute-done.5.refs_3_), channel_id=1, source_target_pairs={{0,4},{4,0},{8,12},{12,8},{16,20},{20,16},{24,28},{28,24},{1,5},{5... | collective-permute-start | bytes 466952 | tf_op jit(solution)/shard_map/ppermute | solution.py:342
  25.0 1.4 %collective-permute-start.7 = (bf16[19,32,128]{2,1,0:T(8,128)(2,1)S(1)}, bf16[19,32,128]{2,1,0:T(8,128)(2,1)S(1)}, u32[]{:S(2)}, u32[]{:S(2)}) collective-permute-start(bf16[19,32,128]{2,1,0:T(8,128)(2,1)S(1)} %collective-permute-done.3.refs_1_), channel_id=1, source_target_pairs={{0,4},{4,0},{8,12},{12,8},{16,20},{20,16},{24,28},{28,24},{1,5},{5... | collective-permute-start | bytes 466952 | tf_op jit(solution)/shard_map/ppermute | solution.py:342
  25.0 1.6 %collective-permute-start.8 = (bf16[19,32,128]{2,1,0:T(8,128)(2,1)S(1)}, bf16[19,32,128]{2,1,0:T(8,128)(2,1)S(1)}, u32[]{:S(2)}, u32[]{:S(2)}) collective-permute-start(bf16[19,32,128]{2,1,0:T(8,128)(2,1)S(1)} %collective-permute-done.4.refs_2_), channel_id=1, source_target_pairs={{0,4},{4,0},{8,12},{12,8},{16,20},{20,16},{24,28},{28,24},{1,5},{5... | collective-permute-start | bytes 466952 | tf_op jit(solution)/shard_map/ppermute | solution.py:342

commit v7 on v5

--- a/solution.py
+++ b/solution.py
@@ -342,6 +342,15 @@
     return lax.ppermute(block, axis, [(n, n ^ mask) for n in range(size)])
 
 
+def shift(block, axis, hops):
+    size = lax.axis_size(axis)
+    return lax.ppermute(block, axis, [(n, (n + hops) % size) for n in range(size)])
+
+
+def last_first(count):
+    return [*range(1, count)][-1:] + [*range(1, count)][:-1]
+
+
 def shards(activations, out_grads, proj_in, proj_out, damp_level):
     local_ex = activations.shape[0]
     feats = proj_in.shape[1] * proj_out.shape[1]
@@ -359,7 +368,7 @@
     place = jnp.stack([row_at, col_at]).astype(jnp.int32)
 
     packed = project(activations, out_grads, proj_in, proj_out)
-    along = [packed] + [swap(packed, "col", mask) for mask in range(n_cols - 1, 0, -1)]
+    along = [packed] + [shift(packed, "col", hops) for hops in last_first(n_cols)]
     line = jnp.concatenate(along, axis=1)
 
     common = [
@@ -374,7 +383,7 @@
         wanted = lax.dynamic_slice_in_dim(line, pair * 2 * row_blocks, 2 * row_blocks)
         return jnp.concatenate([wanted] + common)
 
-    got = [bundle(pair_at)] + [swap(bundle(pair_at ^ mask), "row", 2 * mask) for mask in range(1, pairs)]
+    got = [bundle(pair_at)] + [swap(bundle(pair_at ^ mask), "row", 2 * mask) for mask in last_first(pairs)]
     arrived = got + [swap(piece, "row", 1) for piece in got]
     return fisher(
         place, col_levels, levels[:, :BOTH], arrived, row_blocks, col_blocks, total_ex, feats

time: 36.2 us -> 35.3 us (0.975)
  waiting for transfers between devices: 12 us -> 9.35 us
  starting transfers between devices: 9.74 us -> 11.5 us
    ppermute x0 -> x3, starting transfers between devices: none -> 7.92 us  [shift(): lax.ppermute(block, axis, [(n, (n + hops) % size) for n in range(size)])]
    ppermute x10 -> x7, starting transfers between devices: 9.74 us -> 3.56 us  [swap(): return lax.ppermute(block, axis, [(n, n ^ mask) for n in range(size)])]
    ppermute x10 -> x7, waiting for transfers between devices: 12 us -> 6.59 us  [swap(): return lax.ppermute(block, axis, [(n, n ^ mask) for n in range(size)])]
    ppermute x0 -> x3, waiting for transfers between devices: none -> 2.76 us  [shift(): lax.ppermute(block, axis, [(n, (n + hops) % size) for n in range(size)])]
  transfers between devices with their start and end apart: 10 -> 10, of which waited for: 6 -> 7; matrix products, arithmetic and copies ran while one was open for 0% -> 0% of each run, Pallas kernels for 0% -> 0%
where the time goes in v7:
time: 35.3 us; the launch traced here: 35.2 us
  Pallas kernels  14 us (40%)
  starting transfers between devices  11.5 us (33%)
  waiting for transfers between devices  9.35 us (26%)
    pallas_call x1, Pallas kernels, fisher(): pl.pallas_call(functools.partial(fisher_kernel, sources=sources, total_ex...  8.74 us
    ppermute x3, starting transfers between devices, shift(): lax.ppermute(block, axis, [(n, (n + hops) % size) for n in range(size)])  7.92 us
    ppermute x7, waiting for transfers between devices, swap(): return lax.ppermute(block, axis, [(n, n ^ mask) for n in range(size)])  6.59 us
    pallas_call x1, Pallas kernels, project(): pl.pallas_call(functools.partial(project_kernel, local_ex=local_ex, tok_l...  5.27 us
    ppermute x7, starting transfers between devices, swap(): return lax.ppermute(block, axis, [(n, n ^ mask) for n in range(size)])  3.56 us
    ppermute x3, waiting for transfers between devices, shift(): lax.ppermute(block, axis, [(n, (n + hops) % size) for n in range(size)])  2.76 us
  transfers between devices with their start and end apart: 10, of which 7 were waited for; matrix products, arithmetic and copies ran while one was open for 0% of the time, Pallas kernels for 0%

profile of v7, /device:TPU:0, one launch (start us, length us, event | category | flops | bytes accessed | tf_op | source)
XLA Modules:
  0.0 35.2 jit_solution(10923620903188766870)
XLA Ops:
  0.0 0.0 copy-start
  0.0 5.3 %project.1 = bf16[264,128]{1,0:T(8,128)(2,1)S(1)} custom-call(bf16[256,8192]{1,0:T(8,128)(2,1)} %bitcast.14, bf16[256,8192]{1,0:T(8,128)(2,1)} %bitcast.15, bf16[64,8192]{1,0:T(8,128)(2,1)} %bitcast.16, bf16[64,8192]{1,0:T(8,128)(2,1)} %bitcast.17), custom_call_target="tpu_custom_call" | custom-call | tf_op jit(solution)/shard_map/project/pallas_call | solution.py:104
  5.3 4.1 %collective-permute-start.2 = (bf16[33,8,128]{2,1,0:T(8,128)(2,1)S(1)}, bf16[33,8,128]{2,1,0:T(8,128)(2,1)S(1)}, u32[]{:S(2)}, u32[]{:S(2)}) collective-permute-start(bf16[33,8,128]{2,1,0:T(8,128)(2,1)S(1)} %bitcast.9), channel_id=1, source_target_pairs={{0,2},{1,3},{2,0},{3,1},{4,6},{5,7},{6,4},{7,5},{8,10},{9,11},{10,... | collective-permute-start | bytes 202760 | tf_op jit(solution)/shard_map/ppermute | solution.py:347
  9.4 1.6 %collective-permute-start.1 = (bf16[33,8,128]{2,1,0:T(8,128)(2,1)S(1)}, bf16[33,8,128]{2,1,0:T(8,128)(2,1)S(1)}, u32[]{:S(2)}, u32[]{:S(2)}) collective-permute-start(bf16[33,8,128]{2,1,0:T(8,128)(2,1)S(1)} %bitcast.10), channel_id=1, source_target_pairs={{0,1},{1,2},{2,3},{3,0},{4,5},{5,6},{6,7},{7,4},{8,9},{9,10},{10,1... | collective-permute-start | bytes 202760 | tf_op jit(solution)/shard_map/ppermute | solution.py:347
  11.0 2.2 %collective-permute-start = (bf16[33,8,128]{2,1,0:T(8,128)(2,1)S(1)}, bf16[33,8,128]{2,1,0:T(8,128)(2,1)S(1)}, u32[]{:S(2)}, u32[]{:S(2)}) collective-permute-start(bf16[33,8,128]{2,1,0:T(8,128)(2,1)S(1)} %bitcast.11), channel_id=1, source_target_pairs={{0,3},{1,0},{2,1},{3,2},{4,7},{5,4},{6,5},{7,6},{8,11},{9,8},{10,9... | collective-permute-start | bytes 202760 | tf_op jit(solution)/shard_map/ppermute | solution.py:347
  13.2 0.0 collective-permute-done.2
  13.2 2.5 %collective-permute-done.1 = bf16[33,8,128]{2,1,0:T(8,128)(2,1)S(1)} collective-permute-done((bf16[33,8,128]{2,1,0:T(8,128)(2,1)S(1)}, bf16[33,8,128]{2,1,0:T(8,128)(2,1)S(1)}, u32[]{:S(2)}, u32[]{:S(2)}) %collective-permute-start.1) | collective-permute-done | bytes 67616 | tf_op jit(solution)/shard_map/ppermute | solution.py:347
  15.7 0.3 collective-permute-done
  16.1 0.1 pad_maximum_fusion
  16.2 1.6 %collective-permute-start.5 = (bf16[19,32,128]{2,1,0:T(8,128)(2,1)S(1)}, bf16[19,32,128]{2,1,0:T(8,128)(2,1)S(1)}, u32[]{:S(2)}, u32[]{:S(2)}) collective-permute-start(bf16[19,32,128]{2,1,0:T(8,128)(2,1)S(1)} %get-tuple-element.10), channel_id=1, source_target_pairs={{0,16},{4,20},{8,24},{12,28},{16,0},{20,4},{24,8},{28,12},{1,17},{... | collective-permute-start | bytes 466952 | tf_op jit(solution)/shard_map/ppermute | solution.py:342
  17.8 1.4 %collective-permute-start.3 = (bf16[19,32,128]{2,1,0:T(8,128)(2,1)S(1)}, bf16[19,32,128]{2,1,0:T(8,128)(2,1)S(1)}, u32[]{:S(2)}, u32[]{:S(2)}) collective-permute-start(bf16[19,32,128]{2,1,0:T(8,128)(2,1)S(1)} %get-tuple-element.11), channel_id=1, source_target_pairs={{0,24},{4,28},{8,16},{12,20},{16,8},{20,12},{24,0},{28,4},{1,25},{... | collective-permute-start | bytes 466952 | tf_op jit(solution)/shard_map/ppermute | solution.py:342
  19.3 0.5 %collective-permute-start.4 = (bf16[19,32,128]{2,1,0:T(8,128)(2,1)S(1)}, bf16[19,32,128]{2,1,0:T(8,128)(2,1)S(1)}, u32[]{:S(2)}, u32[]{:S(2)}) collective-permute-start(bf16[19,32,128]{2,1,0:T(8,128)(2,1)S(1)} %get-tuple-element.12), channel_id=1, source_target_pairs={{0,8},{4,12},{8,0},{12,4},{16,24},{20,28},{24,16},{28,20},{1,9},{5... | collective-permute-start | bytes 466952 | tf_op jit(solution)/shard_map/ppermute | solution.py:342
  19.7 0.0 collective-permute-start.6
  19.7 3.4 %collective-permute-done.5.refs_3_ = bf16[19,32,128]{2,1,0:T(8,128)(2,1)S(1)} collective-permute-done((bf16[19,32,128]{2,1,0:T(8,128)(2,1)S(1)}, bf16[19,32,128]{2,1,0:T(8,128)(2,1)S(1)}, u32[]{:S(2)}, u32[]{:S(2)}) %collective-permute-start.5) | collective-permute-done | bytes 155680 | tf_op jit(solution)/shard_map/ppermute | solution.py:342
  23.1 0.0 collective-permute-start.9
  23.1 1.3 %collective-permute-done.3.refs_1_ = bf16[19,32,128]{2,1,0:T(8,128)(2,1)S(1)} collective-permute-done((bf16[19,32,128]{2,1,0:T(8,128)(2,1)S(1)}, bf16[19,32,128]{2,1,0:T(8,128)(2,1)S(1)}, u32[]{:S(2)}, u32[]{:S(2)}) %collective-permute-start.3) | collective-permute-done | bytes 155680 | tf_op jit(solution)/shard_map/ppermute | solution.py:342
  24.4 0.0 collective-permute-start.7
  24.4 0.7 %collective-permute-done.4.refs_2_ = bf16[19,32,128]{2,1,0:T(8,128)(2,1)S(1)} collective-permute-done((bf16[19,32,128]{2,1,0:T(8,128)(2,1)S(1)}, bf16[19,32,128]{2,1,0:T(8,128)(2,1)S(1)}, u32[]{:S(2)}, u32[]{:S(2)}) %collective-permute-start.4) | collective-permute-done | bytes 155680 | tf_op jit(solution)/shard_map/ppermute | solution.py:342
  25.1 0.0 collective-permute-start.8
  25.1 0.0 copy-done
  25.1 0.1 pad_add_fusion.place_ref
  25.2 0.0 collective-permute-done.6.refs_4_
  25.2 0.0 collective-permute-done.9.refs_7_
  25.2 0.6 %collective-permute-done.7.refs_5_ = bf16[19,32,128]{2,1,0:T(8,128)(2,1)S(1)} collective-permute-done((bf16[19,32,128]{2,1,0:T(8,128)(2,1)S(1)}, bf16[19,32,128]{2,1,0:T(8,128)(2,1)S(1)}, u32[]{:S(2)}, u32[]{:S(2)}) %collective-permute-start.7) | collective-permute-done | bytes 155680 | tf_op jit(solution)/shard_map/ppermute | solution.py:342
  25.8 0.7 %collective-permute-done.8.refs_6_ = bf16[19,32,128]{2,1,0:T(8,128)(2,1)S(1)} collective-permute-done((bf16[19,32,128]{2,1,0:T(8,128)(2,1)S(1)}, bf16[19,32,128]{2,1,0:T(8,128)(2,1)S(1)}, u32[]{:S(2)}, u32[]{:S(2)}) %collective-permute-start.8) | collective-permute-done | bytes 155680 | tf_op jit(solution)/shard_map/ppermute | solution.py:342
  26.4 8.7 %fisher.1 = f32[512,1024]{1,0:T(8,128)} custom-call(s32[2]{0:T(128)S(1)} %pad_add_fusion.place_ref, f32[1,1024]{1,0:T(1,128)S(1)} %bitcast.13, f32[1,256]{1,0:T(1,128)S(1)} %slice.12.panel_level_ref, bf16[19,32,128]{2,1,0:T(8,128)(2,1)S(1)} %get-tuple-element.13.refs_0_, bf16[19,32,128]{2,1,0:T(8,128)(2,1)S(1)} %collective-permute-done.3.refs_1_, ...), custom_call_target="tpu_custom_call" | custom-call | tf_op jit(solution)/shard_map/fisher/pallas_call | solution.py:319
  (7 shorter events, 0.1 us)
Async XLA Ops:
  0.0 25.1 %copy-start = (s32[4096]{0:T(1024)S(1)}, s32[4096]{0:T(1024)}, u32[]{:S(2)}) copy-start(s32[4096]{0:T(1024)} %param.9) | copy-start | bytes 49156
  5.3 7.9 %collective-permute-start.2 = (bf16[33,8,128]{2,1,0:T(8,128)(2,1)S(1)}, bf16[33,8,128]{2,1,0:T(8,128)(2,1)S(1)}, u32[]{:S(2)}, u32[]{:S(2)}) collective-permute-start(bf16[33,8,128]{2,1,0:T(8,128)(2,1)S(1)} %bitcast.9), channel_id=1, source_target_pairs={{0,2},{1,3},{2,0},{3,1},{4,6},{5,7},{6,4},{7,5},{8,10},{9,11},{10,... | collective-permute-start | bytes 202760 | tf_op jit(solution)/shard_map/ppermute | solution.py:347
  9.4 6.3 %collective-permute-start.1 = (bf16[33,8,128]{2,1,0:T(8,128)(2,1)S(1)}, bf16[33,8,128]{2,1,0:T(8,128)(2,1)S(1)}, u32[]{:S(2)}, u32[]{:S(2)}) collective-permute-start(bf16[33,8,128]{2,1,0:T(8,128)(2,1)S(1)} %bitcast.10), channel_id=1, source_target_pairs={{0,1},{1,2},{2,3},{3,0},{4,5},{5,6},{6,7},{7,4},{8,9},{9,10},{10,1... | collective-permute-start | bytes 202760 | tf_op jit(solution)/shard_map/ppermute | solution.py:347
  11.0 5.0 %collective-permute-start = (bf16[33,8,128]{2,1,0:T(8,128)(2,1)S(1)}, bf16[33,8,128]{2,1,0:T(8,128)(2,1)S(1)}, u32[]{:S(2)}, u32[]{:S(2)}) collective-permute-start(bf16[33,8,128]{2,1,0:T(8,128)(2,1)S(1)} %bitcast.11), channel_id=1, source_target_pairs={{0,3},{1,0},{2,1},{3,2},{4,7},{5,4},{6,5},{7,6},{8,11},{9,8},{10,9... | collective-permute-start | bytes 202760 | tf_op jit(solution)/shard_map/ppermute | solution.py:347
  16.2 7.0 %collective-permute-start.5 = (bf16[19,32,128]{2,1,0:T(8,128)(2,1)S(1)}, bf16[19,32,128]{2,1,0:T(8,128)(2,1)S(1)}, u32[]{:S(2)}, u32[]{:S(2)}) collective-permute-start(bf16[19,32,128]{2,1,0:T(8,128)(2,1)S(1)} %get-tuple-element.10), channel_id=1, source_target_pairs={{0,16},{4,20},{8,24},{12,28},{16,0},{20,4},{24,8},{28,12},{1,17},{... | collective-permute-start | bytes 466952 | tf_op jit(solution)/shard_map/ppermute | solution.py:342
  17.8 6.6 %collective-permute-start.3 = (bf16[19,32,128]{2,1,0:T(8,128)(2,1)S(1)}, bf16[19,32,128]{2,1,0:T(8,128)(2,1)S(1)}, u32[]{:S(2)}, u32[]{:S(2)}) collective-permute-start(bf16[19,32,128]{2,1,0:T(8,128)(2,1)S(1)} %get-tuple-element.11), channel_id=1, source_target_pairs={{0,24},{4,28},{8,16},{12,20},{16,8},{20,12},{24,0},{28,4},{1,25},{... | collective-permute-start | bytes 466952 | tf_op jit(solution)/shard_map/ppermute | solution.py:342
  19.3 5.8 %collective-permute-start.4 = (bf16[19,32,128]{2,1,0:T(8,128)(2,1)S(1)}, bf16[19,32,128]{2,1,0:T(8,128)(2,1)S(1)}, u32[]{:S(2)}, u32[]{:S(2)}) collective-permute-start(bf16[19,32,128]{2,1,0:T(8,128)(2,1)S(1)} %get-tuple-element.12), channel_id=1, source_target_pairs={{0,8},{4,12},{8,0},{12,4},{16,24},{20,28},{24,16},{28,20},{1,9},{5... | collective-permute-start | bytes 466952 | tf_op jit(solution)/shard_map/ppermute | solution.py:342
  19.7 5.5 %collective-permute-start.6 = (bf16[19,32,128]{2,1,0:T(8,128)(2,1)S(1)}, bf16[19,32,128]{2,1,0:T(8,128)(2,1)S(1)}, u32[]{:S(2)}, u32[]{:S(2)}) collective-permute-start(bf16[19,32,128]{2,1,0:T(8,128)(2,1)S(1)} %get-tuple-element.13.refs_0_), channel_id=1, source_target_pairs={{0,4},{4,0},{8,12},{12,8},{16,20},{20,16},{24,28},{28,24},{1,5},{5... | collective-permute-start | bytes 466952 | tf_op jit(solution)/shard_map/ppermute | solution.py:342
  23.1 2.0 %collective-permute-start.9 = (bf16[19,32,128]{2,1,0:T(8,128)(2,1)S(1)}, bf16[19,32,128]{2,1,0:T(8,128)(2,1)S(1)}, u32[]{:S(2)}, u32[]{:S(2)}) collective-permute-start(bf16[19,32,128]{2,1,0:T(8,128)(2,1)S(1)} %collective-permute-done.5.refs_3_), channel_id=1, source_target_pairs={{0,4},{4,0},{8,12},{12,8},{16,20},{20,16},{24,28},{28,24},{1,5},{5... | collective-permute-start | bytes 466952 | tf_op jit(solution)/shard_map/ppermute | solution.py:342
  24.4 1.4 %collective-permute-start.7 = (bf16[19,32,128]{2,1,0:T(8,128)(2,1)S(1)}, bf16[19,32,128]{2,1,0:T(8,128)(2,1)S(1)}, u32[]{:S(2)}, u32[]{:S(2)}) collective-permute-start(bf16[19,32,128]{2,1,0:T(8,128)(2,1)S(1)} %collective-permute-done.3.refs_1_), channel_id=1, source_target_pairs={{0,4},{4,0},{8,12},{12,8},{16,20},{20,16},{24,28},{28,24},{1,5},{5... | collective-permute-start | bytes 466952 | tf_op jit(solution)/shard_map/ppermute | solution.py:342
  25.1 1.4 %collective-permute-start.8 = (bf16[19,32,128]{2,1,0:T(8,128)(2,1)S(1)}, bf16[19,32,128]{2,1,0:T(8,128)(2,1)S(1)}, u32[]{:S(2)}, u32[]{:S(2)}) collective-permute-start(bf16[19,32,128]{2,1,0:T(8,128)(2,1)S(1)} %collective-permute-done.4.refs_2_), channel_id=1, source_target_pairs={{0,4},{4,0},{8,12},{12,8},{16,20},{20,16},{24,28},{28,24},{1,5},{5... | collective-permute-start | bytes 466952 | tf_op jit(solution)/shard_map/ppermute | solution.py:342

commit v8 on v7

--- a/solution.py
+++ b/solution.py
@@ -155,7 +155,7 @@
 
         cols = spread(0, 0, groups)
         for block in range(groups):
-            near = min(block + 1 + AHEAD, groups)
+            near = min(block + 1 + (AHEAD if block < groups // 2 else 3), groups)
             ahead = spread(block + 1, block + 1, near) if block + 1 < groups else None
             pivots = jnp.ones((SUB, LANES), jnp.float32)
             inverses = []

time: 35.3 us -> 35.3 us (level)
  no operation moved by 1% of the time
where the time goes in v8:
time: 35.3 us; the launch traced here: 35.2 us
  Pallas kernels  14 us (40%)
  starting transfers between devices  11.5 us (33%)
  waiting for transfers between devices  9.35 us (26%)
    pallas_call x1, Pallas kernels, fisher(): pl.pallas_call(functools.partial(fisher_kernel, sources=sources, total_ex...  8.74 us
    ppermute x3, starting transfers between devices, shift(): lax.ppermute(block, axis, [(n, (n + hops) % size) for n in range(size)])  7.92 us
    ppermute x7, waiting for transfers between devices, swap(): return lax.ppermute(block, axis, [(n, n ^ mask) for n in range(size)])  6.59 us
    pallas_call x1, Pallas kernels, project(): pl.pallas_call(functools.partial(project_kernel, local_ex=local_ex, tok_l...  5.27 us
    ppermute x7, starting transfers between devices, swap(): return lax.ppermute(block, axis, [(n, n ^ mask) for n in range(size)])  3.56 us
    ppermute x3, waiting for transfers between devices, shift(): lax.ppermute(block, axis, [(n, (n + hops) % size) for n in range(size)])  2.76 us
  transfers between devices with their start and end apart: 10, of which 7 were waited for; matrix products, arithmetic and copies ran while one was open for 0% of the time, Pallas kernels for 0%

profile of v8, /device:TPU:0, one launch (start us, length us, event | category | flops | bytes accessed | tf_op | source)
XLA Modules:
  0.0 35.2 jit_solution(11996162767653966483)
XLA Ops:
  0.0 0.0 copy-start
  0.0 5.3 %project.1 = bf16[264,128]{1,0:T(8,128)(2,1)S(1)} custom-call(bf16[256,8192]{1,0:T(8,128)(2,1)} %bitcast.14, bf16[256,8192]{1,0:T(8,128)(2,1)} %bitcast.15, bf16[64,8192]{1,0:T(8,128)(2,1)} %bitcast.16, bf16[64,8192]{1,0:T(8,128)(2,1)} %bitcast.17), custom_call_target="tpu_custom_call" | custom-call | tf_op jit(solution)/shard_map/project/pallas_call | solution.py:104
  5.3 4.1 %collective-permute-start.2 = (bf16[33,8,128]{2,1,0:T(8,128)(2,1)S(1)}, bf16[33,8,128]{2,1,0:T(8,128)(2,1)S(1)}, u32[]{:S(2)}, u32[]{:S(2)}) collective-permute-start(bf16[33,8,128]{2,1,0:T(8,128)(2,1)S(1)} %bitcast.9), channel_id=1, source_target_pairs={{0,2},{1,3},{2,0},{3,1},{4,6},{5,7},{6,4},{7,5},{8,10},{9,11},{10,... | collective-permute-start | bytes 202760 | tf_op jit(solution)/shard_map/ppermute | solution.py:347
  9.4 1.6 %collective-permute-start.1 = (bf16[33,8,128]{2,1,0:T(8,128)(2,1)S(1)}, bf16[33,8,128]{2,1,0:T(8,128)(2,1)S(1)}, u32[]{:S(2)}, u32[]{:S(2)}) collective-permute-start(bf16[33,8,128]{2,1,0:T(8,128)(2,1)S(1)} %bitcast.10), channel_id=1, source_target_pairs={{0,1},{1,2},{2,3},{3,0},{4,5},{5,6},{6,7},{7,4},{8,9},{9,10},{10,1... | collective-permute-start | bytes 202760 | tf_op jit(solution)/shard_map/ppermute | solution.py:347
  11.0 2.2 %collective-permute-start = (bf16[33,8,128]{2,1,0:T(8,128)(2,1)S(1)}, bf16[33,8,128]{2,1,0:T(8,128)(2,1)S(1)}, u32[]{:S(2)}, u32[]{:S(2)}) collective-permute-start(bf16[33,8,128]{2,1,0:T(8,128)(2,1)S(1)} %bitcast.11), channel_id=1, source_target_pairs={{0,3},{1,0},{2,1},{3,2},{4,7},{5,4},{6,5},{7,6},{8,11},{9,8},{10,9... | collective-permute-start | bytes 202760 | tf_op jit(solution)/shard_map/ppermute | solution.py:347
  13.2 0.0 collective-permute-done.2
  13.2 2.5 %collective-permute-done.1 = bf16[33,8,128]{2,1,0:T(8,128)(2,1)S(1)} collective-permute-done((bf16[33,8,128]{2,1,0:T(8,128)(2,1)S(1)}, bf16[33,8,128]{2,1,0:T(8,128)(2,1)S(1)}, u32[]{:S(2)}, u32[]{:S(2)}) %collective-permute-start.1) | collective-permute-done | bytes 67616 | tf_op jit(solution)/shard_map/ppermute | solution.py:347
  15.7 0.3 collective-permute-done
  16.1 0.1 pad_maximum_fusion
  16.2 1.6 %collective-permute-start.5 = (bf16[19,32,128]{2,1,0:T(8,128)(2,1)S(1)}, bf16[19,32,128]{2,1,0:T(8,128)(2,1)S(1)}, u32[]{:S(2)}, u32[]{:S(2)}) collective-permute-start(bf16[19,32,128]{2,1,0:T(8,128)(2,1)S(1)} %get-tuple-element.10), channel_id=1, source_target_pairs={{0,16},{4,20},{8,24},{12,28},{16,0},{20,4},{24,8},{28,12},{1,17},{... | collective-permute-start | bytes 466952 | tf_op jit(solution)/shard_map/ppermute | solution.py:342
  17.8 1.4 %collective-permute-start.3 = (bf16[19,32,128]{2,1,0:T(8,128)(2,1)S(1)}, bf16[19,32,128]{2,1,0:T(8,128)(2,1)S(1)}, u32[]{:S(2)}, u32[]{:S(2)}) collective-permute-start(bf16[19,32,128]{2,1,0:T(8,128)(2,1)S(1)} %get-tuple-element.11), channel_id=1, source_target_pairs={{0,24},{4,28},{8,16},{12,20},{16,8},{20,12},{24,0},{28,4},{1,25},{... | collective-permute-start | bytes 466952 | tf_op jit(solution)/shard_map/ppermute | solution.py:342
  19.3 0.5 %collective-permute-start.4 = (bf16[19,32,128]{2,1,0:T(8,128)(2,1)S(1)}, bf16[19,32,128]{2,1,0:T(8,128)(2,1)S(1)}, u32[]{:S(2)}, u32[]{:S(2)}) collective-permute-start(bf16[19,32,128]{2,1,0:T(8,128)(2,1)S(1)} %get-tuple-element.12), channel_id=1, source_target_pairs={{0,8},{4,12},{8,0},{12,4},{16,24},{20,28},{24,16},{28,20},{1,9},{5... | collective-permute-start | bytes 466952 | tf_op jit(solution)/shard_map/ppermute | solution.py:342
  19.7 0.0 collective-permute-start.6
  19.7 3.4 %collective-permute-done.5.refs_3_ = bf16[19,32,128]{2,1,0:T(8,128)(2,1)S(1)} collective-permute-done((bf16[19,32,128]{2,1,0:T(8,128)(2,1)S(1)}, bf16[19,32,128]{2,1,0:T(8,128)(2,1)S(1)}, u32[]{:S(2)}, u32[]{:S(2)}) %collective-permute-start.5) | collective-permute-done | bytes 155680 | tf_op jit(solution)/shard_map/ppermute | solution.py:342
  23.1 0.0 collective-permute-start.9
  23.1 1.3 %collective-permute-done.3.refs_1_ = bf16[19,32,128]{2,1,0:T(8,128)(2,1)S(1)} collective-permute-done((bf16[19,32,128]{2,1,0:T(8,128)(2,1)S(1)}, bf16[19,32,128]{2,1,0:T(8,128)(2,1)S(1)}, u32[]{:S(2)}, u32[]{:S(2)}) %collective-permute-start.3) | collective-permute-done | bytes 155680 | tf_op jit(solution)/shard_map/ppermute | solution.py:342
  24.4 0.0 collective-permute-start.7
  24.4 0.7 %collective-permute-done.4.refs_2_ = bf16[19,32,128]{2,1,0:T(8,128)(2,1)S(1)} collective-permute-done((bf16[19,32,128]{2,1,0:T(8,128)(2,1)S(1)}, bf16[19,32,128]{2,1,0:T(8,128)(2,1)S(1)}, u32[]{:S(2)}, u32[]{:S(2)}) %collective-permute-start.4) | collective-permute-done | bytes 155680 | tf_op jit(solution)/shard_map/ppermute | solution.py:342
  25.1 0.0 collective-permute-start.8
  25.1 0.0 copy-done
  25.1 0.1 pad_add_fusion.place_ref
  25.2 0.0 collective-permute-done.6.refs_4_
  25.2 0.0 collective-permute-done.9.refs_7_
  25.2 0.6 %collective-permute-done.7.refs_5_ = bf16[19,32,128]{2,1,0:T(8,128)(2,1)S(1)} collective-permute-done((bf16[19,32,128]{2,1,0:T(8,128)(2,1)S(1)}, bf16[19,32,128]{2,1,0:T(8,128)(2,1)S(1)}, u32[]{:S(2)}, u32[]{:S(2)}) %collective-permute-start.7) | collective-permute-done | bytes 155680 | tf_op jit(solution)/shard_map/ppermute | solution.py:342
  25.8 0.7 %collective-permute-done.8.refs_6_ = bf16[19,32,128]{2,1,0:T(8,128)(2,1)S(1)} collective-permute-done((bf16[19,32,128]{2,1,0:T(8,128)(2,1)S(1)}, bf16[19,32,128]{2,1,0:T(8,128)(2,1)S(1)}, u32[]{:S(2)}, u32[]{:S(2)}) %collective-permute-start.8) | collective-permute-done | bytes 155680 | tf_op jit(solution)/shard_map/ppermute | solution.py:342
  26.4 8.7 %fisher.1 = f32[512,1024]{1,0:T(8,128)} custom-call(s32[2]{0:T(128)S(1)} %pad_add_fusion.place_ref, f32[1,1024]{1,0:T(1,128)S(1)} %bitcast.13, f32[1,256]{1,0:T(1,128)S(1)} %slice.12.panel_level_ref, bf16[19,32,128]{2,1,0:T(8,128)(2,1)S(1)} %get-tuple-element.13.refs_0_, bf16[19,32,128]{2,1,0:T(8,128)(2,1)S(1)} %collective-permute-done.3.refs_1_, ...), custom_call_target="tpu_custom_call" | custom-call | tf_op jit(solution)/shard_map/fisher/pallas_call | solution.py:319
  (7 shorter events, 0.1 us)
Async XLA Ops:
  0.0 25.1 %copy-start = (s32[4096]{0:T(1024)S(1)}, s32[4096]{0:T(1024)}, u32[]{:S(2)}) copy-start(s32[4096]{0:T(1024)} %param.9) | copy-start | bytes 49156
  5.3 7.9 %collective-permute-start.2 = (bf16[33,8,128]{2,1,0:T(8,128)(2,1)S(1)}, bf16[33,8,128]{2,1,0:T(8,128)(2,1)S(1)}, u32[]{:S(2)}, u32[]{:S(2)}) collective-permute-start(bf16[33,8,128]{2,1,0:T(8,128)(2,1)S(1)} %bitcast.9), channel_id=1, source_target_pairs={{0,2},{1,3},{2,0},{3,1},{4,6},{5,7},{6,4},{7,5},{8,10},{9,11},{10,... | collective-permute-start | bytes 202760 | tf_op jit(solution)/shard_map/ppermute | solution.py:347
  9.4 6.3 %collective-permute-start.1 = (bf16[33,8,128]{2,1,0:T(8,128)(2,1)S(1)}, bf16[33,8,128]{2,1,0:T(8,128)(2,1)S(1)}, u32[]{:S(2)}, u32[]{:S(2)}) collective-permute-start(bf16[33,8,128]{2,1,0:T(8,128)(2,1)S(1)} %bitcast.10), channel_id=1, source_target_pairs={{0,1},{1,2},{2,3},{3,0},{4,5},{5,6},{6,7},{7,4},{8,9},{9,10},{10,1... | collective-permute-start | bytes 202760 | tf_op jit(solution)/shard_map/ppermute | solution.py:347
  11.0 5.0 %collective-permute-start = (bf16[33,8,128]{2,1,0:T(8,128)(2,1)S(1)}, bf16[33,8,128]{2,1,0:T(8,128)(2,1)S(1)}, u32[]{:S(2)}, u32[]{:S(2)}) collective-permute-start(bf16[33,8,128]{2,1,0:T(8,128)(2,1)S(1)} %bitcast.11), channel_id=1, source_target_pairs={{0,3},{1,0},{2,1},{3,2},{4,7},{5,4},{6,5},{7,6},{8,11},{9,8},{10,9... | collective-permute-start | bytes 202760 | tf_op jit(solution)/shard_map/ppermute | solution.py:347
  16.2 7.0 %collective-permute-start.5 = (bf16[19,32,128]{2,1,0:T(8,128)(2,1)S(1)}, bf16[19,32,128]{2,1,0:T(8,128)(2,1)S(1)}, u32[]{:S(2)}, u32[]{:S(2)}) collective-permute-start(bf16[19,32,128]{2,1,0:T(8,128)(2,1)S(1)} %get-tuple-element.10), channel_id=1, source_target_pairs={{0,16},{4,20},{8,24},{12,28},{16,0},{20,4},{24,8},{28,12},{1,17},{... | collective-permute-start | bytes 466952 | tf_op jit(solution)/shard_map/ppermute | solution.py:342
  17.8 6.6 %collective-permute-start.3 = (bf16[19,32,128]{2,1,0:T(8,128)(2,1)S(1)}, bf16[19,32,128]{2,1,0:T(8,128)(2,1)S(1)}, u32[]{:S(2)}, u32[]{:S(2)}) collective-permute-start(bf16[19,32,128]{2,1,0:T(8,128)(2,1)S(1)} %get-tuple-element.11), channel_id=1, source_target_pairs={{0,24},{4,28},{8,16},{12,20},{16,8},{20,12},{24,0},{28,4},{1,25},{... | collective-permute-start | bytes 466952 | tf_op jit(solution)/shard_map/ppermute | solution.py:342
  19.3 5.8 %collective-permute-start.4 = (bf16[19,32,128]{2,1,0:T(8,128)(2,1)S(1)}, bf16[19,32,128]{2,1,0:T(8,128)(2,1)S(1)}, u32[]{:S(2)}, u32[]{:S(2)}) collective-permute-start(bf16[19,32,128]{2,1,0:T(8,128)(2,1)S(1)} %get-tuple-element.12), channel_id=1, source_target_pairs={{0,8},{4,12},{8,0},{12,4},{16,24},{20,28},{24,16},{28,20},{1,9},{5... | collective-permute-start | bytes 466952 | tf_op jit(solution)/shard_map/ppermute | solution.py:342
  19.7 5.5 %collective-permute-start.6 = (bf16[19,32,128]{2,1,0:T(8,128)(2,1)S(1)}, bf16[19,32,128]{2,1,0:T(8,128)(2,1)S(1)}, u32[]{:S(2)}, u32[]{:S(2)}) collective-permute-start(bf16[19,32,128]{2,1,0:T(8,128)(2,1)S(1)} %get-tuple-element.13.refs_0_), channel_id=1, source_target_pairs={{0,4},{4,0},{8,12},{12,8},{16,20},{20,16},{24,28},{28,24},{1,5},{5... | collective-permute-start | bytes 466952 | tf_op jit(solution)/shard_map/ppermute | solution.py:342
  23.1 2.0 %collective-permute-start.9 = (bf16[19,32,128]{2,1,0:T(8,128)(2,1)S(1)}, bf16[19,32,128]{2,1,0:T(8,128)(2,1)S(1)}, u32[]{:S(2)}, u32[]{:S(2)}) collective-permute-start(bf16[19,32,128]{2,1,0:T(8,128)(2,1)S(1)} %collective-permute-done.5.refs_3_), channel_id=1, source_target_pairs={{0,4},{4,0},{8,12},{12,8},{16,20},{20,16},{24,28},{28,24},{1,5},{5... | collective-permute-start | bytes 466952 | tf_op jit(solution)/shard_map/ppermute | solution.py:342
  24.4 1.4 %collective-permute-start.7 = (bf16[19,32,128]{2,1,0:T(8,128)(2,1)S(1)}, bf16[19,32,128]{2,1,0:T(8,128)(2,1)S(1)}, u32[]{:S(2)}, u32[]{:S(2)}) collective-permute-start(bf16[19,32,128]{2,1,0:T(8,128)(2,1)S(1)} %collective-permute-done.3.refs_1_), channel_id=1, source_target_pairs={{0,4},{4,0},{8,12},{12,8},{16,20},{20,16},{24,28},{28,24},{1,5},{5... | collective-permute-start | bytes 466952 | tf_op jit(solution)/shard_map/ppermute | solution.py:342
  25.1 1.4 %collective-permute-start.8 = (bf16[19,32,128]{2,1,0:T(8,128)(2,1)S(1)}, bf16[19,32,128]{2,1,0:T(8,128)(2,1)S(1)}, u32[]{:S(2)}, u32[]{:S(2)}) collective-permute-start(bf16[19,32,128]{2,1,0:T(8,128)(2,1)S(1)} %collective-permute-done.4.refs_2_), channel_id=1, source_target_pairs={{0,4},{4,0},{8,12},{12,8},{16,20},{20,16},{24,28},{28,24},{1,5},{5... | collective-permute-start | bytes 466952 | tf_op jit(solution)/shard_map/ppermute | solution.py:342
